TPU v7x, 256 devices: a whole 4x4x8 slice. The times are simulated.
256 devices in a mesh: tgt: 32 (over z, y_lo, core), blk: 8 (over x, y_hi).
Axes of the slice: x: 4, y: 4 (y_hi: 2, y_lo: 2; y = y_hi * 2 + y_lo), z: 8, core: 2. Of those that a mesh axis runs over, the one named last changes fastest.
Arguments:
- target_feats: bfloat16 [32768, 32768], P('tgt', 'blk'), may hold values from -6 to 6
- support_feats: bfloat16 [512, 32768], P('tgt', 'blk'), may hold values from -6 to 6
- coefs: bfloat16 [1000, 512], replicated, may hold values from -0.25 to 0.25
- labels: int32 [32768], P('tgt'), may hold values from 0 to 999
Outputs:
- support_grad: float32 [512, 32768], P('tgt', 'blk')
- coef_grad: float32 [1000, 512], P('blk')
All inputs are finite; a program needn't handle non-finite values.
Results may differ from a plain program's by a relative error of at most 0.0031.
Values may be sent and summed in bfloat16 or wider, within the bound.
No kernel may reach another device: no remote copies, remote signals or barrier semaphores. Data moves between devices by JAX's collectives and lax.ppermute only.
A program may use at most 64 MiB of HBM per device.

v0:
```python
import math

import jax
import jax.numpy as jnp
from jax import lax
from jax.sharding import PartitionSpec as P

FEATURES = 32768


def class_table(labels, classes):
    return (jnp.arange(classes, dtype=jnp.int32)[:, None] == labels[None, :]).astype(jnp.float32)


def shards(target_feats, support_feats, coefs, labels):
    scale = 1.0 / math.sqrt(FEATURES)
    classes = coefs.shape[0]
    tgt_rows = target_feats.shape[0]
    blk_count = lax.axis_size("blk")
    blk_index = lax.axis_index("blk")
    class_rows = classes // blk_count
    root_count = math.sqrt(tgt_rows * lax.axis_size("tgt"))
    partial_kernel = (
        lax.dot_general(
            lax.all_gather(support_feats, "tgt", axis=0, tiled=True),
            target_feats,
            (((1,), (1,)), ((), ())),
            preferred_element_type=jnp.float32,
        )
        * scale
    )
    kernel = lax.psum(partial_kernel, "blk")
    kernel_low = kernel.astype(jnp.bfloat16)
    predict = jnp.dot(coefs, kernel_low, preferred_element_type=jnp.float32)
    residual = predict - class_table(labels, classes)
    residual_low = residual.astype(jnp.bfloat16)
    kernel_grad = lax.dot_general(
        coefs, residual_low, (((0,), (0,)), ((), ())), preferred_element_type=jnp.float32
    ).astype(jnp.bfloat16)
    own_rows = lax.dynamic_slice_in_dim(residual_low, blk_index * class_rows, class_rows, 0)
    coef_part = lax.dot_general(
        own_rows, kernel_low, (((1,), (1,)), ((), ())), preferred_element_type=jnp.float32
    )
    support_grad = lax.psum_scatter(
        jnp.dot(kernel_grad, target_feats, preferred_element_type=jnp.float32) * scale,
        "tgt",
        scatter_dimension=0,
        tiled=True,
    )
    coef_grad = lax.psum(coef_part, "tgt") / root_count
    return (support_grad, coef_grad)


def solution(mesh):
    in_specs = (P("tgt", "blk"), P("tgt", "blk"), P(), P("tgt"))
    out_specs = (P("tgt", "blk"), P("blk", None))
    return jax.shard_map(shards, mesh=mesh, in_specs=in_specs, out_specs=out_specs, check_vma=False)
```

profile of v0, /device:TPU:1, one launch (start us, length us, event | category | flops | bytes accessed | tf_op | source)
XLA Modules:
  0.0 553.8 jit_solution(203090867141755617)
XLA Ops:
  7.2 0.0 copy-start
  7.2 0.0 all-gather.2.cloned.1.call-start
  7.2 0.7 all-gather.2.cloned.1.call-update
  7.9 0.0 all-reduce.3.cloned.1.call-start
  8.0 0.0 copy-start.2
  8.0 73.0 %all-gather.2.cloned.1.call-done = bf16[512,4096]{1,0:T(8,128)(2,1)} async-done(((bf16[16,4096]{1,0:T(8,128)(2,1)}), bf16[512,4096]{1,0:T(8,128)(2,1)}) %all-gather.2.cloned.1.call-update) | async-done | bytes 4194320 | tf_op jit(solution)/shard_map/all_gather | solution.py:25
  80.9 8.2 %convolution_multiply_fusion.1 = f32[512,1024]{1,0:T(8,128)S(1)} fusion(bf16[512,4096]{1,0:T(8,128)(2,1)} %all-gather.2.cloned.1.call-done, bf16[1024,4096]{1,0:T(8,128)(2,1)} %param.4), kind=kOutput, calls=%fused_computation.4 | convolution fusion | flops 4295491584 | bytes 14680064 | tf_op jit(solution)/shard_map/dot_general | solution.py:24
  89.2 92.0 %all-reduce.4 = bf16[512,1024]{1,0:T(8,128)(2,1)} all-reduce(f32[512,1024]{1,0:T(8,128)S(1)} %convolution_multiply_fusion.1), channel_id=1, replica_groups=mesh['tgt'=32,'blk'=8] {'blk'}, use_global_device_ids=true, to_apply=%region_0.0 | all-reduce | flops 524288 | bytes 3145728 | tf_op jit(solution)/shard_map/psum | solution.py:32
  181.2 0.0 copy-done
  181.2 0.0 copy-done.2
  181.2 0.0 copy-start.1
  181.2 2.7 fusion
  183.8 0.0 copy-done.1
  183.9 1.2 fusion.1
  185.0 0.0 all-reduce.3.cloned.1.call-update
  185.1 0.0 reduce-scatter.2.cloned.1.call-start
  185.1 11.2 %convolution_multiply_fusion = f32[512,4096]{1,0:T(8,128)} fusion(bf16[1024,4096]{1,0:T(8,128)(2,1)} %param.4, bf16[1000,1024]{1,0:T(8,128)(2,1)S(1)} %fusion, bf16[1000,512]{1,0:T(8,128)(2,1)S(1)} %copy-done), kind=kOutput, calls=%fused_computation | convolution fusion | flops 5346164736 | bytes 19849216 | tf_op jit(solution)/shard_map/dot_general | solution.py:45
  196.3 0.0 reduce-scatter.2.cloned.1.call-update
  196.3 220.3 %all-reduce.3.cloned.1.call-done = f32[125,512]{1,0:T(8,128)} async-done(((f32[125,512]{1,0:T(8,128)}), f32[125,512]{1,0:T(8,128)}) %all-reduce.3.cloned.1.call-update) | async-done | bytes 256016 | tf_op jit(solution)/shard_map/psum | solution.py:50
  416.6 1.7 broadcast_multiply_fusion
  418.3 128.9 %reduce-scatter.2.cloned.1.call-done = f32[16,4096]{1,0:T(8,128)} async-done(((f32[512,4096]{1,0:T(8,128)}), f32[16,4096]{1,0:T(8,128)}) %reduce-scatter.2.cloned.1.call-update) | async-done | bytes 262160 | tf_op jit(solution)/shard_map/reduce_scatter | solution.py:44
Async XLA Ops:
  7.2 174.0 %copy-start = (bf16[1000,512]{1,0:T(8,128)(2,1)S(1)}, bf16[1000,512]{1,0:T(8,128)(2,1)}, u32[]{:S(2)}) copy-start(bf16[1000,512]{1,0:T(8,128)(2,1)} %param.6) | copy-start | bytes 3072004
  7.2 73.8 %all-gather.2.cloned.1.call-start = ((), (), s32[]{:S(2)}) async-start(), calls=%async_computation.1 | async-start | bytes 4325376 | tf_op jit(solution)/shard_map/all_gather | solution.py:25
  7.9 408.7 %all-reduce.3.cloned.1.call-start = ((), (), s32[]{:S(2)}) async-start(), calls=%async_computation.3 | async-start | bytes 524288 | tf_op jit(solution)/shard_map/psum | solution.py:50
  8.0 173.2 %copy-start.2 = (s32[1024]{0:T(1024)S(1)}, s32[1024]{0:T(1024)}, u32[]{:S(2)}) copy-start(s32[1024]{0:T(1024)} %param.7) | copy-start | bytes 12292
  181.2 2.7 copy-start.1
  185.1 362.2 %reduce-scatter.2.cloned.1.call-start = ((), (), s32[]{:S(2)}) async-start(), calls=%async_computation.2 | async-start | bytes 8650752 | tf_op jit(solution)/shard_map/reduce_scatter | solution.py:44
Sparse Core Ops, SparseCore 0:
  9.9 71.0 all-gather.1
  185.2 231.3 all-reduce.2
  419.9 127.2 reduce-scatter.1
where the time goes:
time: 557 us; the launch traced here: 554 us
  waiting for transfers between devices  423 us (76%)
  blocking collectives  92 us (17%)
  matrix products  23.2 us (4%)
  between operations  13.8 us (2%)
    psum x1, waiting for transfers between devices, shards(): coef_grad = lax.psum(coef_part, 'tgt') / root_count  220 us
    reduce_scatter x1, waiting for transfers between devices, shards(): lax.psum_scatter(jnp.dot(kernel_grad, target_feats, preferred_element_typ...  129 us
    psum x1, blocking collectives, shards(): kernel = lax.psum(partial_kernel, 'blk')  92 us
    all_gather x1, waiting for transfers between devices, shards(): lax.all_gather(support_feats, 'tgt', axis=0, tiled=True)  73 us
    dot_general x1, matrix products, shards(): jnp.dot(kernel_grad, target_feats, preferred_element_type=jnp.float32)  11.2 us
  transfers between devices with their start and end apart: 3, of which 3 were waited for; matrix products, arithmetic and copies ran while one was open for 2% of the time, Pallas kernels for 0%

commit v1 on v0

v1 whole, which is shorter than its diff:
```python
import math

import jax
import jax.numpy as jnp
from jax import lax
from jax.sharding import PartitionSpec as P

FEATURES = 32768
LOW = jnp.bfloat16
FULL = jnp.float32
DEPTH, PAIR, CORES = 8, 2, 2


def tgt_move(array, dz, dy, dc):
    pairs = []
    for z in range(DEPTH):
        for y in range(PAIR):
            for c in range(CORES):
                source = (z * PAIR + y) * CORES + c
                target = ((z + dz) % DEPTH * PAIR + (y + dy) % PAIR) * CORES + (c + dc) % CORES
                pairs.append((source, target))
    return lax.ppermute(array, "tgt", pairs)


def z_xor(array, bit):
    per = PAIR * CORES
    return lax.ppermute(array, "tgt", [(i, ((i // per) ^ bit) * per + i % per) for i in range(DEPTH * per)])


def place():
    index = lax.axis_index("tgt")
    return index // (PAIR * CORES), index // CORES % PAIR, index % CORES


def gather_support(support):
    levels, offsets = [], []
    up = down = support
    ring = [([support], [0])]
    for step in range(1, DEPTH // 2 + 1):
        up = tgt_move(up, 1, 0, 0)
        if step < DEPTH // 2:
            down = tgt_move(down, -1, 0, 0)
            ring.append(([up, down], [-step, step]))
        else:
            ring.append(([up], [-step]))
    for pieces, shifts in ring:
        own = jnp.concatenate(pieces, 0) if len(pieces) > 1 else pieces[0]
        near = tgt_move(own, 0, 1, 0)
        both = jnp.concatenate([own, near], 0)
        other = tgt_move(both, 0, 0, 1)
        levels.append(jnp.concatenate([both, other], 0))
        offsets.append([(dz, dy, dc) for dc in (0, 1) for dy in (0, 1) for dz in shifts])
    return levels, offsets


def order_matrix(offsets, rows):
    z, y, c = place()
    shards = [((z + dz) % DEPTH * PAIR + (y + dy) % PAIR) * CORES + (c + dc) % CORES for dz, dy, dc in offsets]
    ids = (jnp.stack(shards)[:, None] * rows + jnp.arange(rows)[None, :]).reshape(-1)
    return (ids[:, None] == jnp.arange(ids.shape[0])[None, :]).astype(LOW)


def sum_coef(part):
    z, y, c = place()
    rows, columns = part.shape

    def halves(array, which):
        half = array.shape[1] // 2
        keep = lax.dynamic_slice_in_dim(array, which * half, half, 1)
        give = lax.dynamic_slice_in_dim(array, (1 - which) * half, half, 1)
        return keep, give

    def joined(mine, other, which):
        return jnp.where(which == 0, jnp.concatenate([mine, other], 1), jnp.concatenate([other, mine], 1))

    keep, give = halves(part, c)
    part = keep + tgt_move(give, 0, 0, 1)
    keep, give = halves(part, y)
    part = keep + tgt_move(give, 0, 1, 0)
    for bit in (1, 2, 4):
        part = part + z_xor(part, bit)
    part = joined(part, tgt_move(part, 0, 1, 0), y)
    return joined(part, tgt_move(part, 0, 0, 1), c)


def shards(target_feats, support_feats, coefs, labels):
    scale = 1.0 / math.sqrt(FEATURES)
    classes = coefs.shape[0]
    targets, features = target_feats.shape
    rows = support_feats.shape[0]
    blks = lax.axis_size("blk")
    tgts = lax.axis_size("tgt")
    blk_index = lax.axis_index("blk")
    z, y, c = place()
    half = features // 2

    give = lax.dynamic_slice_in_dim(target_feats, (1 - c) * half, half, 1)
    keep = lax.dynamic_slice_in_dim(target_feats, c * half, half, 1)
    taken = tgt_move(give, 0, 0, 1)

    levels, offsets = gather_support(support_feats)
    order = order_matrix(sum(offsets, []), rows)
    coefs_here = lax.dot_general(coefs, order, (((1,), (1,)), ((), ())), preferred_element_type=FULL).astype(LOW)

    groups = [levels[:3], levels[3:]]
    low_parts = []
    for group in groups:
        block = jnp.concatenate(group, 0)
        part = lax.dot_general(target_feats, block, (((1,), (1,)), ((), ())), preferred_element_type=FULL) * scale
        got = lax.all_to_all(part.astype(LOW), "blk", 0, 0, tiled=True)
        total = jnp.sum(got.reshape(blks, targets // blks, block.shape[0]).astype(FULL), 0)
        low_parts.append(total.astype(LOW))
    own_low = jnp.concatenate(low_parts, 1)
    spread = jnp.broadcast_to(own_low[None], (blks,) + own_low.shape).reshape(targets, -1)
    kernel_low = lax.all_to_all(spread, "blk", 0, 0, tiled=True)

    predict = lax.dot_general(kernel_low, coefs_here, (((1,), (1,)), ((), ())), preferred_element_type=FULL)
    onehot = (labels[:, None] == jnp.arange(classes, dtype=jnp.int32)[None, :]).astype(FULL)
    residual_low = (predict - onehot).astype(LOW)
    kernel_grad = lax.dot_general(coefs, residual_low, (((0,), (1,)), ((), ())), preferred_element_type=FULL).astype(LOW)
    other_grad = tgt_move(kernel_grad, 0, 0, 1)

    partial = jnp.dot(kernel_grad, keep, preferred_element_type=FULL) + jnp.dot(other_grad, taken, preferred_element_type=FULL)
    z_groups = [[zz * PAIR * CORES + r for zz in range(DEPTH)] for r in range(PAIR * CORES)]
    got = lax.all_to_all(partial.astype(LOW), "tgt", 0, 0, tiled=True, axis_index_groups=z_groups)
    chip_rows = rows * PAIR * CORES
    total = jnp.sum(got.reshape(DEPTH, chip_rows, half).astype(FULL), 0)
    total = total.reshape(PAIR, CORES * rows, half)
    mine = lax.dynamic_index_in_dim(total, y, 0, False) + tgt_move(lax.dynamic_index_in_dim(total, 1 - y, 0, False), 0, 1, 0)
    mine = mine.reshape(CORES, rows, half) * scale
    here = lax.dynamic_index_in_dim(mine, c, 0, False)
    there = tgt_move(lax.dynamic_index_in_dim(mine, 1 - c, 0, False), 0, 0, 1)
    support_grad = jnp.where(c == 0, jnp.concatenate([here, there], 1), jnp.concatenate([there, here], 1))

    class_rows = classes // blks
    own_classes = lax.dynamic_slice_in_dim(residual_low, blk_index * class_rows, class_rows, 1)
    ordered = lax.dot_general(kernel_low, order, (((1,), (0,)), ((), ())), preferred_element_type=FULL).astype(LOW)
    coef_part = lax.dot_general(own_classes, ordered, (((0,), (0,)), ((), ())), preferred_element_type=FULL)
    coef_grad = sum_coef(coef_part) / math.sqrt(targets * tgts)
    return support_grad, coef_grad


def solution(mesh):
    in_specs = (P("tgt", "blk"), P("tgt", "blk"), P(), P("tgt"))
    out_specs = (P("tgt", "blk"), P("blk", None))
    return jax.shard_map(shards, mesh=mesh, in_specs=in_specs, out_specs=out_specs, check_vma=False)
```

time: 557 us -> 199 us (0.36)
  waiting for transfers between devices: 423 us -> 97.5 us
  blocking collectives: 92 us -> 0 us
  starting transfers between devices: 0.12 us -> 56.7 us
  between operations: 13.8 us -> 1.37 us
  local copies, waits for them, and re-layouts: 0.02 us -> 9.4 us
  matrix products: 23.2 us -> 29.1 us
    psum x1 -> x0, waiting for transfers between devices: 220 us -> none  [shards(): coef_grad = lax.psum(coef_part, 'tgt') / root_count]
    reduce_scatter x1 -> x0, waiting for transfers between devices: 129 us -> none  [shards(): lax.psum_scatter(jnp.dot(kernel_grad, target_feats, preferred_element_typ...]
    psum x1 -> x0, blocking collectives: 92 us -> none  [shards(): kernel = lax.psum(partial_kernel, 'blk')]
    all_gather x1 -> x0, waiting for transfers between devices: 73 us -> none  [shards(): lax.all_gather(support_feats, 'tgt', axis=0, tiled=True)]
    ppermute x0 -> x28, waiting for transfers between devices: none -> 66.9 us  [the longest x3 45.7 us: z_xor(): lax.ppermute(array, 'tgt', [(i, (i // per ^ bit) * per + i % per) for i i...]
    ppermute x0 -> x28, starting transfers between devices: none -> 35.7 us  [the longest x25 31.8 us: tgt_move(): return lax.ppermute(array, 'tgt', pairs)]
    all_to_all x0 -> x4, waiting for transfers between devices: none -> 30.6 us  [the longest x1 15 us: shards(): kernel_low = lax.all_to_all(spread, 'blk', 0, 0, tiled=True)]
    all_to_all x0 -> x4, starting transfers between devices: none -> 20.9 us  [the longest x2 11.9 us: shards(): got = lax.all_to_all(part.astype(LOW), 'blk', 0, 0, tiled=True)]
  transfers between devices with their start and end apart: 3 -> 32, of which waited for: 3 -> 16; matrix products, arithmetic and copies ran while one was open for 2% -> 18% of each run, Pallas kernels for 0% -> 0%
where the time goes in v1:
time: 199 us; the launch traced here: 198 us
  waiting for transfers between devices  97.5 us (49%)
  starting transfers between devices  56.7 us (28%)
  matrix products  29.1 us (15%)
  local copies, waits for them, and re-layouts  9.4 us (5%)
  other arithmetic  4.22 us (2%)
    ppermute x3, waiting for transfers between devices, z_xor(): lax.ppermute(array, 'tgt', [(i, (i // per ^ bit) * per + i % per) for i i...  45.7 us
    ppermute x25, starting transfers between devices, tgt_move(): return lax.ppermute(array, 'tgt', pairs)  31.8 us
    ppermute x25, waiting for transfers between devices, tgt_move(): return lax.ppermute(array, 'tgt', pairs)  21.2 us
    all_to_all x1, waiting for transfers between devices, shards(): kernel_low = lax.all_to_all(spread, 'blk', 0, 0, tiled=True)  15 us
    all_to_all x2, waiting for transfers between devices, shards(): got = lax.all_to_all(part.astype(LOW), 'blk', 0, 0, tiled=True)  13.1 us
    all_to_all x2, starting transfers between devices, shards(): got = lax.all_to_all(part.astype(LOW), 'blk', 0, 0, tiled=True)  11.9 us
    dot_general x2, matrix products, shards(): lax.dot_general(target_feats, block, (((1,), (1,)), ((), ())), preferred_...  9.98 us
    dot_general x1, matrix products, shards(): jnp.dot(other_grad, taken, preferred_element_type=FULL)  6.08 us
  transfers between devices with their start and end apart: 32, of which 16 were waited for; matrix products, arithmetic and copies ran while one was open for 18% of the time, Pallas kernels for 0%

profile of v1, /device:TPU:1, one launch (start us, length us, event | category | flops | bytes accessed | tf_op | source)
XLA Modules:
  0.0 198.3 jit_solution(7148192148263138826)
XLA Ops:
  0.6 2.5 %collective-permute-start.2 = (bf16[16,4096]{1,0:T(8,128)(2,1)}, bf16[16,4096]{1,0:T(8,128)(2,1)S(1)}, u32[]{:S(2)}, u32[]{:S(2)}) collective-permute-start(bf16[16,4096]{1,0:T(8,128)(2,1)} %param.5), channel_id=1, source_target_pairs={{0,32},{8,40},{16,48},{24,56},{32,64},{40,72},{48,80},{56,88},{64,... | collective-permute-start | bytes 393224 | tf_op jit(solution)/shard_map/ppermute | solution.py:22
  4.5 4.0 %collective-permute-start.3 = (bf16[16,4096]{1,0:T(8,128)(2,1)}, bf16[16,4096]{1,0:T(8,128)(2,1)S(1)}, u32[]{:S(2)}, u32[]{:S(2)}) collective-permute-start(bf16[16,4096]{1,0:T(8,128)(2,1)} %param.5), channel_id=1, source_target_pairs={{0,224},{8,232},{16,240},{24,248},{32,0},{40,8},{48,16},{56,24},{6... | collective-permute-start | bytes 393224 | tf_op jit(solution)/shard_map/ppermute | solution.py:22
  8.5 4.9 %constant_dynamic-slice_fusion.2 = bf16[1024,2048]{1,0:T(8,128)(2,1)} fusion(bf16[1024,4096]{1,0:T(8,128)(2,1)} %param.4, s32[]{:T(128)S(6)} %select_n.321), kind=kLoop, calls=%fused_computation.64 | loop fusion | bytes 8388612 | tf_op jit(solution)/shard_map/dynamic_slice | solution.py:97
  15.2 2.7 %collective-permute-start.7 = (bf16[16,4096]{1,0:T(8,128)(2,1)S(1)}, bf16[16,4096]{1,0:T(8,128)(2,1)S(1)}, u32[]{:S(2)}, u32[]{:S(2)}) collective-permute-start(bf16[16,4096]{1,0:T(8,128)(2,1)S(1)} %collective-permute-done.3), channel_id=1, source_target_pairs={{0,224},{8,232},{16,240},{24,248},{32,0},{40,8},{48,16},{56,24},{6... | collective-permute-start | bytes 393224 | tf_op jit(solution)/shard_map/ppermute | solution.py:22
  17.9 2.8 %collective-permute-done.6 = bf16[16,4096]{1,0:T(8,128)(2,1)S(1)} collective-permute-done((bf16[16,4096]{1,0:T(8,128)(2,1)S(1)}, bf16[16,4096]{1,0:T(8,128)(2,1)S(1)}, u32[]{:S(2)}, u32[]{:S(2)}) %collective-permute-start.6) | collective-permute-done | bytes 131104 | tf_op jit(solution)/shard_map/ppermute | solution.py:22
  20.7 2.7 %collective-permute-start.11 = (bf16[16,4096]{1,0:T(8,128)(2,1)S(1)}, bf16[16,4096]{1,0:T(8,128)(2,1)S(1)}, u32[]{:S(2)}, u32[]{:S(2)}) collective-permute-start(bf16[16,4096]{1,0:T(8,128)(2,1)S(1)} %collective-permute-done.7), channel_id=1, source_target_pairs={{0,224},{8,232},{16,240},{24,248},{32,0},{40,8},{48,16},{56,24},{6... | collective-permute-start | bytes 393224 | tf_op jit(solution)/shard_map/ppermute | solution.py:22
  27.3 3.4 %collective-permute-start.5 = (bf16[64,4096]{1,0:T(8,128)(2,1)S(1)}, bf16[64,4096]{1,0:T(8,128)(2,1)S(1)}, u32[]{:S(2)}, u32[]{:S(2)}) collective-permute-start(bf16[64,4096]{1,0:T(8,128)(2,1)S(1)} %pad_maximum_fusion), channel_id=1, source_target_pairs={{0,8},{8,0},{16,24},{24,16},{32,40},{40,32},{48,56},{56,48},{64,72... | collective-permute-start | bytes 1572872 | tf_op jit(solution)/shard_map/ppermute | solution.py:22
  31.0 6.2 %collective-permute-done.14 = bf16[16,4096]{1,0:T(8,128)(2,1)S(1)} collective-permute-done((bf16[16,4096]{1,0:T(8,128)(2,1)S(1)}, bf16[16,4096]{1,0:T(8,128)(2,1)S(1)}, u32[]{:S(2)}, u32[]{:S(2)}) %collective-permute-start.14) | collective-permute-done | bytes 131104 | tf_op jit(solution)/shard_map/ppermute | solution.py:22
  45.6 2.9 %fusion.6 = bf16[24,8,8,128]{3,2,1,0:T(8,128)(2,1)S(1)} fusion(bf16[192,4096]{1,0:T(8,128)(2,1)S(1)} %constant_dynamic-update-slice_fusion.11, bf16[1024,4096]{1,0:T(8,128)(2,1)S(1)} %bitcast.75), kind=kOutput, calls=%fused_computation.15 | convolution fusion | flops 1611005952 | bytes 10354688 | tf_op jit(solution)/shard_map/dot_general | solution.py:109
  49.3 6.6 %all-to-all-start.1 = ((bf16[8,128,192]{1,2,0:T(8,128)(2,1)}), bf16[8,128,192]{1,2,0:T(8,128)(2,1)S(1)}, u32[]{:S(2)}, u32[]{:S(2)}) async-start(bf16[8,128,192]{1,2,0:T(8,128)(2,1)} %bitcast.70), calls=%async_computation.1 | async-start | bytes 786432 | tf_op jit(solution)/shard_map/all_to_all | solution.py:110
  56.0 7.1 %fusion.4 = bf16[40,8,8,128]{3,2,1,0:T(8,128)(2,1)S(1)} fusion(bf16[320,4096]{1,0:T(8,128)(2,1)} %copy-done.4, bf16[1024,4096]{1,0:T(8,128)(2,1)} %param.4), kind=kOutput, calls=%fused_computation.13 | convolution fusion | flops 2685009920 | bytes 11665408 | tf_op jit(solution)/shard_map/dot_general | solution.py:109
  65.5 5.2 %all-to-all-start = ((bf16[8,128,320]{1,2,0:T(8,128)(2,1)}), bf16[8,128,320]{1,2,0:T(8,128)(2,1)S(1)}, u32[]{:S(2)}, u32[]{:S(2)}) async-start(bf16[8,128,320]{1,2,0:T(8,128)(2,1)} %bitcast.69), calls=%async_computation | async-start | bytes 1310720 | tf_op jit(solution)/shard_map/all_to_all | solution.py:110
  70.8 11.7 %all-to-all-done = bf16[8,128,320]{1,2,0:T(8,128)(2,1)S(1)} async-done(((bf16[8,128,320]{1,2,0:T(8,128)(2,1)}), bf16[8,128,320]{1,2,0:T(8,128)(2,1)S(1)}, u32[]{:S(2)}, u32[]{:S(2)}) %all-to-all-start) | async-done | bytes 655392 | tf_op jit(solution)/shard_map/all_to_all | solution.py:110
  83.8 3.6 %all-to-all-start.2 = ((bf16[8,128,512]{2,1,0:T(8,128)(2,1)}), bf16[8,128,512]{2,1,0:T(8,128)(2,1)S(1)}, u32[]{:S(2)}, u32[]{:S(2)}) async-start(bf16[8,128,512]{2,1,0:T(8,128)(2,1)} %broadcast_in_dim.2), calls=%async_computation.2 | async-start | bytes 2097152 | tf_op jit(solution)/shard_map/all_to_all | solution.py:115
  87.9 15.0 %all-to-all-done.2 = bf16[8,128,512]{2,1,0:T(8,128)(2,1)S(1)} async-done(((bf16[8,128,512]{2,1,0:T(8,128)(2,1)}), bf16[8,128,512]{2,1,0:T(8,128)(2,1)S(1)}, u32[]{:S(2)}, u32[]{:S(2)}) %all-to-all-start.2) | async-done | bytes 1048608 | tf_op jit(solution)/shard_map/all_to_all | solution.py:115
  102.9 3.3 %subtract_convert_fusion = bf16[1024,1000]{0,1:T(8,128)(2,1)} fusion(bf16[1024,512]{1,0:T(8,128)(2,1)S(1)} %bitcast.76, s32[1024]{0:T(1024)S(1)} %copy-done.5, bf16[1000,512]{1,0:T(8,128)(2,1)S(1)} %copy-done, s32[512]{0:T(512)S(1)} %add.523), kind=kOutput, calls=%fused_computation.4 | convolution fusion | flops 1577734144 | bytes 4126720 | tf_op jit(solution)/shard_map/dot_general | solution.py:117
  106.2 2.9 %convolution_convert_fusion.1 = bf16[1024,512]{1,0:T(8,128)(2,1)S(1)} fusion(bf16[1024,1000]{0,1:T(8,128)(2,1)} %subtract_convert_fusion, bf16[1000,512]{1,0:T(8,128)(2,1)S(1)} %copy-done), kind=kOutput, calls=%fused_computation.7 | convolution fusion | flops 1049100288 | bytes 4120576 | tf_op jit(solution)/shard_map/dot_general | solution.py:120
  110.6 4.6 %fusion = f32[512,2048]{1,0:T(8,128)S(1)} fusion(bf16[1024,512]{1,0:T(8,128)(2,1)S(1)} %convolution_convert_fusion.1, bf16[1024,4096]{1,0:T(8,128)(2,1)} %param.4, s32[]{:T(128)S(6)} %select_n.320), kind=kOutput, calls=%fused_computation.2 | convolution fusion | flops 2147483648 | bytes 9437188 | tf_op jit(solution)/shard_map/dot_general | solution.py:123
  115.3 6.1 %add_convert_fusion = bf16[512,2048]{1,0:T(8,128)(2,1)} fusion(f32[512,2048]{1,0:T(8,128)S(1)} %fusion, bf16[512,1024]{0,1:T(8,128)(2,1)S(1)} %collective-permute-done.17, bf16[1024,2048]{1,0:T(8,128)(2,1)} %collective-permute-done.18), kind=kOutput, calls=%fused_computation.1 | convolution fusion | flops 2149580800 | bytes 11534336 | tf_op jit(solution)/shard_map/dot_general | solution.py:123
  121.3 5.5 %all-to-all-start.3 = ((bf16[8,64,2048]{2,1,0:T(8,128)(2,1)}), bf16[8,64,2048]{2,1,0:T(8,128)(2,1)S(1)}, u32[]{:S(2)}, u32[]{:S(2)}) async-start(bf16[8,64,2048]{2,1,0:T(8,128)(2,1)} %bitcast.71), calls=%async_computation.3 | async-start | bytes 4194304 | tf_op jit(solution)/shard_map/all_to_all | solution.py:125
  132.1 3.0 %collective-permute-done.22 = f32[125,128]{1,0:T(8,128)S(1)} collective-permute-done((f32[125,128]{1,0:T(8,128)S(1)}, f32[125,128]{1,0:T(8,128)S(1)}, u32[]{:S(2)}, u32[]{:S(2)}) %collective-permute-start.22) | collective-permute-done | bytes 64032 | tf_op jit(solution)/shard_map/ppermute | solution.py:22
  136.9 38.4 %collective-permute-done.23 = f32[125,128]{1,0:T(8,128)S(1)} collective-permute-done((f32[125,128]{1,0:T(8,128)S(1)}, f32[125,128]{1,0:T(8,128)S(1)}, u32[]{:S(2)}, u32[]{:S(2)}) %collective-permute-start.23) | collective-permute-done | bytes 64032 | tf_op jit(solution)/shard_map/ppermute | solution.py:27
  183.5 5.6 %collective-permute-done.25 = f32[125,128]{1,0:T(8,128)S(1)} collective-permute-done((f32[125,128]{1,0:T(8,128)S(1)}, f32[125,128]{1,0:T(8,128)S(1)}, u32[]{:S(2)}, u32[]{:S(2)}) %collective-permute-start.25) | collective-permute-done | bytes 64032 | tf_op jit(solution)/shard_map/ppermute | solution.py:27
  192.3 2.9 %collective-permute-start.27 = (f32[125,256]{1,0:T(8,128)S(1)}, f32[125,256]{1,0:T(8,128)S(1)}, u32[]{:S(2)}, u32[]{:S(2)}) collective-permute-start(f32[125,256]{1,0:T(8,128)S(1)} %maximum_select_fusion.2), channel_id=1, source_target_pairs={{0,8},{8,0},{16,24},{24,16},{32,40},{40,32},{48,56},{56,48},{64,72... | collective-permute-start | bytes 384008 | tf_op jit(solution)/shard_map/ppermute | solution.py:22
  (116 shorter events, 43.3 us)
Async XLA Ops:
  0.6 14.2 %collective-permute-start.2 = (bf16[16,4096]{1,0:T(8,128)(2,1)}, bf16[16,4096]{1,0:T(8,128)(2,1)S(1)}, u32[]{:S(2)}, u32[]{:S(2)}) collective-permute-start(bf16[16,4096]{1,0:T(8,128)(2,1)} %param.5), channel_id=1, source_target_pairs={{0,32},{8,40},{16,48},{24,56},{32,64},{40,72},{48,80},{56,88},{64,... | collective-permute-start | bytes 393224 | tf_op jit(solution)/shard_map/ppermute | solution.py:22
  3.2 11.5 %collective-permute-start = (bf16[16,4096]{1,0:T(8,128)(2,1)}, bf16[16,4096]{1,0:T(8,128)(2,1)S(1)}, u32[]{:S(2)}, u32[]{:S(2)}) collective-permute-start(bf16[16,4096]{1,0:T(8,128)(2,1)} %param.5), channel_id=1, source_target_pairs={{0,16},{8,24},{16,0},{24,8},{32,48},{40,56},{48,32},{56,40},{64,80... | collective-permute-start | bytes 393224 | tf_op jit(solution)/shard_map/ppermute | solution.py:22
  4.5 10.4 %collective-permute-start.3 = (bf16[16,4096]{1,0:T(8,128)(2,1)}, bf16[16,4096]{1,0:T(8,128)(2,1)S(1)}, u32[]{:S(2)}, u32[]{:S(2)}) collective-permute-start(bf16[16,4096]{1,0:T(8,128)(2,1)} %param.5), channel_id=1, source_target_pairs={{0,224},{8,232},{16,240},{24,248},{32,0},{40,8},{48,16},{56,24},{6... | collective-permute-start | bytes 393224 | tf_op jit(solution)/shard_map/ppermute | solution.py:22
  13.5 101.8 %collective-permute-start.18 = (bf16[1024,2048]{1,0:T(8,128)(2,1)}, bf16[1024,2048]{1,0:T(8,128)(2,1)}, u32[]{:S(2)}, u32[]{:S(2)}) collective-permute-start(bf16[1024,2048]{1,0:T(8,128)(2,1)} %constant_dynamic-slice_fusion.2), channel_id=1, source_target_pairs={{0,8},{8,0},{16,24},{24,16},{32,40},{40,32},{48,56},{56,48},{64,72... | collective-permute-start | bytes 12582920 | tf_op jit(solution)/shard_map/ppermute | solution.py:22
  14.8 16.0 %collective-permute-start.1 = (bf16[32,4096]{1,0:T(8,128)(2,1)S(1)}, bf16[32,4096]{1,0:T(8,128)(2,1)S(1)}, u32[]{:S(2)}, u32[]{:S(2)}) collective-permute-start(bf16[32,4096]{1,0:T(8,128)(2,1)S(1)} %pad_maximum_fusion.3), channel_id=1, source_target_pairs={{0,8},{8,0},{16,24},{24,16},{32,40},{40,32},{48,56},{56,48},{64,72... | collective-permute-start | bytes 786440 | tf_op jit(solution)/shard_map/ppermute | solution.py:22
  14.9 12.4 %collective-permute-start.4 = (bf16[32,4096]{1,0:T(8,128)(2,1)S(1)}, bf16[32,4096]{1,0:T(8,128)(2,1)S(1)}, u32[]{:S(2)}, u32[]{:S(2)}) collective-permute-start(bf16[32,4096]{1,0:T(8,128)(2,1)S(1)} %pad_maximum_fusion.4), channel_id=1, source_target_pairs={{0,16},{8,24},{16,0},{24,8},{32,48},{40,56},{48,32},{56,40},{64,80... | collective-permute-start | bytes 786440 | tf_op jit(solution)/shard_map/ppermute | solution.py:22
  15.2 5.5 %collective-permute-start.6 = (bf16[16,4096]{1,0:T(8,128)(2,1)S(1)}, bf16[16,4096]{1,0:T(8,128)(2,1)S(1)}, u32[]{:S(2)}, u32[]{:S(2)}) collective-permute-start(bf16[16,4096]{1,0:T(8,128)(2,1)S(1)} %collective-permute-done.2), channel_id=1, source_target_pairs={{0,32},{8,40},{16,48},{24,56},{32,64},{40,72},{48,80},{56,88},{64,... | collective-permute-start | bytes 393224 | tf_op jit(solution)/shard_map/ppermute | solution.py:22
  15.2 5.5 %collective-permute-start.7 = (bf16[16,4096]{1,0:T(8,128)(2,1)S(1)}, bf16[16,4096]{1,0:T(8,128)(2,1)S(1)}, u32[]{:S(2)}, u32[]{:S(2)}) collective-permute-start(bf16[16,4096]{1,0:T(8,128)(2,1)S(1)} %collective-permute-done.3), channel_id=1, source_target_pairs={{0,224},{8,232},{16,240},{24,248},{32,0},{40,8},{48,16},{56,24},{6... | collective-permute-start | bytes 393224 | tf_op jit(solution)/shard_map/ppermute | solution.py:22
  20.6 5.0 %collective-permute-start.10 = (bf16[16,4096]{1,0:T(8,128)(2,1)S(1)}, bf16[16,4096]{1,0:T(8,128)(2,1)S(1)}, u32[]{:S(2)}, u32[]{:S(2)}) collective-permute-start(bf16[16,4096]{1,0:T(8,128)(2,1)S(1)} %collective-permute-done.6), channel_id=1, source_target_pairs={{0,32},{8,40},{16,48},{24,56},{32,64},{40,72},{48,80},{56,88},{64,... | collective-permute-start | bytes 393224 | tf_op jit(solution)/shard_map/ppermute | solution.py:22
  20.7 6.3 %collective-permute-start.11 = (bf16[16,4096]{1,0:T(8,128)(2,1)S(1)}, bf16[16,4096]{1,0:T(8,128)(2,1)S(1)}, u32[]{:S(2)}, u32[]{:S(2)}) collective-permute-start(bf16[16,4096]{1,0:T(8,128)(2,1)S(1)} %collective-permute-done.7), channel_id=1, source_target_pairs={{0,224},{8,232},{16,240},{24,248},{32,0},{40,8},{48,16},{56,24},{6... | collective-permute-start | bytes 393224 | tf_op jit(solution)/shard_map/ppermute | solution.py:22
  25.7 12.8 %collective-permute-start.8 = (bf16[32,4096]{1,0:T(8,128)(2,1)S(1)}, bf16[32,4096]{1,0:T(8,128)(2,1)S(1)}, u32[]{:S(2)}, u32[]{:S(2)}) collective-permute-start(bf16[32,4096]{1,0:T(8,128)(2,1)S(1)} %pad_maximum_fusion.5), channel_id=1, source_target_pairs={{0,16},{8,24},{16,0},{24,8},{32,48},{40,56},{48,32},{56,40},{64,80... | collective-permute-start | bytes 786440 | tf_op jit(solution)/shard_map/ppermute | solution.py:22
  27.0 16.2 %collective-permute-start.12 = (bf16[32,4096]{1,0:T(8,128)(2,1)S(1)}, bf16[32,4096]{1,0:T(8,128)(2,1)S(1)}, u32[]{:S(2)}, u32[]{:S(2)}) collective-permute-start(bf16[32,4096]{1,0:T(8,128)(2,1)S(1)} %pad_maximum_fusion.6), channel_id=1, source_target_pairs={{0,16},{8,24},{16,0},{24,8},{32,48},{40,56},{48,32},{56,40},{64,80... | collective-permute-start | bytes 786440 | tf_op jit(solution)/shard_map/ppermute | solution.py:22
  27.3 16.2 %collective-permute-start.5 = (bf16[64,4096]{1,0:T(8,128)(2,1)S(1)}, bf16[64,4096]{1,0:T(8,128)(2,1)S(1)}, u32[]{:S(2)}, u32[]{:S(2)}) collective-permute-start(bf16[64,4096]{1,0:T(8,128)(2,1)S(1)} %pad_maximum_fusion), channel_id=1, source_target_pairs={{0,8},{8,0},{16,24},{24,16},{32,40},{40,32},{48,56},{56,48},{64,72... | collective-permute-start | bytes 1572872 | tf_op jit(solution)/shard_map/ppermute | solution.py:22
  30.8 6.4 %collective-permute-start.14 = (bf16[16,4096]{1,0:T(8,128)(2,1)S(1)}, bf16[16,4096]{1,0:T(8,128)(2,1)S(1)}, u32[]{:S(2)}, u32[]{:S(2)}) collective-permute-start(bf16[16,4096]{1,0:T(8,128)(2,1)S(1)} %collective-permute-done.10), channel_id=1, source_target_pairs={{0,32},{8,40},{16,48},{24,56},{32,64},{40,72},{48,80},{56,88},{64,... | collective-permute-start | bytes 393224 | tf_op jit(solution)/shard_map/ppermute | solution.py:22
  38.5 5.2 %collective-permute-start.9 = (bf16[64,4096]{1,0:T(8,128)(2,1)S(1)}, bf16[64,4096]{1,0:T(8,128)(2,1)S(1)}, u32[]{:S(2)}, u32[]{:S(2)}) collective-permute-start(bf16[64,4096]{1,0:T(8,128)(2,1)S(1)} %pad_maximum_fusion.1), channel_id=1, source_target_pairs={{0,8},{8,0},{16,24},{24,16},{32,40},{40,32},{48,56},{56,48},{64,72... | collective-permute-start | bytes 1572872 | tf_op jit(solution)/shard_map/ppermute | solution.py:22
  49.3 16.2 %all-to-all-start.1 = ((bf16[8,128,192]{1,2,0:T(8,128)(2,1)}), bf16[8,128,192]{1,2,0:T(8,128)(2,1)S(1)}, u32[]{:S(2)}, u32[]{:S(2)}) async-start(bf16[8,128,192]{1,2,0:T(8,128)(2,1)} %bitcast.70), calls=%async_computation.1 | async-start | bytes 786432 | tf_op jit(solution)/shard_map/all_to_all | solution.py:110
  65.5 17.0 %all-to-all-start = ((bf16[8,128,320]{1,2,0:T(8,128)(2,1)}), bf16[8,128,320]{1,2,0:T(8,128)(2,1)S(1)}, u32[]{:S(2)}, u32[]{:S(2)}) async-start(bf16[8,128,320]{1,2,0:T(8,128)(2,1)} %bitcast.69), calls=%async_computation | async-start | bytes 1310720 | tf_op jit(solution)/shard_map/all_to_all | solution.py:110
  83.8 19.1 %all-to-all-start.2 = ((bf16[8,128,512]{2,1,0:T(8,128)(2,1)}), bf16[8,128,512]{2,1,0:T(8,128)(2,1)S(1)}, u32[]{:S(2)}, u32[]{:S(2)}) async-start(bf16[8,128,512]{2,1,0:T(8,128)(2,1)} %broadcast_in_dim.2), calls=%async_computation.2 | async-start | bytes 2097152 | tf_op jit(solution)/shard_map/all_to_all | solution.py:115
  109.1 6.1 %collective-permute-start.17 = (bf16[512,1024]{0,1:T(8,128)(2,1)S(1)}, bf16[512,1024]{0,1:T(8,128)(2,1)S(1)}, u32[]{:S(2)}, u32[]{:S(2)}) collective-permute-start(bf16[512,1024]{0,1:T(8,128)(2,1)S(1)} %bitcast.79), channel_id=1, source_target_pairs={{0,8},{8,0},{16,24},{24,16},{32,40},{40,32},{48,56},{56,48},{64,72... | collective-permute-start | bytes 3145736 | tf_op jit(solution)/shard_map/ppermute | solution.py:22
  121.3 57.2 %all-to-all-start.3 = ((bf16[8,64,2048]{2,1,0:T(8,128)(2,1)}), bf16[8,64,2048]{2,1,0:T(8,128)(2,1)S(1)}, u32[]{:S(2)}, u32[]{:S(2)}) async-start(bf16[8,64,2048]{2,1,0:T(8,128)(2,1)} %bitcast.71), calls=%async_computation.3 | async-start | bytes 4194304 | tf_op jit(solution)/shard_map/all_to_all | solution.py:125
  135.2 40.2 %collective-permute-start.23 = (f32[125,128]{1,0:T(8,128)S(1)}, f32[125,128]{1,0:T(8,128)S(1)}, u32[]{:S(2)}, u32[]{:S(2)}) collective-permute-start(f32[125,128]{1,0:T(8,128)S(1)} %dynamic-slice_add_fusion.1), channel_id=1, source_target_pairs={{0,32},{8,40},{16,48},{24,56},{32,0},{40,8},{48,16},{56,24},{64,96... | collective-permute-start | bytes 192008 | tf_op jit(solution)/shard_map/ppermute | solution.py:27
  175.3 6.6 %collective-permute-start.24 = (f32[125,128]{1,0:T(8,128)S(1)}, f32[125,128]{1,0:T(8,128)S(1)}, u32[]{:S(2)}, u32[]{:S(2)}) collective-permute-start(f32[125,128]{1,0:T(8,128)S(1)} %add.539), channel_id=1, source_target_pairs={{0,64},{8,72},{16,80},{24,88},{32,96},{40,104},{48,112},{56,120},{... | collective-permute-start | bytes 192008 | tf_op jit(solution)/shard_map/ppermute | solution.py:27
  179.7 15.4 %collective-permute-start.19 = (f32[32,2048]{1,0:T(8,128)S(1)}, f32[32,2048]{1,0:T(8,128)S(1)}, u32[]{:S(2)}, u32[]{:S(2)}) collective-permute-start(f32[32,2048]{1,0:T(8,128)S(1)} %dynamic-slice_bitcast_fusion), channel_id=1, source_target_pairs={{0,16},{8,24},{16,0},{24,8},{32,48},{40,56},{48,32},{56,40},{64,80... | collective-permute-start | bytes 786440 | tf_op jit(solution)/shard_map/ppermute | solution.py:22
  181.9 7.1 %collective-permute-start.25 = (f32[125,128]{1,0:T(8,128)S(1)}, f32[125,128]{1,0:T(8,128)S(1)}, u32[]{:S(2)}, u32[]{:S(2)}) collective-permute-start(f32[125,128]{1,0:T(8,128)S(1)} %add.540), channel_id=1, source_target_pairs={{0,128},{8,136},{16,144},{24,152},{32,160},{40,168},{48,176},{56,1... | collective-permute-start | bytes 192008 | tf_op jit(solution)/shard_map/ppermute | solution.py:27
  (16 other events, 229.3 us)

commit v2 on v0

v2 whole, which is shorter than its diff:
```python
import math

import jax
import jax.numpy as jnp
from jax import lax
from jax.experimental import pallas as pl
from jax.experimental.pallas import tpu as pltpu
from jax.sharding import PartitionSpec as P

FEATURES = 32768
LOW = jnp.bfloat16
FULL = jnp.float32
DEPTH, PAIR, CORES = 8, 2, 2
FAR = DEPTH // 2
RING = (4, 3, -3, 2, -2, 1, -1, 0)


def tgt_move(array, dz, dy, dc):
    pairs = []
    for z in range(DEPTH):
        for y in range(PAIR):
            for c in range(CORES):
                source = (z * PAIR + y) * CORES + c
                target = ((z + dz) % DEPTH * PAIR + (y + dy) % PAIR) * CORES + (c + dc) % CORES
                pairs.append((source, target))
    return lax.ppermute(array, "tgt", pairs)


def place():
    index = lax.axis_index("tgt")
    return index // (PAIR * CORES), index // CORES % PAIR, index % CORES


def together(*values):
    return lax.optimization_barrier(values)


def dot(a, b, left, right):
    return lax.dot_general(a, b, (((left,), (right,)), ((), ())), preferred_element_type=FULL)


def call(kernel, out, grid, in_specs, out_specs, flops, bytes_accessed, scratch=(), prefetch=0):
    return pl.pallas_call(
        kernel,
        out_shape=out,
        grid_spec=pltpu.PrefetchScalarGridSpec(
            num_scalar_prefetch=prefetch, grid=grid, in_specs=in_specs, out_specs=out_specs, scratch_shapes=list(scratch)
        ),
        compiler_params=pltpu.CompilerParams(dimension_semantics=("arbitrary",), vmem_limit_bytes=48 * 2**20),
        cost_estimate=pl.CostEstimate(flops=flops, bytes_accessed=bytes_accessed, transcendentals=0),
    )


def kernel_part(target_feats, pieces, scale, kind, blks):
    targets, features = target_feats.shape
    rows = sum(p.shape[0] for p in pieces)
    count = len(pieces)
    tile = 256
    block = targets // blks
    per = tile // block

    def body(*refs):
        feats, parts, out, held, sem = refs[0], refs[1 : 1 + count], refs[1 + count], refs[2 + count], refs[3 + count]

        @pl.when(pl.program_id(0) == 0)
        def _():
            copies, start = [], 0
            for i, part in enumerate(parts):
                copies.append(pltpu.make_async_copy(part, held.at[pl.ds(start, part.shape[0])], sem.at[i]))
                start += part.shape[0]
            for copy in copies:
                copy.start()
            for copy in copies:
                copy.wait()

        product = lax.dot_general(feats[...], held[...], (((1,), (1,)), ((), ())), preferred_element_type=FULL)
        out[...] = (product * scale).astype(kind).reshape(per, block, rows)

    return call(
        body,
        jax.ShapeDtypeStruct((blks, block, rows), kind),
        (targets // tile,),
        [pl.BlockSpec((tile, features), lambda i: (i, 0))] + [pl.BlockSpec(memory_space=pl.ANY)] * count,
        pl.BlockSpec((per, block, rows), lambda i: (i, 0, 0)),
        2 * targets * features * rows,
        2 * features * (targets + rows) + 4 * targets * rows,
        [pltpu.VMEM((rows, features), LOW), pltpu.SemaphoreType.DMA((count,))],
    )(target_feats, *pieces)


def take_half(target_feats, which):
    targets, features = target_feats.shape
    tile = targets // 8

    def body(which_ref, feats, out):
        out[...] = feats[...]

    return call(
        body,
        jax.ShapeDtypeStruct((targets, features // 2), LOW),
        (8,),
        [pl.BlockSpec((tile, features // 2), lambda i, w: (i, w[0]))],
        pl.BlockSpec((tile, features // 2), lambda i, w: (i, 0)),
        0,
        2 * targets * features,
        prefetch=1,
    )(which, target_feats)


def gradients(kernel_low, labels, coefs_here, coefs_ring, own_coefs, order, first_class):
    targets, supports = kernel_low.shape
    padded = coefs_here.shape[0]
    own = own_coefs.shape[0]
    tile = 256
    nt = (((1,), (1,)), ((), ()))

    def body(first_ref, low, column, row, here, ring, mine, order_ref, grad, part):
        predict = lax.dot_general(low[...], here[...], nt, preferred_element_type=FULL)
        ids = lax.broadcasted_iota(jnp.int32, (tile, padded), 1)
        residual = jnp.where(ids == column[...], predict - 1.0, predict).astype(LOW)
        grad[...] = lax.dot_general(ring[...], residual, nt, preferred_element_type=FULL).astype(LOW)
        predict = lax.dot_general(mine[...], low[...], nt, preferred_element_type=FULL)
        ids = lax.broadcasted_iota(jnp.int32, (own, tile), 0) + first_ref[0]
        residual = jnp.where(ids == row[...], predict - 1.0, predict).astype(LOW)
        ordered = jnp.dot(low[...], order_ref[...], preferred_element_type=FULL).astype(LOW)
        product = jnp.dot(residual, ordered, preferred_element_type=FULL)

        @pl.when(pl.program_id(0) == 0)
        def _():
            part[...] = product

        @pl.when(pl.program_id(0) > 0)
        def _():
            part[...] += product

    whole = lambda i, f: (0, 0)
    return call(
        body,
        (jax.ShapeDtypeStruct((supports, targets), LOW), jax.ShapeDtypeStruct((own, supports), FULL)),
        (targets // tile,),
        [
            pl.BlockSpec((tile, supports), lambda i, f: (i, 0)),
            pl.BlockSpec((tile, 1), lambda i, f: (i, 0)),
            pl.BlockSpec((1, tile), lambda i, f: (0, i)),
            pl.BlockSpec((padded, supports), whole),
            pl.BlockSpec((supports, padded), whole),
            pl.BlockSpec((own, supports), whole),
            pl.BlockSpec((supports, supports), whole),
        ],
        (pl.BlockSpec((supports, tile), lambda i, f: (0, i)), pl.BlockSpec((own, supports), whole)),
        2 * targets * supports * (2 * padded + supports),
        2 * supports * (2 * targets + 3 * padded),
        prefetch=1,
    )(first_class, kernel_low, labels[:, None], labels[None, :], coefs_here, coefs_ring, own_coefs, order)


def support_part(own_grad, other_grad, target_feats, taken, which, start, count):
    targets, features = target_feats.shape
    half = features // 2
    tile = 512
    steps = half // tile

    def body(which_ref, own, other, feats, theirs, out):
        rows = pl.ds(start, count)
        out[...] = jnp.dot(own[rows, :], feats[...], preferred_element_type=FULL) + jnp.dot(
            other[rows, :], theirs[...], preferred_element_type=FULL
        )

    whole = lambda i, w: (0, 0)
    return call(
        body,
        jax.ShapeDtypeStruct((count, half), FULL),
        (steps,),
        [
            pl.BlockSpec(own_grad.shape, whole),
            pl.BlockSpec(other_grad.shape, whole),
            pl.BlockSpec((targets, tile), lambda i, w: (0, w[0] * steps + i)),
            pl.BlockSpec((targets, tile), lambda i, w: (0, i)),
        ],
        pl.BlockSpec((count, tile), lambda i, w: (0, i)),
        4 * count * targets * half,
        4 * targets * half + 4 * count * half,
        prefetch=1,
    )(which, own_grad, other_grad, target_feats, taken)


def order_matrix(shards, rows):
    ids = (jnp.stack(shards)[:, None] * rows + jnp.arange(rows)[None, :]).reshape(-1)
    return (ids[:, None] == jnp.arange(ids.shape[0])[None, :]).astype(LOW)


def split(array, which):
    half = array.shape[1] // 2
    left, right = array[:, :half], array[:, half:]
    return jnp.where(which == 0, left, right), jnp.where(which == 0, right, left)


def join(mine, other, which):
    return jnp.where(which == 0, jnp.concatenate([mine, other], 1), jnp.concatenate([other, mine], 1))


def sums(factors, coef, rows):
    z, y, c = place()
    chip_rows = rows * PAIR * CORES
    wide = factors[3].shape[1]
    half = wide // 2

    keep, give = split(coef, c)
    coef = keep + tgt_move(give, 0, 0, 1)
    keep, give = split(coef, y)
    coef = keep + tgt_move(give, 0, 1, 0)

    partial, start = {}, 0
    for count in (3, 5):
        product = support_part(*factors, start * chip_rows, count * chip_rows)
        for i in range(count):
            partial[RING[start + i]] = product[i * chip_rows : (i + 1) * chip_rows]
        start += count

    far = partial[FAR].astype(LOW)
    up, coef_up = together(far[:, :half], coef)
    down, coef_down = together(far[:, half:], coef)
    total = coef
    for step in range(FAR, 0, -1):
        if step < FAR:
            above, below = partial[step], partial[-step]
            if step == FAR - 1:
                above = jnp.concatenate([above[:, :half] + up.astype(FULL), above[:, half:]], 1)
                below = jnp.concatenate([below[:, :half], below[:, half:] + down.astype(FULL)], 1)
            else:
                above, below = above + up.astype(FULL), below + down.astype(FULL)
            up, coef_up = together(above.astype(LOW), coef_up)
            down, coef_down = together(below.astype(LOW), coef_down)
        up, coef_up = tgt_move(up, 1, 0, 0), tgt_move(coef_up, 1, 0, 0)
        down = tgt_move(down, -1, 0, 0)
        total = total + coef_up
        if step > 1:
            coef_down = tgt_move(coef_down, -1, 0, 0)
            total = total + coef_down
    mine = (partial[0] + up.astype(FULL) + down.astype(FULL)).reshape(PAIR, CORES * rows, wide)
    give, total = together(mine[1].astype(LOW), total)
    mine = (mine[0] + tgt_move(give, 0, 1, 0).astype(FULL)).reshape(CORES, rows, wide)
    total = join(total, tgt_move(total, 0, 1, 0), y)
    here = jnp.where(c == 0, mine[0], mine[1])
    give, total = together(jnp.where(c == 0, mine[1], mine[0]), total)
    support = join(here, tgt_move(give, 0, 0, 1), c)
    return support, join(total, tgt_move(total, 0, 0, 1), c)


def shards(target_feats, support_feats, coefs, labels):
    scale = 1.0 / math.sqrt(FEATURES)
    classes = coefs.shape[0]
    targets, features = target_feats.shape
    rows = support_feats.shape[0]
    blks = lax.axis_size("blk")
    tgts = lax.axis_size("tgt")
    blk_index = lax.axis_index("blk")
    z, y, c = place()

    half = features // 2
    padded = -(-classes // 128) * 128

    pair = jnp.concatenate([support_feats, tgt_move(support_feats, 0, 1, 0)], 0)
    up = down = pair
    pieces = [(pair, 0, 0), (tgt_move(pair, 0, 0, 1), 0, 1)]

    def parts(some, kind):
        return kernel_part(target_feats, [p for p, _, _ in some], scale, kind, blks)

    def offsets(some):
        return [(dz, dy, dc) for _, dz, dc in some for dy in range(PAIR)]

    for step in range(1, FAR):
        up, down = tgt_move(up, 1, 0, 0), tgt_move(down, -1, 0, 0)
        if step == 1:
            late_c, up, down = together(c, up, down)
            give = take_half(target_feats, (1 - late_c)[None])
        if step == FAR - 1:
            near, part = pieces, parts(pieces, FULL)
            up, down, part = together(up, down, part)
            near_got = lax.all_to_all(part, "blk", 0, 0, tiled=True)
            pieces = []
        pieces += [(up, -step, 0), (down, step, 0), (tgt_move(up, 0, 0, 1), -step, 1), (tgt_move(down, 0, 0, 1), step, 1)]
    up, down = tgt_move(up[:, :half], 1, 0, 0), tgt_move(down[:, half:], -1, 0, 0)
    last = jnp.concatenate([up, down], 1)
    pieces += [(last, FAR, 0), (tgt_move(last, 0, 0, 1), FAR, 1)]
    far_part, give = together(parts(pieces, LOW), give)
    far_got = lax.all_to_all(far_part, "blk", 0, 0, tiled=True)
    taken = tgt_move(give, 0, 0, 1)

    order = order_matrix(
        [((z + dz) % DEPTH * PAIR + (y + dy) % PAIR) * CORES + (c + dc) % CORES for dz, dy, dc in offsets(near + pieces)], rows
    )
    ring_order = order_matrix(
        [((z + dz) % DEPTH * PAIR + (y + dy) % PAIR) * CORES + dc for dz in RING for dy in range(PAIR) for dc in range(CORES)], rows
    )
    class_rows = classes // blks
    first_class = blk_index * class_rows
    all_coefs = jnp.pad(coefs, ((0, padded - classes), (0, 0)))
    coefs_here = dot(all_coefs, order, 1, 1).astype(LOW)
    coefs_ring = dot(ring_order, all_coefs, 1, 1).astype(LOW)
    own_coefs = lax.dynamic_slice_in_dim(coefs_here, first_class, class_rows, 0)

    own_low = jnp.concatenate([jnp.sum(got.astype(FULL), 0).astype(LOW) for got in (near_got, far_got)], 1)
    spread = jnp.broadcast_to(own_low[None], (blks,) + own_low.shape)
    kernel_low = lax.all_to_all(spread, "blk", 0, 0, tiled=True).reshape(targets, -1)

    kernel_grad, coef_part = gradients(kernel_low, labels, coefs_here, coefs_ring, own_coefs, order, first_class[None])
    other_grad = tgt_move(kernel_grad, 0, 0, 1)
    factors = (kernel_grad, other_grad, target_feats, taken, c[None])
    support_grad, coef_grad = sums(factors, coef_part, rows)
    return support_grad * scale, coef_grad / math.sqrt(targets * tgts)


def solution(mesh):
    in_specs = (P("tgt", "blk"), P("tgt", "blk"), P(), P("tgt"))
    out_specs = (P("tgt", "blk"), P("blk", None))
    return jax.shard_map(shards, mesh=mesh, in_specs=in_specs, out_specs=out_specs, check_vma=False)
```

time: 557 us -> 203 us (0.36)
  waiting for transfers between devices: 423 us -> 77.9 us
  blocking collectives: 92 us -> 0 us
  starting transfers between devices: 0.12 us -> 70.2 us
  Pallas kernels: 0 us -> 35.8 us
  matrix products: 23.2 us -> 3.81 us
  between operations: 13.8 us -> 1.28 us
  local copies, waits for them, and re-layouts: 0.02 us -> 10.4 us
    psum x1 -> x0, waiting for transfers between devices: 220 us -> none  [shards(): coef_grad = lax.psum(coef_part, 'tgt') / root_count]
    reduce_scatter x1 -> x0, waiting for transfers between devices: 129 us -> none  [shards(): lax.psum_scatter(jnp.dot(kernel_grad, target_feats, preferred_element_typ...]
    psum x1 -> x0, blocking collectives: 92 us -> none  [shards(): kernel = lax.psum(partial_kernel, 'blk')]
    all_gather x1 -> x0, waiting for transfers between devices: 73 us -> none  [shards(): lax.all_gather(support_feats, 'tgt', axis=0, tiled=True)]
    ppermute x0 -> x40, starting transfers between devices: none -> 56 us  [tgt_move(): return lax.ppermute(array, 'tgt', pairs)]
    ppermute x0 -> x40, waiting for transfers between devices: none -> 42.7 us  [tgt_move(): return lax.ppermute(array, 'tgt', pairs)]
    pallas_call x0 -> x6, Pallas kernels: none -> 35.8 us  [the longest x2 13.1 us: kernel_part(): call(body, jax.ShapeDtypeStruct((blks, block, rows), kind), (targets // t...]
    all_to_all x0 -> x3, waiting for transfers between devices: none -> 35.2 us  [the longest x1 17.6 us: shards(): near_got = lax.all_to_all(part, 'blk', 0, 0, tiled=True)]
  transfers between devices with their start and end apart: 3 -> 43, of which waited for: 3 -> 21; matrix products, arithmetic and copies ran while one was open for 2% -> 5% of each run, Pallas kernels for 0% -> 12%
where the time goes in v2:
time: 203 us; the launch traced here: 202 us
  waiting for transfers between devices  77.9 us (38%)
  starting transfers between devices  70.2 us (35%)
  Pallas kernels  35.8 us (18%)
  local copies, waits for them, and re-layouts  10.4 us (5%)
  matrix products  3.81 us (2%)
  other arithmetic  2.54 us (1%)
    ppermute x40, starting transfers between devices, tgt_move(): return lax.ppermute(array, 'tgt', pairs)  56 us
    ppermute x40, waiting for transfers between devices, tgt_move(): return lax.ppermute(array, 'tgt', pairs)  42.7 us
    all_to_all x1, waiting for transfers between devices, shards(): near_got = lax.all_to_all(part, 'blk', 0, 0, tiled=True)  17.6 us
    pallas_call x2, Pallas kernels, kernel_part(): call(body, jax.ShapeDtypeStruct((blks, block, rows), kind), (targets // t...  13.1 us
    pallas_call x2, Pallas kernels, support_part(): call(body, jax.ShapeDtypeStruct((count, half), FULL), (steps,), [pl.Block...  11.1 us
    all_to_all x1, waiting for transfers between devices, shards(): lax.all_to_all(spread, 'blk', 0, 0, tiled=True).reshape(targets, -1)  10 us
    all_to_all x1, waiting for transfers between devices, shards(): far_got = lax.all_to_all(far_part, 'blk', 0, 0, tiled=True)  7.61 us
    all_to_all x1, starting transfers between devices, shards(): far_got = lax.all_to_all(far_part, 'blk', 0, 0, tiled=True)  6.65 us
  transfers between devices with their start and end apart: 43, of which 21 were waited for; matrix products, arithmetic and copies ran while one was open for 5% of the time, Pallas kernels for 12%

profile of v2, /device:TPU:1, one launch (start us, length us, event | category | flops | bytes accessed | tf_op | source)
XLA Modules:
  0.0 202.0 jit_solution(16084903698091446105)
XLA Ops:
  5.4 6.4 %collective-permute-start.2 = (bf16[32,4096]{1,0:T(8,128)(2,1)S(1)}, bf16[32,4096]{1,0:T(8,128)(2,1)S(1)}, u32[]{:S(2)}, u32[]{:S(2)}) collective-permute-start(bf16[32,4096]{1,0:T(8,128)(2,1)S(1)} %constant_dynamic-update-slice_fusion.refs_1_), channel_id=1, source_target_pairs={{0,224},{8,232},{16,240},{24,248},{32,0},{40,8},{48,16},{56,24},{6... | collective-permute-start | bytes 786440 | tf_op jit(solution)/shard_map/ppermute | solution.py:26
  11.8 4.0 %collective-permute-done.2.refs_4_ = bf16[32,4096]{1,0:T(8,128)(2,1)S(1)} collective-permute-done((bf16[32,4096]{1,0:T(8,128)(2,1)S(1)}, bf16[32,4096]{1,0:T(8,128)(2,1)S(1)}, u32[]{:S(2)}, u32[]{:S(2)}) %collective-permute-start.2) | collective-permute-done | bytes 262176 | tf_op jit(solution)/shard_map/ppermute | solution.py:26
  15.8 3.1 %collective-permute-done.1.refs_3_ = bf16[32,4096]{1,0:T(8,128)(2,1)S(1)} collective-permute-done((bf16[32,4096]{1,0:T(8,128)(2,1)S(1)}, bf16[32,4096]{1,0:T(8,128)(2,1)S(1)}, u32[]{:S(2)}, u32[]{:S(2)}) %collective-permute-start.1) | collective-permute-done | bytes 262176 | tf_op jit(solution)/shard_map/ppermute | solution.py:26
  21.6 3.3 %collective-permute-start.7 = (bf16[32,4096]{1,0:T(8,128)(2,1)S(1)}, bf16[32,4096]{1,0:T(8,128)(2,1)S(1)}, u32[]{:S(2)}, u32[]{:S(2)}) collective-permute-start(bf16[32,4096]{1,0:T(8,128)(2,1)S(1)} %constant_dynamic-update-slice_fusion.refs_1_), channel_id=1, source_target_pairs={{0,8},{8,0},{16,24},{24,16},{32,40},{40,32},{48,56},{56,48},{64,72... | collective-permute-start | bytes 786440 | tf_op jit(solution)/shard_map/ppermute | solution.py:26
  25.5 3.8 %collective-permute-start.10 = (bf16[32,4096]{1,0:T(8,128)(2,1)S(1)}, bf16[32,4096]{1,0:T(8,128)(2,1)S(1)}, u32[]{:S(2)}, u32[]{:S(2)}) collective-permute-start(bf16[32,4096]{1,0:T(8,128)(2,1)S(1)} %collective-permute-done.3.refs_7_), channel_id=1, source_target_pairs={{0,8},{8,0},{16,24},{24,16},{32,40},{40,32},{48,56},{56,48},{64,72... | collective-permute-start | bytes 786440 | tf_op jit(solution)/shard_map/ppermute | solution.py:26
  29.4 2.9 %collective-permute-start.6 = (bf16[32,4096]{1,0:T(8,128)(2,1)S(1)}, bf16[32,4096]{1,0:T(8,128)(2,1)S(1)}, u32[]{:S(2)}, u32[]{:S(2)}) collective-permute-start(bf16[32,4096]{1,0:T(8,128)(2,1)S(1)} %collective-permute-done.5.refs_8_), channel_id=1, source_target_pairs={{0,224},{8,232},{16,240},{24,248},{32,0},{40,8},{48,16},{56,24},{6... | collective-permute-start | bytes 786440 | tf_op jit(solution)/shard_map/ppermute | solution.py:26
  32.4 7.4 %shard_map.59 = f32[8,128,320]{2,1,0:T(8,128)S(1)} custom-call(bf16[1024,4096]{1,0:T(8,128)(2,1)} %feats.5, bf16[32,4096]{1,0:T(8,128)(2,1)S(1)} %constant_dynamic-update-slice_fusion.refs_1_, bf16[32,4096]{1,0:T(8,128)(2,1)S(1)} %collective-permute-done.7.refs_2_, bf16[32,4096]{1,0:T(8,128)(2,1)S(1)} %collective-permute-done.1.refs_3_, ...), custom_call_target="tpu_custom_call" | custom-call | flops 2684354560 | bytes 12320768 | tf_op jit(solution)/shard_map/pallas_call | solution.py:79
  40.8 2.9 %collective-permute-start.15 = (bf16[32,2048]{1,0:T(8,128)(2,1)S(1)}, bf16[32,2048]{1,0:T(8,128)(2,1)S(1)}, u32[]{:S(2)}, u32[]{:S(2)}) collective-permute-start(bf16[32,2048]{1,0:T(8,128)(2,1)S(1)} %slice.83), channel_id=1, source_target_pairs={{0,224},{8,232},{16,240},{24,248},{32,0},{40,8},{48,16},{56,24},{6... | collective-permute-start | bytes 393224 | tf_op jit(solution)/shard_map/ppermute | solution.py:26
  47.7 6.6 %shard_map.61 = bf16[1024,2048]{1,0:T(8,128)(2,1)} custom-call(s32[1]{0:T(128)} %bitcast.2.which_ref, bf16[1024,4096]{1,0:T(8,128)(2,1)} %feats.5), custom_call_target="tpu_custom_call" | custom-call | bytes 8388608 | tf_op jit(solution)/shard_map/pallas_call | solution.py:98
  56.0 5.7 %shard_map.60 = bf16[8,128,192]{2,1,0:T(8,128)(2,1)S(1)} custom-call(bf16[1024,4096]{1,0:T(8,128)(2,1)} %feats.5, bf16[32,4096]{1,0:T(8,128)(2,1)S(1)} %collective-permute-done.4.refs_1_, bf16[32,4096]{1,0:T(8,128)(2,1)S(1)} %collective-permute-done.6.refs_2_, bf16[32,4096]{1,0:T(8,128)(2,1)S(1)} %collective-permute-done.12.refs_3_, ...), custom_call_target="tpu_custom_call" | custom-call | flops 1610612736 | bytes 10747904 | tf_op jit(solution)/shard_map/pallas_call | solution.py:79
  62.8 6.6 %all-to-all-start.1 = ((bf16[8,128,192]{1,2,0:T(8,128)(2,1)}), bf16[8,128,192]{1,2,0:T(8,128)(2,1)S(1)}, u32[]{:S(2)}, u32[]{:S(2)}) async-start(bf16[8,128,192]{1,2,0:T(8,128)(2,1)} %copy.11), calls=%async_computation.1 | async-start | bytes 786432 | tf_op jit(solution)/shard_map/all_to_all | solution.py:288
  71.0 7.6 %all-to-all-done.1 = bf16[8,128,192]{1,2,0:T(8,128)(2,1)S(1)} async-done(((bf16[8,128,192]{1,2,0:T(8,128)(2,1)}), bf16[8,128,192]{1,2,0:T(8,128)(2,1)S(1)}, u32[]{:S(2)}, u32[]{:S(2)}) %all-to-all-start.1) | async-done | bytes 393248 | tf_op jit(solution)/shard_map/all_to_all | solution.py:288
  78.6 3.6 %all-to-all-start = ((f32[8,128,320]{1,2,0:T(8,128)}), f32[8,128,320]{1,2,0:T(8,128)S(1)}, u32[]{:S(2)}, u32[]{:S(2)}) async-start(f32[8,128,320]{1,2,0:T(8,128)} %copy.10), calls=%async_computation | async-start | bytes 2621440 | tf_op jit(solution)/shard_map/all_to_all | solution.py:281
  82.8 17.6 %all-to-all-done = f32[8,128,320]{1,2,0:T(8,128)S(1)} async-done(((f32[8,128,320]{1,2,0:T(8,128)}), f32[8,128,320]{1,2,0:T(8,128)S(1)}, u32[]{:S(2)}, u32[]{:S(2)}) %all-to-all-start) | async-done | bytes 1310752 | tf_op jit(solution)/shard_map/all_to_all | solution.py:281
  101.7 4.0 %all-to-all-start.2 = ((bf16[8,128,512]{2,1,0:T(8,128)(2,1)}), bf16[8,128,512]{2,1,0:T(8,128)(2,1)S(1)}, u32[]{:S(2)}, u32[]{:S(2)}) async-start(bf16[8,128,512]{2,1,0:T(8,128)(2,1)} %broadcast_in_dim.30), calls=%async_computation.2 | async-start | bytes 2097152 | tf_op jit(solution)/shard_map/all_to_all | solution.py:306
  111.2 10.0 %all-to-all-done.2 = bf16[8,128,512]{2,1,0:T(8,128)(2,1)S(1)} async-done(((bf16[8,128,512]{2,1,0:T(8,128)(2,1)}), bf16[8,128,512]{2,1,0:T(8,128)(2,1)S(1)}, u32[]{:S(2)}, u32[]{:S(2)}) %all-to-all-start.2) | async-done | bytes 1048608 | tf_op jit(solution)/shard_map/all_to_all | solution.py:306
  123.6 5.0 %shard_map.62 = (bf16[512,1024]{1,0:T(8,128)(2,1)S(1)}, f32[125,512]{1,0:T(8,128)S(1)}) custom-call(s32[1]{0:T(128)} %bitcast.1.first_ref, bf16[1024,512]{1,0:T(8,128)(2,1)S(1)} %bitcast.70, s32[1024,1]{1,0:T(8,128)S(1)} %copy.13.column, s32[1,1024]{1,0:T(1,128)S(1)} %bitcast.72, bf16[1024,512]{1,0:T(8,128)(2,1)S(1)} %copy-done.3, ...), custom_call_target="tpu_custom_call" | custom-call | flops 2684354560 | bytes 5242880 | tf_op jit(solution)/shard_map/pallas_call | solution.py:137
  135.8 5.1 %shard_map.64 = f32[192,2048]{1,0:T(8,128)S(1)} custom-call(s32[1]{0:T(128)} %bitcast.which_ref, bf16[512,1024]{1,0:T(8,128)(2,1)S(1)} %get-tuple-element.38.own, bf16[512,1024]{1,0:T(8,128)(2,1)S(1)} %collective-permute-done.17.other, bf16[1024,4096]{1,0:T(8,128)(2,1)} %feats.5, bf16[1024,2048]{1,0:T(8,128)(2,1)} %collective-permute-done.18.theirs), custom_call_target="tpu_custom_call" | custom-call | flops 1610612736 | bytes 9961472 | tf_op jit(solution)/shard_map/pallas_call | solution.py:170
  141.1 3.5 %collective-permute-start.28 = (bf16[64,1024]{1,0:T(8,128)(2,1)S(1)}, bf16[64,1024]{1,0:T(8,128)(2,1)S(1)}, u32[]{:S(2)}, u32[]{:S(2)}) collective-permute-start(bf16[64,1024]{1,0:T(8,128)(2,1)S(1)} %get-tuple-element.48), channel_id=1, source_target_pairs={{0,224},{8,232},{16,240},{24,248},{32,0},{40,8},{48,16},{56,24},{6... | collective-permute-start | bytes 393224 | tf_op jit(solution)/shard_map/ppermute | solution.py:26
  152.5 5.9 %shard_map.63 = f32[320,2048]{1,0:T(8,128)S(1)} custom-call(s32[1]{0:T(128)} %bitcast.which_ref, bf16[512,1024]{1,0:T(8,128)(2,1)S(1)} %get-tuple-element.38.own, bf16[512,1024]{1,0:T(8,128)(2,1)S(1)} %collective-permute-done.17.other, bf16[1024,4096]{1,0:T(8,128)(2,1)} %feats.5, bf16[1024,2048]{1,0:T(8,128)(2,1)} %collective-permute-done.18.theirs), custom_call_target="tpu_custom_call" | custom-call | flops 2684354560 | bytes 11010048 | tf_op jit(solution)/shard_map/pallas_call | solution.py:170
  165.7 3.8 %collective-permute-done.25 = bf16[64,2048]{1,0:T(8,128)(2,1)S(1)} collective-permute-done((bf16[64,2048]{1,0:T(8,128)(2,1)S(1)}, bf16[64,2048]{1,0:T(8,128)(2,1)S(1)}, u32[]{:S(2)}, u32[]{:S(2)}) %collective-permute-start.25) | collective-permute-done | bytes 262176 | tf_op jit(solution)/shard_map/ppermute | solution.py:26
  171.1 4.2 %collective-permute-done.26 = f32[125,128]{1,0:T(8,128)S(1)} collective-permute-done((f32[125,128]{1,0:T(8,128)S(1)}, f32[125,128]{1,0:T(8,128)S(1)}, u32[]{:S(2)}, u32[]{:S(2)}) %collective-permute-start.26) | collective-permute-done | bytes 64032 | tf_op jit(solution)/shard_map/ppermute | solution.py:26
  179.7 4.2 %collective-permute-done.27 = bf16[64,2048]{1,0:T(8,128)(2,1)S(1)} collective-permute-done((bf16[64,2048]{1,0:T(8,128)(2,1)S(1)}, bf16[64,2048]{1,0:T(8,128)(2,1)S(1)}, u32[]{:S(2)}, u32[]{:S(2)}) %collective-permute-start.27) | collective-permute-done | bytes 262176 | tf_op jit(solution)/shard_map/ppermute | solution.py:26
  189.7 9.8 %collective-permute-start.39 = (f32[125,256]{1,0:T(8,128)S(1)}, f32[125,256]{1,0:T(8,128)S(1)}, u32[]{:S(2)}, u32[]{:S(2)}) collective-permute-start(f32[125,256]{1,0:T(8,128)S(1)} %maximum_select_fusion.2), channel_id=1, source_target_pairs={{0,8},{8,0},{16,24},{24,16},{32,40},{40,32},{48,56},{56,48},{64,72... | collective-permute-start | bytes 384008 | tf_op jit(solution)/shard_map/ppermute | solution.py:26
  (128 shorter events, 63.4 us)
Async XLA Ops:
  5.4 10.4 %collective-permute-start.2 = (bf16[32,4096]{1,0:T(8,128)(2,1)S(1)}, bf16[32,4096]{1,0:T(8,128)(2,1)S(1)}, u32[]{:S(2)}, u32[]{:S(2)}) collective-permute-start(bf16[32,4096]{1,0:T(8,128)(2,1)S(1)} %constant_dynamic-update-slice_fusion.refs_1_), channel_id=1, source_target_pairs={{0,224},{8,232},{16,240},{24,248},{32,0},{40,8},{48,16},{56,24},{6... | collective-permute-start | bytes 786440 | tf_op jit(solution)/shard_map/ppermute | solution.py:26
  11.8 7.2 %collective-permute-start.1 = (bf16[32,4096]{1,0:T(8,128)(2,1)S(1)}, bf16[32,4096]{1,0:T(8,128)(2,1)S(1)}, u32[]{:S(2)}, u32[]{:S(2)}) collective-permute-start(bf16[32,4096]{1,0:T(8,128)(2,1)S(1)} %constant_dynamic-update-slice_fusion.refs_1_), channel_id=1, source_target_pairs={{0,32},{8,40},{16,48},{24,56},{32,64},{40,72},{48,80},{56,88},{64,... | collective-permute-start | bytes 786440 | tf_op jit(solution)/shard_map/ppermute | solution.py:26
  19.0 6.5 %collective-permute-start.3 = (bf16[32,4096]{1,0:T(8,128)(2,1)S(1)}, bf16[32,4096]{1,0:T(8,128)(2,1)S(1)}, u32[]{:S(2)}, u32[]{:S(2)}) collective-permute-start(bf16[32,4096]{1,0:T(8,128)(2,1)S(1)} %collective-permute-done.1.refs_3_), channel_id=1, source_target_pairs={{0,32},{8,40},{16,48},{24,56},{32,64},{40,72},{48,80},{56,88},{64,... | collective-permute-start | bytes 786440 | tf_op jit(solution)/shard_map/ppermute | solution.py:26
  19.0 10.3 %collective-permute-start.5 = (bf16[32,4096]{1,0:T(8,128)(2,1)S(1)}, bf16[32,4096]{1,0:T(8,128)(2,1)S(1)}, u32[]{:S(2)}, u32[]{:S(2)}) collective-permute-start(bf16[32,4096]{1,0:T(8,128)(2,1)S(1)} %collective-permute-done.2.refs_4_), channel_id=1, source_target_pairs={{0,224},{8,232},{16,240},{24,248},{32,0},{40,8},{48,16},{56,24},{6... | collective-permute-start | bytes 786440 | tf_op jit(solution)/shard_map/ppermute | solution.py:26
  21.6 7.7 %collective-permute-start.7 = (bf16[32,4096]{1,0:T(8,128)(2,1)S(1)}, bf16[32,4096]{1,0:T(8,128)(2,1)S(1)}, u32[]{:S(2)}, u32[]{:S(2)}) collective-permute-start(bf16[32,4096]{1,0:T(8,128)(2,1)S(1)} %constant_dynamic-update-slice_fusion.refs_1_), channel_id=1, source_target_pairs={{0,8},{8,0},{16,24},{24,16},{32,40},{40,32},{48,56},{56,48},{64,72... | collective-permute-start | bytes 786440 | tf_op jit(solution)/shard_map/ppermute | solution.py:26
  25.0 7.4 %collective-permute-start.9 = (bf16[32,4096]{1,0:T(8,128)(2,1)S(1)}, bf16[32,4096]{1,0:T(8,128)(2,1)S(1)}, u32[]{:S(2)}, u32[]{:S(2)}) collective-permute-start(bf16[32,4096]{1,0:T(8,128)(2,1)S(1)} %collective-permute-done.2.refs_4_), channel_id=1, source_target_pairs={{0,8},{8,0},{16,24},{24,16},{32,40},{40,32},{48,56},{56,48},{64,72... | collective-permute-start | bytes 786440 | tf_op jit(solution)/shard_map/ppermute | solution.py:26
  25.5 6.9 %collective-permute-start.10 = (bf16[32,4096]{1,0:T(8,128)(2,1)S(1)}, bf16[32,4096]{1,0:T(8,128)(2,1)S(1)}, u32[]{:S(2)}, u32[]{:S(2)}) collective-permute-start(bf16[32,4096]{1,0:T(8,128)(2,1)S(1)} %collective-permute-done.3.refs_7_), channel_id=1, source_target_pairs={{0,8},{8,0},{16,24},{24,16},{32,40},{40,32},{48,56},{56,48},{64,72... | collective-permute-start | bytes 786440 | tf_op jit(solution)/shard_map/ppermute | solution.py:26
  29.3 10.5 %collective-permute-start.4 = (bf16[32,4096]{1,0:T(8,128)(2,1)S(1)}, bf16[32,4096]{1,0:T(8,128)(2,1)S(1)}, u32[]{:S(2)}, u32[]{:S(2)}) collective-permute-start(bf16[32,4096]{1,0:T(8,128)(2,1)S(1)} %collective-permute-done.3.refs_7_), channel_id=1, source_target_pairs={{0,32},{8,40},{16,48},{24,56},{32,64},{40,72},{48,80},{56,88},{64,... | collective-permute-start | bytes 786440 | tf_op jit(solution)/shard_map/ppermute | solution.py:26
  29.4 10.4 %collective-permute-start.6 = (bf16[32,4096]{1,0:T(8,128)(2,1)S(1)}, bf16[32,4096]{1,0:T(8,128)(2,1)S(1)}, u32[]{:S(2)}, u32[]{:S(2)}) collective-permute-start(bf16[32,4096]{1,0:T(8,128)(2,1)S(1)} %collective-permute-done.5.refs_8_), channel_id=1, source_target_pairs={{0,224},{8,232},{16,240},{24,248},{32,0},{40,8},{48,16},{56,24},{6... | collective-permute-start | bytes 786440 | tf_op jit(solution)/shard_map/ppermute | solution.py:26
  39.9 14.5 %collective-permute-start.12 = (bf16[32,4096]{1,0:T(8,128)(2,1)S(1)}, bf16[32,4096]{1,0:T(8,128)(2,1)S(1)}, u32[]{:S(2)}, u32[]{:S(2)}) collective-permute-start(bf16[32,4096]{1,0:T(8,128)(2,1)S(1)} %collective-permute-done.4.refs_1_), channel_id=1, source_target_pairs={{0,8},{8,0},{16,24},{24,16},{32,40},{40,32},{48,56},{56,48},{64,72... | collective-permute-start | bytes 786440 | tf_op jit(solution)/shard_map/ppermute | solution.py:26
  40.7 13.6 %collective-permute-start.13 = (bf16[32,4096]{1,0:T(8,128)(2,1)S(1)}, bf16[32,4096]{1,0:T(8,128)(2,1)S(1)}, u32[]{:S(2)}, u32[]{:S(2)}) collective-permute-start(bf16[32,4096]{1,0:T(8,128)(2,1)S(1)} %collective-permute-done.6.refs_2_), channel_id=1, source_target_pairs={{0,8},{8,0},{16,24},{24,16},{32,40},{40,32},{48,56},{56,48},{64,72... | collective-permute-start | bytes 786440 | tf_op jit(solution)/shard_map/ppermute | solution.py:26
  46.2 8.2 %collective-permute-start.16 = (bf16[32,4096]{1,0:T(8,128)(2,1)S(1)}, bf16[32,4096]{1,0:T(8,128)(2,1)S(1)}, u32[]{:S(2)}, u32[]{:S(2)}) collective-permute-start(bf16[32,4096]{1,0:T(8,128)(2,1)S(1)} %constant_dynamic-update-slice_fusion.2.refs_5_), channel_id=1, source_target_pairs={{0,8},{8,0},{16,24},{24,16},{32,40},{40,32},{48,56},{56,48},{64,72... | collective-permute-start | bytes 786440 | tf_op jit(solution)/shard_map/ppermute | solution.py:26
  61.8 74.0 %collective-permute-start.18 = (bf16[1024,2048]{1,0:T(8,128)(2,1)}, bf16[1024,2048]{1,0:T(8,128)(2,1)}, u32[]{:S(2)}, u32[]{:S(2)}) collective-permute-start(bf16[1024,2048]{1,0:T(8,128)(2,1)} %shard_map.61), channel_id=1, source_target_pairs={{0,8},{8,0},{16,24},{24,16},{32,40},{40,32},{48,56},{56,48},{64,72... | collective-permute-start | bytes 12582920 | tf_op jit(solution)/shard_map/ppermute | solution.py:26
  62.8 15.8 %all-to-all-start.1 = ((bf16[8,128,192]{1,2,0:T(8,128)(2,1)}), bf16[8,128,192]{1,2,0:T(8,128)(2,1)S(1)}, u32[]{:S(2)}, u32[]{:S(2)}) async-start(bf16[8,128,192]{1,2,0:T(8,128)(2,1)} %copy.11), calls=%async_computation.1 | async-start | bytes 786432 | tf_op jit(solution)/shard_map/all_to_all | solution.py:288
  78.6 21.8 %all-to-all-start = ((f32[8,128,320]{1,2,0:T(8,128)}), f32[8,128,320]{1,2,0:T(8,128)S(1)}, u32[]{:S(2)}, u32[]{:S(2)}) async-start(f32[8,128,320]{1,2,0:T(8,128)} %copy.10), calls=%async_computation | async-start | bytes 2621440 | tf_op jit(solution)/shard_map/all_to_all | solution.py:281
  101.7 19.5 %all-to-all-start.2 = ((bf16[8,128,512]{2,1,0:T(8,128)(2,1)}), bf16[8,128,512]{2,1,0:T(8,128)(2,1)S(1)}, u32[]{:S(2)}, u32[]{:S(2)}) async-start(bf16[8,128,512]{2,1,0:T(8,128)(2,1)} %broadcast_in_dim.30), calls=%async_computation.2 | async-start | bytes 2097152 | tf_op jit(solution)/shard_map/all_to_all | solution.py:306
  128.7 7.1 %collective-permute-start.17 = (bf16[512,1024]{1,0:T(8,128)(2,1)S(1)}, bf16[512,1024]{1,0:T(8,128)(2,1)S(1)}, u32[]{:S(2)}, u32[]{:S(2)}) collective-permute-start(bf16[512,1024]{1,0:T(8,128)(2,1)S(1)} %get-tuple-element.38.own), channel_id=1, source_target_pairs={{0,8},{8,0},{16,24},{24,16},{32,40},{40,32},{48,56},{56,48},{64,72... | collective-permute-start | bytes 3145736 | tf_op jit(solution)/shard_map/ppermute | solution.py:26
  144.6 14.2 %collective-permute-start.29 = (f32[125,128]{1,0:T(8,128)S(1)}, f32[125,128]{1,0:T(8,128)S(1)}, u32[]{:S(2)}, u32[]{:S(2)}) collective-permute-start(f32[125,128]{1,0:T(8,128)S(1)} %select_add_fusion.1), channel_id=1, source_target_pairs={{0,224},{8,232},{16,240},{24,248},{32,0},{40,8},{48,16},{56,24},{6... | collective-permute-start | bytes 192008 | tf_op jit(solution)/shard_map/ppermute | solution.py:26
  152.5 9.0 %collective-permute-start.23 = (bf16[64,2048]{1,0:T(8,128)(2,1)S(1)}, bf16[64,2048]{1,0:T(8,128)(2,1)S(1)}, u32[]{:S(2)}, u32[]{:S(2)}) collective-permute-start(bf16[64,2048]{1,0:T(8,128)(2,1)S(1)} %pad_maximum_fusion), channel_id=1, source_target_pairs={{0,32},{8,40},{16,48},{24,56},{32,64},{40,72},{48,80},{56,88},{64,... | collective-permute-start | bytes 786440 | tf_op jit(solution)/shard_map/ppermute | solution.py:26
  158.8 7.0 %collective-permute-start.30 = (bf16[64,2048]{1,0:T(8,128)(2,1)S(1)}, bf16[64,2048]{1,0:T(8,128)(2,1)S(1)}, u32[]{:S(2)}, u32[]{:S(2)}) collective-permute-start(bf16[64,2048]{1,0:T(8,128)(2,1)S(1)} %pad_maximum_fusion.1), channel_id=1, source_target_pairs={{0,224},{8,232},{16,240},{24,248},{32,0},{40,8},{48,16},{56,24},{6... | collective-permute-start | bytes 786440 | tf_op jit(solution)/shard_map/ppermute | solution.py:26
  163.0 6.5 %collective-permute-start.31 = (f32[125,128]{1,0:T(8,128)S(1)}, f32[125,128]{1,0:T(8,128)S(1)}, u32[]{:S(2)}, u32[]{:S(2)}) collective-permute-start(f32[125,128]{1,0:T(8,128)S(1)} %collective-permute-done.29), channel_id=1, source_target_pairs={{0,224},{8,232},{16,240},{24,248},{32,0},{40,8},{48,16},{56,24},{6... | collective-permute-start | bytes 192008 | tf_op jit(solution)/shard_map/ppermute | solution.py:26
  169.6 7.2 %collective-permute-start.32 = (bf16[64,2048]{1,0:T(8,128)(2,1)S(1)}, bf16[64,2048]{1,0:T(8,128)(2,1)S(1)}, u32[]{:S(2)}, u32[]{:S(2)}) collective-permute-start(bf16[64,2048]{1,0:T(8,128)(2,1)S(1)} %get-tuple-element.52), channel_id=1, source_target_pairs={{0,224},{8,232},{16,240},{24,248},{32,0},{40,8},{48,16},{56,24},{6... | collective-permute-start | bytes 786440 | tf_op jit(solution)/shard_map/ppermute | solution.py:26
  176.8 7.1 %collective-permute-start.27 = (bf16[64,2048]{1,0:T(8,128)(2,1)S(1)}, bf16[64,2048]{1,0:T(8,128)(2,1)S(1)}, u32[]{:S(2)}, u32[]{:S(2)}) collective-permute-start(bf16[64,2048]{1,0:T(8,128)(2,1)S(1)} %get-tuple-element.47), channel_id=1, source_target_pairs={{0,32},{8,40},{16,48},{24,56},{32,64},{40,72},{48,80},{56,88},{64,... | collective-permute-start | bytes 786440 | tf_op jit(solution)/shard_map/ppermute | solution.py:26
  189.7 10.8 %collective-permute-start.39 = (f32[125,256]{1,0:T(8,128)S(1)}, f32[125,256]{1,0:T(8,128)S(1)}, u32[]{:S(2)}, u32[]{:S(2)}) collective-permute-start(f32[125,256]{1,0:T(8,128)S(1)} %maximum_select_fusion.2), channel_id=1, source_target_pairs={{0,8},{8,0},{16,24},{24,16},{32,40},{40,32},{48,56},{56,48},{64,72... | collective-permute-start | bytes 384008 | tf_op jit(solution)/shard_map/ppermute | solution.py:26
  (26 other events, 115.7 us)

commit v3 on v2

v3 whole, which is shorter than its diff:
```python
import math

import jax
import jax.numpy as jnp
from jax import lax
from jax.experimental import pallas as pl
from jax.experimental.pallas import tpu as pltpu
from jax.sharding import PartitionSpec as P

FEATURES = 32768
LOW = jnp.bfloat16
FULL = jnp.float32
HALF = jnp.float16
TOP = 13.0
DEPTH, PAIR, CORES = 8, 2, 2
FAR = DEPTH // 2
NT = (((1,), (1,)), ((), ()))
RING = (4, 3, -3, 2, -2, 1, -1, 0)


def tgt_move(array, dz, dy, dc):
    pairs = []
    for z in range(DEPTH):
        for y in range(PAIR):
            for c in range(CORES):
                source = (z * PAIR + y) * CORES + c
                target = ((z + dz) % DEPTH * PAIR + (y + dy) % PAIR) * CORES + (c + dc) % CORES
                pairs.append((source, target))
    return lax.ppermute(array, "tgt", pairs)


def place():
    index = lax.axis_index("tgt")
    return index // (PAIR * CORES), index // CORES % PAIR, index % CORES


def together(*values):
    return lax.optimization_barrier(values)


def dot(a, b, left, right):
    return lax.dot_general(a, b, (((left,), (right,)), ((), ())), preferred_element_type=FULL)


def call(kernel, out, grid, in_specs, out_specs, flops, bytes_accessed, scratch=(), prefetch=0, vmem=48):
    return pl.pallas_call(
        kernel,
        out_shape=out,
        grid_spec=pltpu.PrefetchScalarGridSpec(
            num_scalar_prefetch=prefetch, grid=grid, in_specs=in_specs, out_specs=out_specs, scratch_shapes=list(scratch)
        ),
        compiler_params=pltpu.CompilerParams(dimension_semantics=("arbitrary",), vmem_limit_bytes=vmem * 2**20),
        cost_estimate=pl.CostEstimate(flops=flops, bytes_accessed=bytes_accessed, transcendentals=0),
    )


def kernel_part(target_feats, pieces, scale, blks):
    targets, features = target_feats.shape
    rows = sum(p.shape[0] for p in pieces)
    count = len(pieces)
    tile = 256
    steps = targets // tile
    block = targets // blks
    per = tile // block

    def body(*refs):
        feats, parts = refs[0], refs[1 : 1 + count]
        out, held, peak, sem = refs[1 + count :]
        step = pl.program_id(0)

        @pl.when(step == 0)
        def _():
            copies, start = [], 0
            for i, part in enumerate(parts):
                copies.append(pltpu.make_async_copy(part, held.at[pl.ds(start, part.shape[0])], sem.at[i]))
                start += part.shape[0]
            for copy in copies:
                copy.start()
            for copy in copies:
                copy.wait()
            peak[...] = jnp.zeros_like(peak)

        product = lax.dot_general(feats[...], held[...], NT, preferred_element_type=FULL) * scale
        for i in range(per):
            out[step * per + i, :block] = product[i * block : (i + 1) * block]
        peak[...] = jnp.maximum(peak[...], jnp.max(jnp.abs(product).reshape(tile // 8, 8, rows), axis=0))

        @pl.when(step == steps - 1)
        def _():
            top = jnp.max(jnp.max(peak[...], axis=1, keepdims=True), axis=0, keepdims=True)
            power = jnp.floor(jnp.log2(jnp.maximum(top, 1e-30)))
            factor = jnp.exp2(TOP - power)
            for i in range(blks):
                out[i, :block] = out[i, :block] * factor
                out[i, block:] = jnp.broadcast_to(power, (16, rows))

    return call(
        body,
        jax.ShapeDtypeStruct((blks, block + 16, rows), FULL),
        (steps,),
        [pl.BlockSpec((tile, features), lambda i: (i, 0))] + [pl.BlockSpec(memory_space=pltpu.HBM)] * count,
        pl.BlockSpec((blks, block + 16, rows), lambda i: (0, 0, 0)),
        2 * targets * features * rows,
        2 * features * (targets + rows) + 4 * targets * rows,
        [pltpu.VMEM((rows, features), LOW), pltpu.VMEM((8, rows), FULL), pltpu.SemaphoreType.DMA((count,))],
    )(target_feats, *pieces)


def gradients(kernel_low, labels, coefs_here, coefs_ring, own_coefs, order, first_class, core):
    targets, supports = kernel_low.shape
    padded = coefs_here.shape[0]
    own = own_coefs.shape[0]
    half = supports // 2
    tile = 256
    steps = targets // tile

    def body(scalars, low, column, row, here, ring, mine, order_ref, grad, keep, give, part):
        step = pl.program_id(0)
        predict = lax.dot_general(low[...], here[...], NT, preferred_element_type=FULL)
        ids = lax.broadcasted_iota(jnp.int32, (tile, padded), 1)
        residual = jnp.where(ids == column[...], predict - 1.0, predict).astype(LOW)
        grad[...] = lax.dot_general(ring[...], residual, NT, preferred_element_type=FULL).astype(LOW)
        predict = lax.dot_general(mine[...], low[...], NT, preferred_element_type=FULL)
        ids = lax.broadcasted_iota(jnp.int32, (own, tile), 0) + scalars[0]
        residual = jnp.where(ids == row[...], predict - 1.0, predict).astype(LOW)
        ordered = jnp.dot(low[...], order_ref[...], preferred_element_type=FULL).astype(LOW)
        product = jnp.dot(residual, ordered, preferred_element_type=FULL)

        @pl.when(step == 0)
        def _():
            part[...] = product

        @pl.when(step > 0)
        def _():
            part[...] += product

        @pl.when(step == steps - 1)
        def _():
            left, right = part[:, :half], part[:, half:]
            first = scalars[1] == 0
            keep[...] = jnp.where(first, left, right)
            give[...] = jnp.where(first, right, left)

    whole = lambda i, f: (0, 0)
    piece = jax.ShapeDtypeStruct((own, half), FULL)
    return call(
        body,
        (jax.ShapeDtypeStruct((supports, targets), LOW), piece, piece),
        (steps,),
        [
            pl.BlockSpec((tile, supports), lambda i, f: (i, 0)),
            pl.BlockSpec((tile, 1), lambda i, f: (i, 0)),
            pl.BlockSpec((1, tile), lambda i, f: (0, i)),
            pl.BlockSpec((padded, supports), whole),
            pl.BlockSpec((supports, padded), whole),
            pl.BlockSpec((own, supports), whole),
            pl.BlockSpec((supports, supports), whole),
        ],
        (pl.BlockSpec((supports, tile), lambda i, f: (0, i)),) + (pl.BlockSpec((own, half), whole),) * 2,
        2 * targets * supports * (2 * padded + supports),
        2 * supports * (2 * targets + 3 * padded),
        [pltpu.VMEM((own, supports), FULL)],
        prefetch=1,
    )(jnp.stack([first_class, core]), kernel_low, labels[:, None], labels[None, :], coefs_here, coefs_ring, own_coefs, order)


def support_part(own_grad, other_grad, target_feats, taken, coef, other_coef, which, chip_rows):
    targets, features = target_feats.shape
    supports = own_grad.shape[0]
    half = features // 2
    edge = half // 2
    tile = 512
    steps = half // tile
    classes, columns = coef.shape
    rest = classes - chip_rows
    fold = 2 * columns

    def body(which_ref, own, other, feats, theirs, coef_ref, other_ref, up, down, folded, *outs):
        step = pl.program_id(0)
        product = jnp.dot(own[...], feats[...], preferred_element_type=FULL) + jnp.dot(
            other[...], theirs[...], preferred_element_type=FULL
        )
        for i, out in enumerate(outs):
            out[...] = product[(i + 1) * chip_rows : (i + 2) * chip_rows]
        far = product[:chip_rows].astype(LOW)

        @pl.when(step < steps // 2)
        def _():
            up[:, pl.ds(pl.multiple_of(step * tile, tile), tile)] = far

        @pl.when(step >= steps // 2)
        def _():
            down[:, pl.ds(pl.multiple_of((step - steps // 2) * tile, tile), tile)] = far

        @pl.when(step == 0)
        def _():
            total = coef_ref[...] + other_ref[...]
            lower = jnp.concatenate([total[chip_rows:], jnp.zeros((chip_rows - rest, columns), FULL)], 0)
            total = jnp.concatenate([total[:chip_rows], lower], 1)
            folded[...] = total
            up[:, edge:] = total.astype(LOW)
            down[:, edge:] = total.astype(LOW)

    whole = lambda i, w: (0, 0)
    first = jax.ShapeDtypeStruct((chip_rows, edge + fold), LOW)
    later = (jax.ShapeDtypeStruct((chip_rows, half), FULL),) * (len(RING) - 1)
    up, down, folded, *parts = call(
        body,
        (first, first, jax.ShapeDtypeStruct((chip_rows, fold), FULL)) + later,
        (steps,),
        [
            pl.BlockSpec(own_grad.shape, whole),
            pl.BlockSpec(other_grad.shape, whole),
            pl.BlockSpec((targets, tile), lambda i, w: (0, w[0] * steps + i)),
            pl.BlockSpec((targets, tile), lambda i, w: (0, i)),
            pl.BlockSpec(coef.shape, whole),
            pl.BlockSpec(coef.shape, whole),
        ],
        (pl.BlockSpec((chip_rows, edge + fold), whole),) * 2
        + (pl.BlockSpec((chip_rows, fold), whole),)
        + (pl.BlockSpec((chip_rows, tile), lambda i, w: (0, i)),) * (len(RING) - 1),
        4 * supports * targets * half,
        4 * targets * half + 4 * supports * half,
        prefetch=1,
    )(which, own_grad, other_grad, target_feats, taken, coef, other_coef)
    return up, down, folded, dict(zip(RING[1:], parts))


def order_matrix(shards, rows):
    ids = (jnp.stack(shards)[:, None] * rows + jnp.arange(rows)[None, :]).reshape(-1)
    return (ids[:, None] == jnp.arange(ids.shape[0])[None, :]).astype(LOW)


def split(array, which):
    half = array.shape[1] // 2
    left, right = array[:, :half], array[:, half:]
    return jnp.where(which == 0, left, right), jnp.where(which == 0, right, left)


def join(mine, other, which):
    return jnp.where(which == 0, jnp.concatenate([mine, other], 1), jnp.concatenate([other, mine], 1))


def sums(up, down, total, part, classes, rows):
    z, y, c = place()
    wide = part[0].shape[1]
    half = wide // 2
    columns = total.shape[1] // 2
    for step in range(FAR, 0, -1):
        up, down = tgt_move(up, 1, 0, 0), tgt_move(down, -1, 0, 0)
        edge = half if step == FAR else wide
        up, coef_up = up[:, :edge], up[:, edge:]
        total = total + coef_up.astype(FULL)
        if step > 1:
            down, coef_down = down[:, :edge], down[:, edge:]
            total = total + coef_down.astype(FULL)
            above, below = part[step - 1], part[1 - step]
            if step == FAR:
                up = jnp.concatenate([above[:, :half] + up.astype(FULL), above[:, half:]], 1)
                down = jnp.concatenate([below[:, :half], below[:, half:] + down.astype(FULL)], 1)
            else:
                up, down = above + up.astype(FULL), below + down.astype(FULL)
            up = jnp.concatenate([up.astype(LOW), coef_up], 1)
            down = down.astype(LOW)
            if step > 2:
                down = jnp.concatenate([down, coef_down], 1)
    mine = (part[0] + up.astype(FULL) + down.astype(FULL)).reshape(PAIR, CORES * rows, wide)
    near_rows = CORES * rows
    beside = jnp.concatenate([total[:near_rows], total[near_rows:]], 1)
    other = tgt_move(jnp.concatenate([mine[1], beside], 1).astype(LOW), 0, 1, 0)
    mine = (mine[0] + other[:, :wide].astype(FULL)).reshape(CORES, rows, wide)
    beside = beside + other[:, wide:].astype(FULL)
    span = beside.shape[1] // 2
    total = jnp.concatenate([beside[:, :span], beside[:, span:]], 0)
    coef = jnp.concatenate([total[:, i * columns : (i + 1) * columns] for i in range(2)], 0)[:classes]
    here, give = jnp.where(c == 0, mine[0], mine[1]), jnp.where(c == 0, mine[1], mine[0])
    return join(here, tgt_move(give, 0, 0, 1), c), join(coef, tgt_move(coef, 0, 0, 1), c)


def shards(target_feats, support_feats, coefs, labels):
    scale = 1.0 / math.sqrt(FEATURES)
    classes = coefs.shape[0]
    targets, features = target_feats.shape
    rows = support_feats.shape[0]
    blks = lax.axis_size("blk")
    tgts = lax.axis_size("tgt")
    blk_index = lax.axis_index("blk")
    z, y, c = place()

    half = features // 2
    padded = -(-classes // 128) * 128

    _, give = split(target_feats, c)
    taken = tgt_move(give, 0, 0, 1)
    near = tgt_move(support_feats, 0, 1, 0)
    pair = jnp.concatenate([support_feats + 0 * give[:1, :1], near], 0)
    pieces = [(pair, 0, 0), (tgt_move(pair, 0, 0, 1), 0, 1)]

    up = down = pair
    for step in range(1, FAR):
        up, down = tgt_move(up, 1, 0, 0), tgt_move(down, -1, 0, 0)
        pieces += [(up, -step, 0), (down, step, 0), (tgt_move(up, 0, 0, 1), -step, 1), (tgt_move(down, 0, 0, 1), step, 1)]
    seen = sum(p[:1, :1] for p, dz, dc in pieces if dc == 1 and abs(dz) == 1)
    left, right = up[:, :half] + 0 * (down[:1, :1] + seen), down[:, half:] + 0 * (up[:1, :1] + seen)
    up, down = tgt_move(left, 1, 0, 0), tgt_move(right, -1, 0, 0)
    last = jnp.concatenate([up, down], 1)
    pieces += [(last, FAR, 0), (tgt_move(last, 0, 0, 1), FAR, 1)]

    order = order_matrix(
        [((z + dz) % DEPTH * PAIR + (y + dy) % PAIR) * CORES + (c + dc) % CORES for _, dz, dc in pieces for dy in range(PAIR)], rows
    )
    ring_order = order_matrix(
        [((z + dz) % DEPTH * PAIR + (y + dy) % PAIR) * CORES + dc for dz in RING for dy in range(PAIR) for dc in range(CORES)], rows
    )
    class_rows = classes // blks
    first_class = blk_index * class_rows
    all_coefs = jnp.pad(coefs, ((0, padded - classes), (0, 0)))
    coefs_here = dot(all_coefs, order, 1, 1).astype(LOW)
    coefs_ring = dot(ring_order, all_coefs, 1, 1).astype(LOW)
    own_coefs = lax.dynamic_slice_in_dim(coefs_here, first_class, class_rows, 0)

    part = kernel_part(target_feats, [p for p, _, _ in pieces], scale, blks)

    got = lax.all_to_all(part.astype(HALF), "blk", 0, 0, tiled=True).astype(FULL)
    block = targets // blks
    own_low = jnp.sum(got[:, :block] * jnp.exp2(got[:, block : block + 1] - TOP), 0).astype(LOW)
    spread = jnp.broadcast_to(own_low[None], (blks,) + own_low.shape)
    kernel_low = lax.all_to_all(spread, "blk", 0, 0, tiled=True).reshape(targets, -1)

    kernel_grad, keep, give = gradients(kernel_low, labels, coefs_here, coefs_ring, own_coefs, order, first_class, c)
    other_grad, other_coef = tgt_move(kernel_grad, 0, 0, 1), tgt_move(give, 0, 0, 1)
    up, down, total, part = support_part(
        kernel_grad, other_grad, target_feats, taken, keep, other_coef, c[None], rows * PAIR * CORES
    )
    support_grad, coef_grad = sums(up, down, total, part, class_rows, rows)
    return support_grad * scale, coef_grad / math.sqrt(targets * tgts)


def solution(mesh):
    in_specs = (P("tgt", "blk"), P("tgt", "blk"), P(), P("tgt"))
    out_specs = (P("tgt", "blk"), P("blk", None))
    return jax.shard_map(shards, mesh=mesh, in_specs=in_specs, out_specs=out_specs, check_vma=False)
```

time: 203 us -> 174 us (0.86)
  Pallas kernels: 35.8 us -> 22.5 us
  starting transfers between devices: 70.2 us -> 58.1 us
  waiting for transfers between devices: 77.9 us -> 66.3 us
  other arithmetic: 2.54 us -> 11.3 us
  local copies, waits for them, and re-layouts: 10.4 us -> 7.29 us
  between operations: 1.28 us -> 4.33 us
    pallas_call x6 -> x3, Pallas kernels: 35.8 us -> 22.5 us  [the longest x1 9.29 us: kernel_part(): call(body, jax.ShapeDtypeStruct((blks, block + 16, rows), FULL), (steps,)...]
    all_to_all x2 -> x1, waiting for transfers between devices: 25.2 us -> 17.1 us  [shards(): lax.all_to_all(part.astype(HALF), 'blk', 0, 0, tiled=True).astype(FULL)]
    ppermute x40 -> x31, starting transfers between devices: 56 us -> 48.2 us  [tgt_move(): return lax.ppermute(array, 'tgt', pairs)]
    select_n x2 -> x1, other arithmetic: 0.03 us -> 5.06 us  [split(): jnp.where(which == 0, right, left)]
    ppermute x40 -> x31, waiting for transfers between devices: 42.7 us -> 37.9 us  [tgt_move(): return lax.ppermute(array, 'tgt', pairs)]
    all_to_all x2 -> x1, starting transfers between devices: 10.2 us -> 6.35 us  [shards(): lax.all_to_all(part.astype(HALF), 'blk', 0, 0, tiled=True).astype(FULL)]
    unnamed x16 -> x12, local copies, waits for them, and re-layouts: 6.02 us -> 2.25 us
    convert_element_type x3 -> x6, other arithmetic: 0.21 us -> 3.55 us  [the longest x1 2.98 us: shards(): part.astype(HALF)]
  transfers between devices with their start and end apart: 43 -> 33, of which waited for: 21 -> 14; matrix products, arithmetic and copies ran while one was open for 5% -> 11% of each run, Pallas kernels for 12% -> 9%
where the time goes in v3:
time: 174 us
  waiting for transfers between devices  66.3 us (38%)
  starting transfers between devices  58.1 us (33%)
  Pallas kernels  22.5 us (13%)
  other arithmetic  11.3 us (6%)
  local copies, waits for them, and re-layouts  7.29 us (4%)
  between operations  4.33 us (2%)
  matrix products  3.89 us (2%)
    ppermute x31, starting transfers between devices, tgt_move(): return lax.ppermute(array, 'tgt', pairs)  48.2 us
    ppermute x31, waiting for transfers between devices, tgt_move(): return lax.ppermute(array, 'tgt', pairs)  37.9 us
    all_to_all x1, waiting for transfers between devices, shards(): lax.all_to_all(part.astype(HALF), 'blk', 0, 0, tiled=True).astype(FULL)  17.1 us
    all_to_all x1, waiting for transfers between devices, shards(): lax.all_to_all(spread, 'blk', 0, 0, tiled=True).reshape(targets, -1)  11.3 us
    pallas_call x1, Pallas kernels, kernel_part(): call(body, jax.ShapeDtypeStruct((blks, block + 16, rows), FULL), (steps,)...  9.29 us
    pallas_call x1, Pallas kernels, support_part(): call(body, (first, first, jax.ShapeDtypeStruct((chip_rows, fold), FULL))...  7.6 us
    all_to_all x1, starting transfers between devices, shards(): lax.all_to_all(part.astype(HALF), 'blk', 0, 0, tiled=True).astype(FULL)  6.35 us
    pallas_call x1, Pallas kernels, gradients(): call(body, (jax.ShapeDtypeStruct((supports, targets), LOW), piece, piece)...  5.65 us
  transfers between devices with their start and end apart: 33, of which 14 were waited for; matrix products, arithmetic and copies ran while one was open for 11% of the time, Pallas kernels for 9%

profile of v3, /device:TPU:1, one launch (start us, length us, event | category | flops | bytes accessed | tf_op | source)
XLA Modules:
  0.0 173.7 jit_solution(13314235922796246549)
XLA Ops:
  2.8 5.1 %slice_select_fusion = bf16[1024,2048]{1,0:T(8,128)(2,1)} fusion(bf16[1024,4096]{1,0:T(8,128)(2,1)} %feats.1, pred[]{:T(512)S(6)} %eq.197), kind=kLoop, calls=%fused_computation | loop fusion | flops 2097152 | bytes 12582913 | tf_op jit(solution)/shard_map/jit(_where)/select_n | solution.py:237
  9.8 5.7 %collective-permute-start.3 = (bf16[32,4096]{1,0:T(8,128)(2,1)S(1)}, bf16[32,4096]{1,0:T(8,128)(2,1)S(1)}, u32[]{:S(2)}, u32[]{:S(2)}) collective-permute-start(bf16[32,4096]{1,0:T(8,128)(2,1)S(1)} %pad_maximum_fusion.5.refs_1_), channel_id=1, source_target_pairs={{0,224},{8,232},{16,240},{24,248},{32,0},{40,8},{48,16},{56,24},{6... | collective-permute-start | bytes 786440 | tf_op jit(solution)/shard_map/ppermute | solution.py:29
  15.5 4.7 %collective-permute-done.3.refs_4_ = bf16[32,4096]{1,0:T(8,128)(2,1)S(1)} collective-permute-done((bf16[32,4096]{1,0:T(8,128)(2,1)S(1)}, bf16[32,4096]{1,0:T(8,128)(2,1)S(1)}, u32[]{:S(2)}, u32[]{:S(2)}) %collective-permute-start.3) | collective-permute-done | bytes 262176 | tf_op jit(solution)/shard_map/ppermute | solution.py:29
  20.1 3.4 %collective-permute-start.7 = (bf16[32,4096]{1,0:T(8,128)(2,1)S(1)}, bf16[32,4096]{1,0:T(8,128)(2,1)S(1)}, u32[]{:S(2)}, u32[]{:S(2)}) collective-permute-start(bf16[32,4096]{1,0:T(8,128)(2,1)S(1)} %collective-permute-done.3.refs_4_), channel_id=1, source_target_pairs={{0,224},{8,232},{16,240},{24,248},{32,0},{40,8},{48,16},{56,24},{6... | collective-permute-start | bytes 786440 | tf_op jit(solution)/shard_map/ppermute | solution.py:29
  27.3 3.4 %collective-permute-start.11 = (bf16[32,4096]{1,0:T(8,128)(2,1)S(1)}, bf16[32,4096]{1,0:T(8,128)(2,1)S(1)}, u32[]{:S(2)}, u32[]{:S(2)}) collective-permute-start(bf16[32,4096]{1,0:T(8,128)(2,1)S(1)} %collective-permute-done.7.refs_8_), channel_id=1, source_target_pairs={{0,224},{8,232},{16,240},{24,248},{32,0},{40,8},{48,16},{56,24},{6... | collective-permute-start | bytes 786440 | tf_op jit(solution)/shard_map/ppermute | solution.py:29
  30.7 3.1 %collective-permute-start.1 = (bf16[32,4096]{1,0:T(8,128)(2,1)S(1)}, bf16[32,4096]{1,0:T(8,128)(2,1)S(1)}, u32[]{:S(2)}, u32[]{:S(2)}) collective-permute-start(bf16[32,4096]{1,0:T(8,128)(2,1)S(1)} %pad_maximum_fusion.5.refs_1_), channel_id=1, source_target_pairs={{0,8},{8,0},{16,24},{24,16},{32,40},{40,32},{48,56},{56,48},{64,72... | collective-permute-start | bytes 786440 | tf_op jit(solution)/shard_map/ppermute | solution.py:29
  39.1 3.0 %collective-permute-start.15 = (bf16[32,2048]{1,0:T(8,128)(2,1)S(1)}, bf16[32,2048]{1,0:T(8,128)(2,1)S(1)}, u32[]{:S(2)}, u32[]{:S(2)}) collective-permute-start(bf16[32,2048]{1,0:T(8,128)(2,1)S(1)} %slice_add_fusion.1), channel_id=1, source_target_pairs={{0,224},{8,232},{16,240},{24,248},{32,0},{40,8},{48,16},{56,24},{6... | collective-permute-start | bytes 393224 | tf_op jit(solution)/shard_map/ppermute | solution.py:29
  43.2 4.4 %collective-permute-start.12 = (bf16[32,4096]{1,0:T(8,128)(2,1)S(1)}, bf16[32,4096]{1,0:T(8,128)(2,1)S(1)}, u32[]{:S(2)}, u32[]{:S(2)}) collective-permute-start(bf16[32,4096]{1,0:T(8,128)(2,1)S(1)} %collective-permute-done.10.refs_11_), channel_id=1, source_target_pairs={{0,8},{8,0},{16,24},{24,16},{32,40},{40,32},{48,56},{56,48},{64,72... | collective-permute-start | bytes 786440 | tf_op jit(solution)/shard_map/ppermute | solution.py:29
  50.1 9.3 %shard_map.59 = f32[8,144,512]{2,1,0:T(8,128)} custom-call(bf16[1024,4096]{1,0:T(8,128)(2,1)} %feats.1, bf16[32,4096]{1,0:T(8,128)(2,1)S(1)} %pad_maximum_fusion.5.refs_1_, bf16[32,4096]{1,0:T(8,128)(2,1)S(1)} %collective-permute-done.1.refs_2_, bf16[32,4096]{1,0:T(8,128)(2,1)S(1)} %collective-permute-done.2.refs_3_, ...), custom_call_target="tpu_custom_call" | custom-call | flops 4294967296 | bytes 14680064 | tf_op jit(solution)/shard_map/pallas_call | solution.py:97
  59.4 3.0 %convert_element_type.91 = f16[8,144,512]{2,1,0:T(8,128)(2,1)} convert(f32[8,144,512]{2,1,0:T(8,128)} %shard_map.59) | non-fusion elementwise | flops 589824 | bytes 3538944 | tf_op jit(solution)/shard_map/convert_element_type | solution.py:324
  62.4 6.4 %all-to-all-start = ((f16[8,144,512]{2,1,0:T(8,128)(2,1)}), f16[8,144,512]{2,1,0:T(8,128)(2,1)S(1)}, u32[]{:S(2)}, u32[]{:S(2)}) async-start(f16[8,144,512]{2,1,0:T(8,128)(2,1)} %convert_element_type.91), calls=%async_computation | async-start | bytes 2359296 | tf_op jit(solution)/shard_map/all_to_all | solution.py:324
  69.6 17.1 %all-to-all-done = f16[8,144,512]{2,1,0:T(8,128)(2,1)S(1)} async-done(((f16[8,144,512]{2,1,0:T(8,128)(2,1)}), f16[8,144,512]{2,1,0:T(8,128)(2,1)S(1)}, u32[]{:S(2)}, u32[]{:S(2)}) %all-to-all-start) | async-done | bytes 1179680 | tf_op jit(solution)/shard_map/all_to_all | solution.py:324
  88.3 3.6 %all-to-all-start.1 = ((bf16[8,128,512]{2,1,0:T(8,128)(2,1)}), bf16[8,128,512]{2,1,0:T(8,128)(2,1)S(1)}, u32[]{:S(2)}, u32[]{:S(2)}) async-start(bf16[8,128,512]{2,1,0:T(8,128)(2,1)} %broadcast_in_dim.9), calls=%async_computation.1 | async-start | bytes 2097152 | tf_op jit(solution)/shard_map/all_to_all | solution.py:328
  96.1 11.3 %all-to-all-done.1 = bf16[8,128,512]{2,1,0:T(8,128)(2,1)S(1)} async-done(((bf16[8,128,512]{2,1,0:T(8,128)(2,1)}), bf16[8,128,512]{2,1,0:T(8,128)(2,1)S(1)}, u32[]{:S(2)}, u32[]{:S(2)}) %all-to-all-start.1) | async-done | bytes 1048608 | tf_op jit(solution)/shard_map/all_to_all | solution.py:328
  108.6 5.7 %shard_map.60 = (bf16[512,1024]{1,0:T(8,128)(2,1)S(1)}, f32[125,256]{1,0:T(8,128)S(1)}, f32[125,256]{1,0:T(8,128)S(1)}) custom-call(s32[2]{0:T(128)S(1)} %pad_add_fusion.scalars, bf16[1024,512]{1,0:T(8,128)(2,1)S(1)} %bitcast.75, s32[1024,1]{1,0:T(8,128)S(1)} %copy.6.column, s32[1,1024]{1,0:T(1,128)S(1)} %bitcast.77, ...), custom_call_target="tpu_custom_call" | custom-call | flops 2684354560 | bytes 5242880 | tf_op jit(solution)/shard_map/pallas_call | solution.py:146
  119.0 7.6 %shard_map.61 = (bf16[64,1536]{1,0:T(8,128)(2,1)S(1)}, bf16[64,1536]{1,0:T(8,128)(2,1)S(1)}, f32[64,512]{1,0:T(8,128)S(1)}, f32[64,2048]{1,0:T(8,128)S(1)}, f32[...) custom-call(s32[1]{0:T(128)} %bitcast.which_ref, ...), custom_call_target="tpu_custom_call" | custom-call | flops 4294967296 | bytes 12582912 | tf_op jit(solution)/shard_map/pallas_call | solution.py:207
  126.7 3.5 %collective-permute-start.24 = (bf16[64,1536]{1,0:T(8,128)(2,1)S(1)}, bf16[64,1536]{1,0:T(8,128)(2,1)S(1)}, u32[]{:S(2)}, u32[]{:S(2)}) collective-permute-start(bf16[64,1536]{1,0:T(8,128)(2,1)S(1)} %get-tuple-element.26), channel_id=1, source_target_pairs={{0,224},{8,232},{16,240},{24,248},{32,0},{40,8},{48,16},{56,24},{6... | collective-permute-start | bytes 589832 | tf_op jit(solution)/shard_map/ppermute | solution.py:29
  130.2 4.8 %collective-permute-done.20 = bf16[64,1536]{1,0:T(8,128)(2,1)S(1)} collective-permute-done((bf16[64,1536]{1,0:T(8,128)(2,1)S(1)}, bf16[64,1536]{1,0:T(8,128)(2,1)S(1)}, u32[]{:S(2)}, u32[]{:S(2)}) %collective-permute-start.20) | collective-permute-done | bytes 196640 | tf_op jit(solution)/shard_map/ppermute | solution.py:29
  138.0 6.7 %collective-permute-done.21 = bf16[64,2560]{1,0:T(8,128)(2,1)S(1)} collective-permute-done((bf16[64,2560]{1,0:T(8,128)(2,1)S(1)}, bf16[64,2560]{1,0:T(8,128)(2,1)S(1)}, u32[]{:S(2)}, u32[]{:S(2)}) %collective-permute-start.21) | collective-permute-done | bytes 327712 | tf_op jit(solution)/shard_map/ppermute | solution.py:29
  145.1 2.9 %collective-permute-start.26 = (bf16[64,2560]{1,0:T(8,128)(2,1)S(1)}, bf16[64,2560]{1,0:T(8,128)(2,1)S(1)}, u32[]{:S(2)}, u32[]{:S(2)}) collective-permute-start(bf16[64,2560]{1,0:T(8,128)(2,1)S(1)} %pad_maximum_fusion.4), channel_id=1, source_target_pairs={{0,224},{8,232},{16,240},{24,248},{32,0},{40,8},{48,16},{56,24},{6... | collective-permute-start | bytes 983048 | tf_op jit(solution)/shard_map/ppermute | solution.py:29
  148.0 5.5 %collective-permute-done.22 = bf16[64,2560]{1,0:T(8,128)(2,1)S(1)} collective-permute-done((bf16[64,2560]{1,0:T(8,128)(2,1)S(1)}, bf16[64,2560]{1,0:T(8,128)(2,1)S(1)}, u32[]{:S(2)}, u32[]{:S(2)}) %collective-permute-start.22) | collective-permute-done | bytes 327712 | tf_op jit(solution)/shard_map/ppermute | solution.py:29
  156.6 4.9 %collective-permute-done.23 = bf16[64,2560]{1,0:T(8,128)(2,1)S(1)} collective-permute-done((bf16[64,2560]{1,0:T(8,128)(2,1)S(1)}, bf16[64,2560]{1,0:T(8,128)(2,1)S(1)}, u32[]{:S(2)}, u32[]{:S(2)}) %collective-permute-start.23) | collective-permute-done | bytes 327712 | tf_op jit(solution)/shard_map/ppermute | solution.py:29
  161.8 4.5 %collective-permute-done.28 = bf16[32,3072]{1,0:T(8,128)(2,1)S(1)} collective-permute-done((bf16[32,3072]{1,0:T(8,128)(2,1)S(1)}, bf16[32,3072]{1,0:T(8,128)(2,1)S(1)}, u32[]{:S(2)}, u32[]{:S(2)}) %collective-permute-start.28) | collective-permute-done | bytes 196640 | tf_op jit(solution)/shard_map/ppermute | solution.py:29
  166.4 4.9 %collective-permute-start.30 = (f32[125,256]{1,0:T(8,128)S(1)}, f32[125,256]{1,0:T(8,128)S(1)}, u32[]{:S(2)}, u32[]{:S(2)}) collective-permute-start(f32[125,256]{1,0:T(8,128)S(1)} %pad_maximum_fusion.7), channel_id=1, source_target_pairs={{0,8},{8,0},{16,24},{24,16},{32,40},{40,32},{48,56},{56,48},{64,72... | collective-permute-start | bytes 384008 | tf_op jit(solution)/shard_map/ppermute | solution.py:29
  (119 shorter events, 35.1 us)
Async XLA Ops:
  0.6 9.1 %collective-permute-start = (bf16[16,4096]{1,0:T(8,128)(2,1)}, bf16[16,4096]{1,0:T(8,128)(2,1)S(1)}, u32[]{:S(2)}, u32[]{:S(2)}) collective-permute-start(bf16[16,4096]{1,0:T(8,128)(2,1)} %param.5), channel_id=1, source_target_pairs={{0,16},{8,24},{16,0},{24,8},{32,48},{40,56},{48,32},{56,40},{64,80... | collective-permute-start | bytes 393224 | tf_op jit(solution)/shard_map/ppermute | solution.py:29
  9.8 10.3 %collective-permute-start.3 = (bf16[32,4096]{1,0:T(8,128)(2,1)S(1)}, bf16[32,4096]{1,0:T(8,128)(2,1)S(1)}, u32[]{:S(2)}, u32[]{:S(2)}) collective-permute-start(bf16[32,4096]{1,0:T(8,128)(2,1)S(1)} %pad_maximum_fusion.5.refs_1_), channel_id=1, source_target_pairs={{0,224},{8,232},{16,240},{24,248},{32,0},{40,8},{48,16},{56,24},{6... | collective-permute-start | bytes 786440 | tf_op jit(solution)/shard_map/ppermute | solution.py:29
  15.5 8.1 %collective-permute-start.2 = (bf16[32,4096]{1,0:T(8,128)(2,1)S(1)}, bf16[32,4096]{1,0:T(8,128)(2,1)S(1)}, u32[]{:S(2)}, u32[]{:S(2)}) collective-permute-start(bf16[32,4096]{1,0:T(8,128)(2,1)S(1)} %pad_maximum_fusion.5.refs_1_), channel_id=1, source_target_pairs={{0,32},{8,40},{16,48},{24,56},{32,64},{40,72},{48,80},{56,88},{64,... | collective-permute-start | bytes 786440 | tf_op jit(solution)/shard_map/ppermute | solution.py:29
  20.1 7.1 %collective-permute-start.7 = (bf16[32,4096]{1,0:T(8,128)(2,1)S(1)}, bf16[32,4096]{1,0:T(8,128)(2,1)S(1)}, u32[]{:S(2)}, u32[]{:S(2)}) collective-permute-start(bf16[32,4096]{1,0:T(8,128)(2,1)S(1)} %collective-permute-done.3.refs_4_), channel_id=1, source_target_pairs={{0,224},{8,232},{16,240},{24,248},{32,0},{40,8},{48,16},{56,24},{6... | collective-permute-start | bytes 786440 | tf_op jit(solution)/shard_map/ppermute | solution.py:29
  23.5 7.1 %collective-permute-start.6 = (bf16[32,4096]{1,0:T(8,128)(2,1)S(1)}, bf16[32,4096]{1,0:T(8,128)(2,1)S(1)}, u32[]{:S(2)}, u32[]{:S(2)}) collective-permute-start(bf16[32,4096]{1,0:T(8,128)(2,1)S(1)} %collective-permute-done.2.refs_3_), channel_id=1, source_target_pairs={{0,32},{8,40},{16,48},{24,56},{32,64},{40,72},{48,80},{56,88},{64,... | collective-permute-start | bytes 786440 | tf_op jit(solution)/shard_map/ppermute | solution.py:29
  23.5 10.2 %collective-permute-start.4 = (bf16[32,4096]{1,0:T(8,128)(2,1)S(1)}, bf16[32,4096]{1,0:T(8,128)(2,1)S(1)}, u32[]{:S(2)}, u32[]{:S(2)}) collective-permute-start(bf16[32,4096]{1,0:T(8,128)(2,1)S(1)} %collective-permute-done.2.refs_3_), channel_id=1, source_target_pairs={{0,8},{8,0},{16,24},{24,16},{32,40},{40,32},{48,56},{56,48},{64,72... | collective-permute-start | bytes 786440 | tf_op jit(solution)/shard_map/ppermute | solution.py:29
  25.7 8.6 %collective-permute-start.5 = (bf16[32,4096]{1,0:T(8,128)(2,1)S(1)}, bf16[32,4096]{1,0:T(8,128)(2,1)S(1)}, u32[]{:S(2)}, u32[]{:S(2)}) collective-permute-start(bf16[32,4096]{1,0:T(8,128)(2,1)S(1)} %collective-permute-done.3.refs_4_), channel_id=1, source_target_pairs={{0,8},{8,0},{16,24},{24,16},{32,40},{40,32},{48,56},{56,48},{64,72... | collective-permute-start | bytes 786440 | tf_op jit(solution)/shard_map/ppermute | solution.py:29
  27.3 9.3 %collective-permute-start.11 = (bf16[32,4096]{1,0:T(8,128)(2,1)S(1)}, bf16[32,4096]{1,0:T(8,128)(2,1)S(1)}, u32[]{:S(2)}, u32[]{:S(2)}) collective-permute-start(bf16[32,4096]{1,0:T(8,128)(2,1)S(1)} %collective-permute-done.7.refs_8_), channel_id=1, source_target_pairs={{0,224},{8,232},{16,240},{24,248},{32,0},{40,8},{48,16},{56,24},{6... | collective-permute-start | bytes 786440 | tf_op jit(solution)/shard_map/ppermute | solution.py:29
  30.7 7.1 %collective-permute-start.10 = (bf16[32,4096]{1,0:T(8,128)(2,1)S(1)}, bf16[32,4096]{1,0:T(8,128)(2,1)S(1)}, u32[]{:S(2)}, u32[]{:S(2)}) collective-permute-start(bf16[32,4096]{1,0:T(8,128)(2,1)S(1)} %collective-permute-done.6.refs_7_), channel_id=1, source_target_pairs={{0,32},{8,40},{16,48},{24,56},{32,64},{40,72},{48,80},{56,88},{64,... | collective-permute-start | bytes 786440 | tf_op jit(solution)/shard_map/ppermute | solution.py:29
  30.7 17.8 %collective-permute-start.1 = (bf16[32,4096]{1,0:T(8,128)(2,1)S(1)}, bf16[32,4096]{1,0:T(8,128)(2,1)S(1)}, u32[]{:S(2)}, u32[]{:S(2)}) collective-permute-start(bf16[32,4096]{1,0:T(8,128)(2,1)S(1)} %pad_maximum_fusion.5.refs_1_), channel_id=1, source_target_pairs={{0,8},{8,0},{16,24},{24,16},{32,40},{40,32},{48,56},{56,48},{64,72... | collective-permute-start | bytes 786440 | tf_op jit(solution)/shard_map/ppermute | solution.py:29
  36.0 12.6 %collective-permute-start.8 = (bf16[32,4096]{1,0:T(8,128)(2,1)S(1)}, bf16[32,4096]{1,0:T(8,128)(2,1)S(1)}, u32[]{:S(2)}, u32[]{:S(2)}) collective-permute-start(bf16[32,4096]{1,0:T(8,128)(2,1)S(1)} %collective-permute-done.6.refs_7_), channel_id=1, source_target_pairs={{0,8},{8,0},{16,24},{24,16},{32,40},{40,32},{48,56},{56,48},{64,72... | collective-permute-start | bytes 786440 | tf_op jit(solution)/shard_map/ppermute | solution.py:29
  36.1 13.0 %collective-permute-start.9 = (bf16[32,4096]{1,0:T(8,128)(2,1)S(1)}, bf16[32,4096]{1,0:T(8,128)(2,1)S(1)}, u32[]{:S(2)}, u32[]{:S(2)}) collective-permute-start(bf16[32,4096]{1,0:T(8,128)(2,1)S(1)} %collective-permute-done.7.refs_8_), channel_id=1, source_target_pairs={{0,8},{8,0},{16,24},{24,16},{32,40},{40,32},{48,56},{56,48},{64,72... | collective-permute-start | bytes 786440 | tf_op jit(solution)/shard_map/ppermute | solution.py:29
  39.1 8.6 %collective-permute-start.15 = (bf16[32,2048]{1,0:T(8,128)(2,1)S(1)}, bf16[32,2048]{1,0:T(8,128)(2,1)S(1)}, u32[]{:S(2)}, u32[]{:S(2)}) collective-permute-start(bf16[32,2048]{1,0:T(8,128)(2,1)S(1)} %slice_add_fusion.1), channel_id=1, source_target_pairs={{0,224},{8,232},{16,240},{24,248},{32,0},{40,8},{48,16},{56,24},{6... | collective-permute-start | bytes 393224 | tf_op jit(solution)/shard_map/ppermute | solution.py:29
  48.6 69.4 %collective-permute-start.18 = (bf16[1024,2048]{1,0:T(8,128)(2,1)}, bf16[1024,2048]{1,0:T(8,128)(2,1)}, u32[]{:S(2)}, u32[]{:S(2)}) collective-permute-start(bf16[1024,2048]{1,0:T(8,128)(2,1)} %slice_select_fusion), channel_id=1, source_target_pairs={{0,8},{8,0},{16,24},{24,16},{32,40},{40,32},{48,56},{56,48},{64,72... | collective-permute-start | bytes 12582920 | tf_op jit(solution)/shard_map/ppermute | solution.py:29
  62.4 24.2 %all-to-all-start = ((f16[8,144,512]{2,1,0:T(8,128)(2,1)}), f16[8,144,512]{2,1,0:T(8,128)(2,1)S(1)}, u32[]{:S(2)}, u32[]{:S(2)}) async-start(f16[8,144,512]{2,1,0:T(8,128)(2,1)} %convert_element_type.91), calls=%async_computation | async-start | bytes 2359296 | tf_op jit(solution)/shard_map/all_to_all | solution.py:324
  88.3 19.1 %all-to-all-start.1 = ((bf16[8,128,512]{2,1,0:T(8,128)(2,1)}), bf16[8,128,512]{2,1,0:T(8,128)(2,1)S(1)}, u32[]{:S(2)}, u32[]{:S(2)}) async-start(bf16[8,128,512]{2,1,0:T(8,128)(2,1)} %broadcast_in_dim.9), calls=%async_computation.1 | async-start | bytes 2097152 | tf_op jit(solution)/shard_map/all_to_all | solution.py:328
  126.6 8.4 %collective-permute-start.20 = (bf16[64,1536]{1,0:T(8,128)(2,1)S(1)}, bf16[64,1536]{1,0:T(8,128)(2,1)S(1)}, u32[]{:S(2)}, u32[]{:S(2)}) collective-permute-start(bf16[64,1536]{1,0:T(8,128)(2,1)S(1)} %get-tuple-element.22), channel_id=1, source_target_pairs={{0,32},{8,40},{16,48},{24,56},{32,64},{40,72},{48,80},{56,88},{64,... | collective-permute-start | bytes 589832 | tf_op jit(solution)/shard_map/ppermute | solution.py:29
  126.7 8.5 %collective-permute-start.24 = (bf16[64,1536]{1,0:T(8,128)(2,1)S(1)}, bf16[64,1536]{1,0:T(8,128)(2,1)S(1)}, u32[]{:S(2)}, u32[]{:S(2)}) collective-permute-start(bf16[64,1536]{1,0:T(8,128)(2,1)S(1)} %get-tuple-element.26), channel_id=1, source_target_pairs={{0,224},{8,232},{16,240},{24,248},{32,0},{40,8},{48,16},{56,24},{6... | collective-permute-start | bytes 589832 | tf_op jit(solution)/shard_map/ppermute | solution.py:29
  135.1 9.6 %collective-permute-start.21 = (bf16[64,2560]{1,0:T(8,128)(2,1)S(1)}, bf16[64,2560]{1,0:T(8,128)(2,1)S(1)}, u32[]{:S(2)}, u32[]{:S(2)}) collective-permute-start(bf16[64,2560]{1,0:T(8,128)(2,1)S(1)} %pad_maximum_fusion), channel_id=1, source_target_pairs={{0,32},{8,40},{16,48},{24,56},{32,64},{40,72},{48,80},{56,88},{64,... | collective-permute-start | bytes 983048 | tf_op jit(solution)/shard_map/ppermute | solution.py:29
  135.3 9.6 %collective-permute-start.25 = (bf16[64,2560]{1,0:T(8,128)(2,1)S(1)}, bf16[64,2560]{1,0:T(8,128)(2,1)S(1)}, u32[]{:S(2)}, u32[]{:S(2)}) collective-permute-start(bf16[64,2560]{1,0:T(8,128)(2,1)S(1)} %pad_maximum_fusion.3), channel_id=1, source_target_pairs={{0,224},{8,232},{16,240},{24,248},{32,0},{40,8},{48,16},{56,24},{6... | collective-permute-start | bytes 983048 | tf_op jit(solution)/shard_map/ppermute | solution.py:29
  144.9 8.7 %collective-permute-start.22 = (bf16[64,2560]{1,0:T(8,128)(2,1)S(1)}, bf16[64,2560]{1,0:T(8,128)(2,1)S(1)}, u32[]{:S(2)}, u32[]{:S(2)}) collective-permute-start(bf16[64,2560]{1,0:T(8,128)(2,1)S(1)} %pad_maximum_fusion.1), channel_id=1, source_target_pairs={{0,32},{8,40},{16,48},{24,56},{32,64},{40,72},{48,80},{56,88},{64,... | collective-permute-start | bytes 983048 | tf_op jit(solution)/shard_map/ppermute | solution.py:29
  145.1 8.7 %collective-permute-start.26 = (bf16[64,2560]{1,0:T(8,128)(2,1)S(1)}, bf16[64,2560]{1,0:T(8,128)(2,1)S(1)}, u32[]{:S(2)}, u32[]{:S(2)}) collective-permute-start(bf16[64,2560]{1,0:T(8,128)(2,1)S(1)} %pad_maximum_fusion.4), channel_id=1, source_target_pairs={{0,224},{8,232},{16,240},{24,248},{32,0},{40,8},{48,16},{56,24},{6... | collective-permute-start | bytes 983048 | tf_op jit(solution)/shard_map/ppermute | solution.py:29
  153.7 7.8 %collective-permute-start.23 = (bf16[64,2560]{1,0:T(8,128)(2,1)S(1)}, bf16[64,2560]{1,0:T(8,128)(2,1)S(1)}, u32[]{:S(2)}, u32[]{:S(2)}) collective-permute-start(bf16[64,2560]{1,0:T(8,128)(2,1)S(1)} %pad_maximum_fusion.2), channel_id=1, source_target_pairs={{0,32},{8,40},{16,48},{24,56},{32,64},{40,72},{48,80},{56,88},{64,... | collective-permute-start | bytes 983048 | tf_op jit(solution)/shard_map/ppermute | solution.py:29
  153.9 7.7 %collective-permute-start.27 = (bf16[64,2048]{1,0:T(8,128)(2,1)S(1)}, bf16[64,2048]{1,0:T(8,128)(2,1)S(1)}, u32[]{:S(2)}, u32[]{:S(2)}) collective-permute-start(bf16[64,2048]{1,0:T(8,128)(2,1)S(1)} %add_convert_fusion), channel_id=1, source_target_pairs={{0,224},{8,232},{16,240},{24,248},{32,0},{40,8},{48,16},{56,24},{6... | collective-permute-start | bytes 786440 | tf_op jit(solution)/shard_map/ppermute | solution.py:29
  (14 other events, 54.3 us)

commit v4 on v3

--- a/solution.py
+++ b/solution.py
@@ -12,6 +12,7 @@
 FULL = jnp.float32
 HALF = jnp.float16
 TOP = 13.0
+SUPPORT_TILE = 512
 DEPTH, PAIR, CORES = 8, 2, 2
 FAR = DEPTH // 2
 NT = (((1,), (1,)), ((), ()))
@@ -59,16 +60,14 @@
     rows = sum(p.shape[0] for p in pieces)
     count = len(pieces)
     tile = 256
-    steps = targets // tile
     block = targets // blks
     per = tile // block
 
     def body(*refs):
         feats, parts = refs[0], refs[1 : 1 + count]
-        out, held, peak, sem = refs[1 + count :]
-        step = pl.program_id(0)
-
-        @pl.when(step == 0)
+        out, held, sem = refs[1 + count :]
+
+        @pl.when(pl.program_id(0) == 0)
         def _():
             copies, start = [], 0
             for i, part in enumerate(parts):
@@ -78,31 +77,25 @@
                 copy.start()
             for copy in copies:
                 copy.wait()
-            peak[...] = jnp.zeros_like(peak)
 
         product = lax.dot_general(feats[...], held[...], NT, preferred_element_type=FULL) * scale
+        top = jnp.max(jnp.abs(product).reshape(tile // 8, 8, rows), axis=0)
+        top = jnp.max(jnp.max(top, axis=1, keepdims=True), axis=0, keepdims=True)
+        power = jnp.floor(jnp.log2(jnp.maximum(top, 1e-30)))
+        product = product * jnp.exp2(TOP - power)
         for i in range(per):
-            out[step * per + i, :block] = product[i * block : (i + 1) * block]
-        peak[...] = jnp.maximum(peak[...], jnp.max(jnp.abs(product).reshape(tile // 8, 8, rows), axis=0))
-
-        @pl.when(step == steps - 1)
-        def _():
-            top = jnp.max(jnp.max(peak[...], axis=1, keepdims=True), axis=0, keepdims=True)
-            power = jnp.floor(jnp.log2(jnp.maximum(top, 1e-30)))
-            factor = jnp.exp2(TOP - power)
-            for i in range(blks):
-                out[i, :block] = out[i, :block] * factor
-                out[i, block:] = jnp.broadcast_to(power, (16, rows))
+            out[i, :block] = product[i * block : (i + 1) * block]
+            out[i, block:] = jnp.broadcast_to(power, (16, rows))
 
     return call(
         body,
         jax.ShapeDtypeStruct((blks, block + 16, rows), FULL),
-        (steps,),
+        (targets // tile,),
         [pl.BlockSpec((tile, features), lambda i: (i, 0))] + [pl.BlockSpec(memory_space=pltpu.HBM)] * count,
-        pl.BlockSpec((blks, block + 16, rows), lambda i: (0, 0, 0)),
+        pl.BlockSpec((per, block + 16, rows), lambda i: (i, 0, 0)),
         2 * targets * features * rows,
         2 * features * (targets + rows) + 4 * targets * rows,
-        [pltpu.VMEM((rows, features), LOW), pltpu.VMEM((8, rows), FULL), pltpu.SemaphoreType.DMA((count,))],
+        [pltpu.VMEM((rows, features), LOW), pltpu.SemaphoreType.DMA((count,))],
     )(target_feats, *pieces)
 
 
@@ -164,33 +157,59 @@
     )(jnp.stack([first_class, core]), kernel_low, labels[:, None], labels[None, :], coefs_here, coefs_ring, own_coefs, order)
 
 
-def support_part(own_grad, other_grad, target_feats, taken, coef, other_coef, which, chip_rows):
+def support_call(body, outs, out_specs, factors, start, count, extra, extra_specs, chip_rows):
+    own_grad, other_grad, target_feats, taken, which = factors
     targets, features = target_feats.shape
-    supports = own_grad.shape[0]
     half = features // 2
+    steps = half // SUPPORT_TILE
+    rows = slice(start * chip_rows, (start + count) * chip_rows)
+
+    def kernel(which_ref, own, other, feats, theirs, *refs):
+        body(
+            jnp.dot(own[rows, :], feats[...], preferred_element_type=FULL)
+            + jnp.dot(other[rows, :], theirs[...], preferred_element_type=FULL),
+            *refs,
+        )
+
+    return call(
+        kernel,
+        outs,
+        (steps,),
+        [
+            pl.BlockSpec(own_grad.shape, lambda i, w: (0, 0)),
+            pl.BlockSpec(other_grad.shape, lambda i, w: (0, 0)),
+            pl.BlockSpec((targets, SUPPORT_TILE), lambda i, w: (0, w[0] * steps + i)),
+            pl.BlockSpec((targets, SUPPORT_TILE), lambda i, w: (0, i)),
+        ]
+        + extra_specs,
+        out_specs,
+        4 * count * chip_rows * targets * half,
+        4 * targets * half + 4 * count * chip_rows * half,
+        prefetch=1,
+    )(which, own_grad, other_grad, target_feats, taken, *extra)
+
+
+def support_first(factors, coef, other_coef, chip_rows):
+    half = factors[3].shape[1]
     edge = half // 2
-    tile = 512
-    steps = half // tile
+    steps = half // SUPPORT_TILE
     classes, columns = coef.shape
     rest = classes - chip_rows
     fold = 2 * columns
 
-    def body(which_ref, own, other, feats, theirs, coef_ref, other_ref, up, down, folded, *outs):
+    def body(product, coef_ref, other_ref, up, down, folded, above, below):
         step = pl.program_id(0)
-        product = jnp.dot(own[...], feats[...], preferred_element_type=FULL) + jnp.dot(
-            other[...], theirs[...], preferred_element_type=FULL
-        )
-        for i, out in enumerate(outs):
-            out[...] = product[(i + 1) * chip_rows : (i + 2) * chip_rows]
+        above[...] = product[chip_rows : 2 * chip_rows]
+        below[...] = product[2 * chip_rows :]
         far = product[:chip_rows].astype(LOW)
 
         @pl.when(step < steps // 2)
         def _():
-            up[:, pl.ds(pl.multiple_of(step * tile, tile), tile)] = far
+            up[:, pl.ds(pl.multiple_of(step * SUPPORT_TILE, SUPPORT_TILE), SUPPORT_TILE)] = far
 
         @pl.when(step >= steps // 2)
         def _():
-            down[:, pl.ds(pl.multiple_of((step - steps // 2) * tile, tile), tile)] = far
+            down[:, pl.ds(pl.multiple_of((step - steps // 2) * SUPPORT_TILE, SUPPORT_TILE), SUPPORT_TILE)] = far
 
         @pl.when(step == 0)
         def _():
@@ -203,27 +222,40 @@
 
     whole = lambda i, w: (0, 0)
     first = jax.ShapeDtypeStruct((chip_rows, edge + fold), LOW)
-    later = (jax.ShapeDtypeStruct((chip_rows, half), FULL),) * (len(RING) - 1)
-    up, down, folded, *parts = call(
+    return support_call(
         body,
-        (first, first, jax.ShapeDtypeStruct((chip_rows, fold), FULL)) + later,
-        (steps,),
-        [
-            pl.BlockSpec(own_grad.shape, whole),
-            pl.BlockSpec(other_grad.shape, whole),
-            pl.BlockSpec((targets, tile), lambda i, w: (0, w[0] * steps + i)),
-            pl.BlockSpec((targets, tile), lambda i, w: (0, i)),
-            pl.BlockSpec(coef.shape, whole),
-            pl.BlockSpec(coef.shape, whole),
-        ],
+        (first, first, jax.ShapeDtypeStruct((chip_rows, fold), FULL)) + (jax.ShapeDtypeStruct((chip_rows, half), FULL),) * 2,
         (pl.BlockSpec((chip_rows, edge + fold), whole),) * 2
         + (pl.BlockSpec((chip_rows, fold), whole),)
-        + (pl.BlockSpec((chip_rows, tile), lambda i, w: (0, i)),) * (len(RING) - 1),
-        4 * supports * targets * half,
-        4 * targets * half + 4 * supports * half,
-        prefetch=1,
-    )(which, own_grad, other_grad, target_feats, taken, coef, other_coef)
-    return up, down, folded, dict(zip(RING[1:], parts))
+        + (pl.BlockSpec((chip_rows, SUPPORT_TILE), lambda i, w: (0, i)),) * 2,
+        factors,
+        0,
+        3,
+        [coef, other_coef],
+        [pl.BlockSpec(coef.shape, whole)] * 2,
+        chip_rows,
+    )
+
+
+def support_rest(factors, chip_rows, earlier):
+    half = factors[3].shape[1]
+    count = len(RING) - 3
+
+    def body(product, *refs):
+        for i, out in enumerate(refs[len(earlier) :]):
+            out[...] = product[i * chip_rows : (i + 1) * chip_rows]
+
+    return support_call(
+        body,
+        (jax.ShapeDtypeStruct((chip_rows, half), FULL),) * count,
+        (pl.BlockSpec((chip_rows, SUPPORT_TILE), lambda i, w: (0, i)),) * count,
+        factors,
+        3,
+        count,
+        list(earlier),
+        [pl.BlockSpec(memory_space=pl.ANY)] * len(earlier),
+        chip_rows,
+    )
 
 
 def order_matrix(shards, rows):
@@ -241,12 +273,18 @@
     return jnp.where(which == 0, jnp.concatenate([mine, other], 1), jnp.concatenate([other, mine], 1))
 
 
-def sums(up, down, total, part, classes, rows):
+def sums(factors, coef, other_coef, rows):
     z, y, c = place()
-    wide = part[0].shape[1]
+    chip_rows = rows * PAIR * CORES
+    classes = coef.shape[0]
+    up, down, total, above, below = support_first(factors, coef, other_coef, chip_rows)
+    part = {FAR - 1: above, 1 - FAR: below}
+    wide = above.shape[1]
     half = wide // 2
     columns = total.shape[1] // 2
     for step in range(FAR, 0, -1):
+        if step == FAR - 1:
+            part.update(zip(RING[3:], support_rest(factors, chip_rows, (up, down))))
         up, down = tgt_move(up, 1, 0, 0), tgt_move(down, -1, 0, 0)
         edge = half if step == FAR else wide
         up, coef_up = up[:, :edge], up[:, edge:]
@@ -293,18 +331,31 @@
     _, give = split(target_feats, c)
     taken = tgt_move(give, 0, 0, 1)
     near = tgt_move(support_feats, 0, 1, 0)
-    pair = jnp.concatenate([support_feats + 0 * give[:1, :1], near], 0)
+    mine = jnp.concatenate([support_feats[:, :half] + 0 * give[:rows], support_feats[:, half:]], 1)
+    pair = jnp.concatenate([mine, near], 0)
     pieces = [(pair, 0, 0), (tgt_move(pair, 0, 0, 1), 0, 1)]
 
     up = down = pair
+    later = []
     for step in range(1, FAR):
         up, down = tgt_move(up, 1, 0, 0), tgt_move(down, -1, 0, 0)
-        pieces += [(up, -step, 0), (down, step, 0), (tgt_move(up, 0, 0, 1), -step, 1), (tgt_move(down, 0, 0, 1), step, 1)]
-    seen = sum(p[:1, :1] for p, dz, dc in pieces if dc == 1 and abs(dz) == 1)
-    left, right = up[:, :half] + 0 * (down[:1, :1] + seen), down[:, half:] + 0 * (up[:1, :1] + seen)
+        here = [(up, -step, 0), (down, step, 0)]
+        there = [(tgt_move(up, 0, 0, 1), -step, 1), (tgt_move(down, 0, 0, 1), step, 1)]
+        if step < FAR - 2:
+            pieces += here + there
+        elif step == FAR - 2:
+            pieces += here
+            near_part = kernel_part(target_feats, [p for p, _, _ in pieces], scale, blks)
+            later += there
+        else:
+            later += here + there
+    seen = jnp.tile(near_part[0, : up.shape[0]].astype(LOW), (1, half // near_part.shape[2]))
+    left, right = up[:, :half] + 0 * (down[:, half:] + seen), down[:, half:] + 0 * (up[:, :half] + seen)
     up, down = tgt_move(left, 1, 0, 0), tgt_move(right, -1, 0, 0)
     last = jnp.concatenate([up, down], 1)
-    pieces += [(last, FAR, 0), (tgt_move(last, 0, 0, 1), FAR, 1)]
+    later += [(last, FAR, 0), (tgt_move(last, 0, 0, 1), FAR, 1)]
+    far_part = kernel_part(target_feats, [p for p, _, _ in later], scale, blks)
+    pieces += later
 
     order = order_matrix(
         [((z + dz) % DEPTH * PAIR + (y + dy) % PAIR) * CORES + (c + dc) % CORES for _, dz, dc in pieces for dy in range(PAIR)], rows
@@ -319,20 +370,21 @@
     coefs_ring = dot(ring_order, all_coefs, 1, 1).astype(LOW)
     own_coefs = lax.dynamic_slice_in_dim(coefs_here, first_class, class_rows, 0)
 
-    part = kernel_part(target_feats, [p for p, _, _ in pieces], scale, blks)
-
-    got = lax.all_to_all(part.astype(HALF), "blk", 0, 0, tiled=True).astype(FULL)
+    part = jnp.concatenate([near_part.astype(HALF), far_part.astype(HALF)], 1)
+    got = lax.all_to_all(part, "blk", 0, 0, tiled=True).astype(FULL)
     block = targets // blks
-    own_low = jnp.sum(got[:, :block] * jnp.exp2(got[:, block : block + 1] - TOP), 0).astype(LOW)
+    own_low = []
+    for i in range(2):
+        rest = got[:, i * (block + 16) :]
+        own_low.append(jnp.sum(rest[:, :block] * jnp.exp2(rest[:, block : block + 1] - TOP), 0).astype(LOW))
+    own_low = jnp.concatenate(own_low, 1)
     spread = jnp.broadcast_to(own_low[None], (blks,) + own_low.shape)
     kernel_low = lax.all_to_all(spread, "blk", 0, 0, tiled=True).reshape(targets, -1)
 
     kernel_grad, keep, give = gradients(kernel_low, labels, coefs_here, coefs_ring, own_coefs, order, first_class, c)
     other_grad, other_coef = tgt_move(kernel_grad, 0, 0, 1), tgt_move(give, 0, 0, 1)
-    up, down, total, part = support_part(
-        kernel_grad, other_grad, target_feats, taken, keep, other_coef, c[None], rows * PAIR * CORES
-    )
-    support_grad, coef_grad = sums(up, down, total, part, class_rows, rows)
+    factors = (kernel_grad, other_grad, target_feats, taken, c[None])
+    support_grad, coef_grad = sums(factors, keep, other_coef, rows)
     return support_grad * scale, coef_grad / math.sqrt(targets * tgts)
 
 

time: 174 us -> 164 us (0.943)
  Pallas kernels: 22.5 us -> 29.4 us
  waiting for transfers between devices: 66.3 us -> 60.7 us
  local copies, waits for them, and re-layouts: 7.29 us -> 3.16 us
  starting transfers between devices: 58.1 us -> 54.7 us
  between operations: 4.33 us -> 1.15 us
    pallas_call x2 -> x4, Pallas kernels: 16.9 us -> 23.7 us  [the longest x2 12.4 us: kernel_part(): call(body, jax.ShapeDtypeStruct((blks, block + 16, rows), FULL), (targets...]
    ppermute x31, waiting for transfers between devices: 37.9 us -> 32.5 us  [tgt_move(): return lax.ppermute(array, 'tgt', pairs)]
    ppermute x31, starting transfers between devices: 48.2 us -> 44.7 us  [tgt_move(): return lax.ppermute(array, 'tgt', pairs)]
    slice x5 -> x0, local copies, waits for them, and re-layouts: 3.19 us -> none  [the longest x1 1.18 us: shards(): pair = jnp.concatenate([support_feats + 0 * give[:1, :1], near], 0)]
    convert_element_type x2 -> x3, other arithmetic: 3.3 us -> 0.42 us  [the longest x2 0.21 us: shards(): part = jnp.concatenate([near_part.astype(HALF), far_part.astype(HALF)], 1)]
  transfers between devices with their start and end apart: 33 -> 33, of which waited for: 14 -> 13; matrix products, arithmetic and copies ran while one was open for 11% -> 9% of each run, Pallas kernels for 9% -> 15%
where the time goes in v4:
time: 164 us; the launch traced here: 163 us
  waiting for transfers between devices  60.7 us (37%)
  starting transfers between devices  54.7 us (33%)
  Pallas kernels  29.4 us (18%)
  other arithmetic  10.4 us (6%)
  matrix products  3.89 us (2%)
  local copies, waits for them, and re-layouts  3.16 us (2%)
    ppermute x31, starting transfers between devices, tgt_move(): return lax.ppermute(array, 'tgt', pairs)  44.7 us
    ppermute x31, waiting for transfers between devices, tgt_move(): return lax.ppermute(array, 'tgt', pairs)  32.5 us
    all_to_all x1, waiting for transfers between devices, shards(): got = lax.all_to_all(part, 'blk', 0, 0, tiled=True).astype(FULL)  16.9 us
    pallas_call x2, Pallas kernels, kernel_part(): call(body, jax.ShapeDtypeStruct((blks, block + 16, rows), FULL), (targets...  12.4 us
    all_to_all x1, waiting for transfers between devices, shards(): lax.all_to_all(spread, 'blk', 0, 0, tiled=True).reshape(targets, -1)  11.4 us
    pallas_call x2, Pallas kernels, support_call(): call(kernel, outs, (steps,), [pl.BlockSpec(own_grad.shape, lambda i, w: (...  11.3 us
    all_to_all x1, starting transfers between devices, shards(): got = lax.all_to_all(part, 'blk', 0, 0, tiled=True).astype(FULL)  6.36 us
    pallas_call x1, Pallas kernels, gradients(): call(body, (jax.ShapeDtypeStruct((supports, targets), LOW), piece, piece)...  5.65 us
  transfers between devices with their start and end apart: 33, of which 13 were waited for; matrix products, arithmetic and copies ran while one was open for 9% of the time, Pallas kernels for 15%

profile of v4, /device:TPU:1, one launch (start us, length us, event | category | flops | bytes accessed | tf_op | source)
XLA Modules:
  0.0 163.3 jit_solution(4599336662170730608)
XLA Ops:
  2.8 5.1 %slice_select_fusion = bf16[1024,2048]{1,0:T(8,128)(2,1)} fusion(bf16[1024,4096]{1,0:T(8,128)(2,1)} %feats.3, pred[]{:T(512)S(6)} %eq.197), kind=kLoop, calls=%fused_computation | loop fusion | flops 2097152 | bytes 12582913 | tf_op jit(solution)/shard_map/jit(_where)/select_n | solution.py:269
  10.5 4.0 %collective-permute-start.3 = (bf16[32,4096]{1,0:T(8,128)(2,1)S(1)}, bf16[32,4096]{1,0:T(8,128)(2,1)S(1)}, u32[]{:S(2)}, u32[]{:S(2)}) collective-permute-start(bf16[32,4096]{1,0:T(8,128)(2,1)S(1)} %pad_maximum_fusion.6.refs_1_), channel_id=1, source_target_pairs={{0,224},{8,232},{16,240},{24,248},{32,0},{40,8},{48,16},{56,24},{6... | collective-permute-start | bytes 786440 | tf_op jit(solution)/shard_map/ppermute | solution.py:30
  14.6 5.6 %collective-permute-done.2.refs_3_ = bf16[32,4096]{1,0:T(8,128)(2,1)S(1)} collective-permute-done((bf16[32,4096]{1,0:T(8,128)(2,1)S(1)}, bf16[32,4096]{1,0:T(8,128)(2,1)S(1)}, u32[]{:S(2)}, u32[]{:S(2)}) %collective-permute-start.2) | collective-permute-done | bytes 262176 | tf_op jit(solution)/shard_map/ppermute | solution.py:30
  20.2 2.7 %collective-permute-start.7 = (bf16[32,4096]{1,0:T(8,128)(2,1)S(1)}, bf16[32,4096]{1,0:T(8,128)(2,1)S(1)}, u32[]{:S(2)}, u32[]{:S(2)}) collective-permute-start(bf16[32,4096]{1,0:T(8,128)(2,1)S(1)} %collective-permute-done.3.refs_4_), channel_id=1, source_target_pairs={{0,224},{8,232},{16,240},{24,248},{32,0},{40,8},{48,16},{56,24},{6... | collective-permute-start | bytes 786440 | tf_op jit(solution)/shard_map/ppermute | solution.py:30
  27.6 2.7 %collective-permute-start.11 = (bf16[32,4096]{1,0:T(8,128)(2,1)S(1)}, bf16[32,4096]{1,0:T(8,128)(2,1)S(1)}, u32[]{:S(2)}, u32[]{:S(2)}) collective-permute-start(bf16[32,4096]{1,0:T(8,128)(2,1)S(1)} %collective-permute-done.7.refs_8_), channel_id=1, source_target_pairs={{0,224},{8,232},{16,240},{24,248},{32,0},{40,8},{48,16},{56,24},{6... | collective-permute-start | bytes 786440 | tf_op jit(solution)/shard_map/ppermute | solution.py:30
  30.3 6.2 %shard_map.59 = f32[8,144,256]{2,1,0:T(8,128)S(1)} custom-call(bf16[1024,4096]{1,0:T(8,128)(2,1)} %feats.3, bf16[32,4096]{1,0:T(8,128)(2,1)S(1)} %pad_maximum_fusion.6.refs_1_, bf16[32,4096]{1,0:T(8,128)(2,1)S(1)} %collective-permute-done.1.refs_2_, bf16[32,4096]{1,0:T(8,128)(2,1)S(1)} %collective-permute-done.2.refs_3_, ...), custom_call_target="tpu_custom_call" | custom-call | flops 2147483648 | bytes 11534336 | tf_op jit(solution)/shard_map/pallas_call | solution.py:90
  36.8 3.1 %collective-permute-start.8 = (bf16[32,4096]{1,0:T(8,128)(2,1)S(1)}, bf16[32,4096]{1,0:T(8,128)(2,1)S(1)}, u32[]{:S(2)}, u32[]{:S(2)}) collective-permute-start(bf16[32,4096]{1,0:T(8,128)(2,1)S(1)} %collective-permute-done.6.refs_7_), channel_id=1, source_target_pairs={{0,8},{8,0},{16,24},{24,16},{32,40},{40,32},{48,56},{56,48},{64,72... | collective-permute-start | bytes 786440 | tf_op jit(solution)/shard_map/ppermute | solution.py:30
  40.0 2.8 %collective-permute-start.15 = (bf16[32,2048]{1,0:T(8,128)(2,1)S(1)}, bf16[32,2048]{1,0:T(8,128)(2,1)S(1)}, u32[]{:S(2)}, u32[]{:S(2)}) collective-permute-start(bf16[32,2048]{1,0:T(8,128)(2,1)S(1)} %get-tuple-element.32), channel_id=1, source_target_pairs={{0,224},{8,232},{16,240},{24,248},{32,0},{40,8},{48,16},{56,24},{6... | collective-permute-start | bytes 393224 | tf_op jit(solution)/shard_map/ppermute | solution.py:30
  47.9 6.2 %shard_map.60 = f32[8,144,256]{2,1,0:T(8,128)S(1)} custom-call(bf16[1024,4096]{1,0:T(8,128)(2,1)} %feats.3, bf16[32,4096]{1,0:T(8,128)(2,1)S(1)} %collective-permute-done.8.refs_1_, bf16[32,4096]{1,0:T(8,128)(2,1)S(1)} %collective-permute-done.9.refs_2_, bf16[32,4096]{1,0:T(8,128)(2,1)S(1)} %collective-permute-done.10.refs_3_, ...), custom_call_target="tpu_custom_call" | custom-call | flops 2147483648 | bytes 11534336 | tf_op jit(solution)/shard_map/pallas_call | solution.py:90
  55.6 6.4 %all-to-all-start = ((f16[8,288,256]{2,1,0:T(8,128)(2,1)}), f16[8,288,256]{2,1,0:T(8,128)(2,1)S(1)}, u32[]{:S(2)}, u32[]{:S(2)}) async-start(f16[8,288,256]{2,1,0:T(8,128)(2,1)} %pad_maximum_fusion), calls=%async_computation | async-start | bytes 2359296 | tf_op jit(solution)/shard_map/all_to_all | solution.py:374
  62.7 16.9 %all-to-all-done = f16[8,288,256]{2,1,0:T(8,128)(2,1)S(1)} async-done(((f16[8,288,256]{2,1,0:T(8,128)(2,1)}), f16[8,288,256]{2,1,0:T(8,128)(2,1)S(1)}, u32[]{:S(2)}, u32[]{:S(2)}) %all-to-all-start) | async-done | bytes 1179680 | tf_op jit(solution)/shard_map/all_to_all | solution.py:374
  81.2 3.6 %all-to-all-start.1 = ((bf16[8,128,512]{2,1,0:T(8,128)(2,1)}), bf16[8,128,512]{2,1,0:T(8,128)(2,1)S(1)}, u32[]{:S(2)}, u32[]{:S(2)}) async-start(bf16[8,128,512]{2,1,0:T(8,128)(2,1)} %broadcast_in_dim.9), calls=%async_computation.1 | async-start | bytes 2097152 | tf_op jit(solution)/shard_map/all_to_all | solution.py:382
  88.9 11.4 %all-to-all-done.1 = bf16[8,128,512]{2,1,0:T(8,128)(2,1)S(1)} async-done(((bf16[8,128,512]{2,1,0:T(8,128)(2,1)}), bf16[8,128,512]{2,1,0:T(8,128)(2,1)S(1)}, u32[]{:S(2)}, u32[]{:S(2)}) %all-to-all-start.1) | async-done | bytes 1048608 | tf_op jit(solution)/shard_map/all_to_all | solution.py:382
  101.5 5.6 %shard_map.61 = (bf16[512,1024]{1,0:T(8,128)(2,1)S(1)}, f32[125,256]{1,0:T(8,128)S(1)}, f32[125,256]{1,0:T(8,128)S(1)}) custom-call(s32[2]{0:T(128)S(1)} %pad_add_fusion.scalars, bf16[1024,512]{1,0:T(8,128)(2,1)S(1)} %bitcast.77, s32[1024,1]{1,0:T(8,128)S(1)} %copy.6.column, s32[1,1024]{1,0:T(1,128)S(1)} %bitcast.79, ...), custom_call_target="tpu_custom_call" | custom-call | flops 2684354560 | bytes 5242880 | tf_op jit(solution)/shard_map/pallas_call | solution.py:139
  110.9 5.2 %shard_map.62 = (bf16[64,1536]{1,0:T(8,128)(2,1)S(1)}, bf16[64,1536]{1,0:T(8,128)(2,1)S(1)}, f32[64,512]{1,0:T(8,128)S(1)}, f32[64,2048]{1,0:T(8,128)S(1)}, f32[64,2048]{1,0:T(8,128)S(1)}) custom-call(s32[1]{0:T(128)} %bitcast.which_ref, bf16[512,1024]{1,0:T(8,128)(2,1)S(1)} %get-tuple-element.15.own, bf16[512,1024]{1,0:T(8,128)(2,1)S(1)} %collective-permute-done.17.other, ...), custom_call_target="tpu_custom_call" | custom-call | flops 1610612736 | bytes 9961472 | tf_op jit(solution)/shard_map/pallas_call | solution.py:174
  119.8 4.9 %collective-permute-done.20 = bf16[64,1536]{1,0:T(8,128)(2,1)S(1)} collective-permute-done((bf16[64,1536]{1,0:T(8,128)(2,1)S(1)}, bf16[64,1536]{1,0:T(8,128)(2,1)S(1)}, u32[]{:S(2)}, u32[]{:S(2)}) %collective-permute-start.20) | collective-permute-done | bytes 196640 | tf_op jit(solution)/shard_map/ppermute | solution.py:30
  124.9 2.7 %collective-permute-start.25 = (bf16[64,2560]{1,0:T(8,128)(2,1)S(1)}, bf16[64,2560]{1,0:T(8,128)(2,1)S(1)}, u32[]{:S(2)}, u32[]{:S(2)}) collective-permute-start(bf16[64,2560]{1,0:T(8,128)(2,1)S(1)} %pad_maximum_fusion.2.refs_1_), channel_id=1, source_target_pairs={{0,224},{8,232},{16,240},{24,248},{32,0},{40,8},{48,16},{56,24},{6... | collective-permute-start | bytes 983048 | tf_op jit(solution)/shard_map/ppermute | solution.py:30
  127.7 6.0 %shard_map.63 = (f32[64,2048]{1,0:T(8,128)S(1)}, f32[64,2048]{1,0:T(8,128)S(1)}, f32[64,2048]{1,0:T(8,128)S(1)}, f32[64,2048]{1,0:T(8,128)S(1)}, f32[64,2048]{1,0:T(8,128)S(1)}) custom-call(s32[1]{0:T(128)} %bitcast.which_ref, bf16[512,1024]{1,0:T(8,128)(2,1)S(1)} %get-tuple-element.15.own, bf16[512,1024]{1,0:T(8,128)(2,1)S(1)} %collective-permute-done.17.other, ...), custom_call_target="tpu_custom_call" | custom-call | flops 2684354560 | bytes 11010048 | tf_op jit(solution)/shard_map/pallas_call | solution.py:174
  134.7 2.9 %collective-permute-start.26 = (bf16[64,2560]{1,0:T(8,128)(2,1)S(1)}, bf16[64,2560]{1,0:T(8,128)(2,1)S(1)}, u32[]{:S(2)}, u32[]{:S(2)}) collective-permute-start(bf16[64,2560]{1,0:T(8,128)(2,1)S(1)} %pad_maximum_fusion.5), channel_id=1, source_target_pairs={{0,224},{8,232},{16,240},{24,248},{32,0},{40,8},{48,16},{56,24},{6... | collective-permute-start | bytes 983048 | tf_op jit(solution)/shard_map/ppermute | solution.py:30
  137.7 5.6 %collective-permute-done.23 = bf16[64,2560]{1,0:T(8,128)(2,1)S(1)} collective-permute-done((bf16[64,2560]{1,0:T(8,128)(2,1)S(1)}, bf16[64,2560]{1,0:T(8,128)(2,1)S(1)}, u32[]{:S(2)}, u32[]{:S(2)}) %collective-permute-start.23) | collective-permute-done | bytes 327712 | tf_op jit(solution)/shard_map/ppermute | solution.py:30
  143.5 2.7 %collective-permute-start.27 = (bf16[64,2048]{1,0:T(8,128)(2,1)S(1)}, bf16[64,2048]{1,0:T(8,128)(2,1)S(1)}, u32[]{:S(2)}, u32[]{:S(2)}) collective-permute-start(bf16[64,2048]{1,0:T(8,128)(2,1)S(1)} %add_convert_fusion), channel_id=1, source_target_pairs={{0,224},{8,232},{16,240},{24,248},{32,0},{40,8},{48,16},{56,24},{6... | collective-permute-start | bytes 786440 | tf_op jit(solution)/shard_map/ppermute | solution.py:30
  146.2 4.9 %collective-permute-done.24 = bf16[64,2560]{1,0:T(8,128)(2,1)S(1)} collective-permute-done((bf16[64,2560]{1,0:T(8,128)(2,1)S(1)}, bf16[64,2560]{1,0:T(8,128)(2,1)S(1)}, u32[]{:S(2)}, u32[]{:S(2)}) %collective-permute-start.24) | collective-permute-done | bytes 327712 | tf_op jit(solution)/shard_map/ppermute | solution.py:30
  151.5 4.5 %collective-permute-done.28 = bf16[32,3072]{1,0:T(8,128)(2,1)S(1)} collective-permute-done((bf16[32,3072]{1,0:T(8,128)(2,1)S(1)}, bf16[32,3072]{1,0:T(8,128)(2,1)S(1)}, u32[]{:S(2)}, u32[]{:S(2)}) %collective-permute-start.28) | collective-permute-done | bytes 196640 | tf_op jit(solution)/shard_map/ppermute | solution.py:30
  156.1 4.8 %collective-permute-start.30 = (f32[125,256]{1,0:T(8,128)S(1)}, f32[125,256]{1,0:T(8,128)S(1)}, u32[]{:S(2)}, u32[]{:S(2)}) collective-permute-start(f32[125,256]{1,0:T(8,128)S(1)} %pad_maximum_fusion.8), channel_id=1, source_target_pairs={{0,8},{8,0},{16,24},{24,16},{32,40},{40,32},{48,56},{56,48},{64,72... | collective-permute-start | bytes 384008 | tf_op jit(solution)/shard_map/ppermute | solution.py:30
  (119 shorter events, 35.6 us)
Async XLA Ops:
  0.6 8.1 %collective-permute-start = (bf16[16,4096]{1,0:T(8,128)(2,1)}, bf16[16,4096]{1,0:T(8,128)(2,1)S(1)}, u32[]{:S(2)}, u32[]{:S(2)}) collective-permute-start(bf16[16,4096]{1,0:T(8,128)(2,1)} %param.5), channel_id=1, source_target_pairs={{0,16},{8,24},{16,0},{24,8},{32,48},{40,56},{48,32},{56,40},{64,80... | collective-permute-start | bytes 393224 | tf_op jit(solution)/shard_map/ppermute | solution.py:30
  8.8 11.4 %collective-permute-start.2 = (bf16[32,4096]{1,0:T(8,128)(2,1)S(1)}, bf16[32,4096]{1,0:T(8,128)(2,1)S(1)}, u32[]{:S(2)}, u32[]{:S(2)}) collective-permute-start(bf16[32,4096]{1,0:T(8,128)(2,1)S(1)} %pad_maximum_fusion.6.refs_1_), channel_id=1, source_target_pairs={{0,32},{8,40},{16,48},{24,56},{32,64},{40,72},{48,80},{56,88},{64,... | collective-permute-start | bytes 786440 | tf_op jit(solution)/shard_map/ppermute | solution.py:30
  10.5 9.7 %collective-permute-start.3 = (bf16[32,4096]{1,0:T(8,128)(2,1)S(1)}, bf16[32,4096]{1,0:T(8,128)(2,1)S(1)}, u32[]{:S(2)}, u32[]{:S(2)}) collective-permute-start(bf16[32,4096]{1,0:T(8,128)(2,1)S(1)} %pad_maximum_fusion.6.refs_1_), channel_id=1, source_target_pairs={{0,224},{8,232},{16,240},{24,248},{32,0},{40,8},{48,16},{56,24},{6... | collective-permute-start | bytes 786440 | tf_op jit(solution)/shard_map/ppermute | solution.py:30
  20.2 7.5 %collective-permute-start.6 = (bf16[32,4096]{1,0:T(8,128)(2,1)S(1)}, bf16[32,4096]{1,0:T(8,128)(2,1)S(1)}, u32[]{:S(2)}, u32[]{:S(2)}) collective-permute-start(bf16[32,4096]{1,0:T(8,128)(2,1)S(1)} %collective-permute-done.2.refs_3_), channel_id=1, source_target_pairs={{0,32},{8,40},{16,48},{24,56},{32,64},{40,72},{48,80},{56,88},{64,... | collective-permute-start | bytes 786440 | tf_op jit(solution)/shard_map/ppermute | solution.py:30
  20.2 7.5 %collective-permute-start.7 = (bf16[32,4096]{1,0:T(8,128)(2,1)S(1)}, bf16[32,4096]{1,0:T(8,128)(2,1)S(1)}, u32[]{:S(2)}, u32[]{:S(2)}) collective-permute-start(bf16[32,4096]{1,0:T(8,128)(2,1)S(1)} %collective-permute-done.3.refs_4_), channel_id=1, source_target_pairs={{0,224},{8,232},{16,240},{24,248},{32,0},{40,8},{48,16},{56,24},{6... | collective-permute-start | bytes 786440 | tf_op jit(solution)/shard_map/ppermute | solution.py:30
  22.9 7.5 %collective-permute-start.1 = (bf16[32,4096]{1,0:T(8,128)(2,1)S(1)}, bf16[32,4096]{1,0:T(8,128)(2,1)S(1)}, u32[]{:S(2)}, u32[]{:S(2)}) collective-permute-start(bf16[32,4096]{1,0:T(8,128)(2,1)S(1)} %pad_maximum_fusion.6.refs_1_), channel_id=1, source_target_pairs={{0,8},{8,0},{16,24},{24,16},{32,40},{40,32},{48,56},{56,48},{64,72... | collective-permute-start | bytes 786440 | tf_op jit(solution)/shard_map/ppermute | solution.py:30
  27.6 9.0 %collective-permute-start.10 = (bf16[32,4096]{1,0:T(8,128)(2,1)S(1)}, bf16[32,4096]{1,0:T(8,128)(2,1)S(1)}, u32[]{:S(2)}, u32[]{:S(2)}) collective-permute-start(bf16[32,4096]{1,0:T(8,128)(2,1)S(1)} %collective-permute-done.6.refs_7_), channel_id=1, source_target_pairs={{0,32},{8,40},{16,48},{24,56},{32,64},{40,72},{48,80},{56,88},{64,... | collective-permute-start | bytes 786440 | tf_op jit(solution)/shard_map/ppermute | solution.py:30
  27.6 9.0 %collective-permute-start.11 = (bf16[32,4096]{1,0:T(8,128)(2,1)S(1)}, bf16[32,4096]{1,0:T(8,128)(2,1)S(1)}, u32[]{:S(2)}, u32[]{:S(2)}) collective-permute-start(bf16[32,4096]{1,0:T(8,128)(2,1)S(1)} %collective-permute-done.7.refs_8_), channel_id=1, source_target_pairs={{0,224},{8,232},{16,240},{24,248},{32,0},{40,8},{48,16},{56,24},{6... | collective-permute-start | bytes 786440 | tf_op jit(solution)/shard_map/ppermute | solution.py:30
  36.7 6.9 %collective-permute-start.14 = (bf16[32,2048]{1,0:T(8,128)(2,1)S(1)}, bf16[32,2048]{1,0:T(8,128)(2,1)S(1)}, u32[]{:S(2)}, u32[]{:S(2)}) collective-permute-start(bf16[32,2048]{1,0:T(8,128)(2,1)S(1)} %get-tuple-element.33), channel_id=1, source_target_pairs={{0,32},{8,40},{16,48},{24,56},{32,64},{40,72},{48,80},{56,88},{64,... | collective-permute-start | bytes 393224 | tf_op jit(solution)/shard_map/ppermute | solution.py:30
  36.8 10.1 %collective-permute-start.8 = (bf16[32,4096]{1,0:T(8,128)(2,1)S(1)}, bf16[32,4096]{1,0:T(8,128)(2,1)S(1)}, u32[]{:S(2)}, u32[]{:S(2)}) collective-permute-start(bf16[32,4096]{1,0:T(8,128)(2,1)S(1)} %collective-permute-done.6.refs_7_), channel_id=1, source_target_pairs={{0,8},{8,0},{16,24},{24,16},{32,40},{40,32},{48,56},{56,48},{64,72... | collective-permute-start | bytes 786440 | tf_op jit(solution)/shard_map/ppermute | solution.py:30
  39.9 7.1 %collective-permute-start.9 = (bf16[32,4096]{1,0:T(8,128)(2,1)S(1)}, bf16[32,4096]{1,0:T(8,128)(2,1)S(1)}, u32[]{:S(2)}, u32[]{:S(2)}) collective-permute-start(bf16[32,4096]{1,0:T(8,128)(2,1)S(1)} %collective-permute-done.7.refs_8_), channel_id=1, source_target_pairs={{0,8},{8,0},{16,24},{24,16},{32,40},{40,32},{48,56},{56,48},{64,72... | collective-permute-start | bytes 786440 | tf_op jit(solution)/shard_map/ppermute | solution.py:30
  40.0 6.0 %collective-permute-start.15 = (bf16[32,2048]{1,0:T(8,128)(2,1)S(1)}, bf16[32,2048]{1,0:T(8,128)(2,1)S(1)}, u32[]{:S(2)}, u32[]{:S(2)}) collective-permute-start(bf16[32,2048]{1,0:T(8,128)(2,1)S(1)} %get-tuple-element.32), channel_id=1, source_target_pairs={{0,224},{8,232},{16,240},{24,248},{32,0},{40,8},{48,16},{56,24},{6... | collective-permute-start | bytes 393224 | tf_op jit(solution)/shard_map/ppermute | solution.py:30
  46.9 64.1 %collective-permute-start.18 = (bf16[1024,2048]{1,0:T(8,128)(2,1)}, bf16[1024,2048]{1,0:T(8,128)(2,1)}, u32[]{:S(2)}, u32[]{:S(2)}) collective-permute-start(bf16[1024,2048]{1,0:T(8,128)(2,1)} %slice_select_fusion), channel_id=1, source_target_pairs={{0,8},{8,0},{16,24},{24,16},{32,40},{40,32},{48,56},{56,48},{64,72... | collective-permute-start | bytes 12582920 | tf_op jit(solution)/shard_map/ppermute | solution.py:30
  55.6 24.1 %all-to-all-start = ((f16[8,288,256]{2,1,0:T(8,128)(2,1)}), f16[8,288,256]{2,1,0:T(8,128)(2,1)S(1)}, u32[]{:S(2)}, u32[]{:S(2)}) async-start(f16[8,288,256]{2,1,0:T(8,128)(2,1)} %pad_maximum_fusion), calls=%async_computation | async-start | bytes 2359296 | tf_op jit(solution)/shard_map/all_to_all | solution.py:374
  81.2 19.1 %all-to-all-start.1 = ((bf16[8,128,512]{2,1,0:T(8,128)(2,1)}), bf16[8,128,512]{2,1,0:T(8,128)(2,1)S(1)}, u32[]{:S(2)}, u32[]{:S(2)}) async-start(bf16[8,128,512]{2,1,0:T(8,128)(2,1)} %broadcast_in_dim.9), calls=%async_computation.1 | async-start | bytes 2097152 | tf_op jit(solution)/shard_map/all_to_all | solution.py:382
  116.2 8.5 %collective-permute-start.20 = (bf16[64,1536]{1,0:T(8,128)(2,1)S(1)}, bf16[64,1536]{1,0:T(8,128)(2,1)S(1)}, u32[]{:S(2)}, u32[]{:S(2)}) collective-permute-start(bf16[64,1536]{1,0:T(8,128)(2,1)S(1)} %get-tuple-element.19), channel_id=1, source_target_pairs={{0,32},{8,40},{16,48},{24,56},{32,64},{40,72},{48,80},{56,88},{64,... | collective-permute-start | bytes 589832 | tf_op jit(solution)/shard_map/ppermute | solution.py:30
  117.2 7.7 %collective-permute-start.21 = (bf16[64,1536]{1,0:T(8,128)(2,1)S(1)}, bf16[64,1536]{1,0:T(8,128)(2,1)S(1)}, u32[]{:S(2)}, u32[]{:S(2)}) collective-permute-start(bf16[64,1536]{1,0:T(8,128)(2,1)S(1)} %get-tuple-element.21), channel_id=1, source_target_pairs={{0,224},{8,232},{16,240},{24,248},{32,0},{40,8},{48,16},{56,24},{6... | collective-permute-start | bytes 589832 | tf_op jit(solution)/shard_map/ppermute | solution.py:30
  124.8 9.7 %collective-permute-start.22 = (bf16[64,2560]{1,0:T(8,128)(2,1)S(1)}, bf16[64,2560]{1,0:T(8,128)(2,1)S(1)}, u32[]{:S(2)}, u32[]{:S(2)}) collective-permute-start(bf16[64,2560]{1,0:T(8,128)(2,1)S(1)} %pad_maximum_fusion.1.refs_0_), channel_id=1, source_target_pairs={{0,32},{8,40},{16,48},{24,56},{32,64},{40,72},{48,80},{56,88},{64,... | collective-permute-start | bytes 983048 | tf_op jit(solution)/shard_map/ppermute | solution.py:30
  124.9 9.7 %collective-permute-start.25 = (bf16[64,2560]{1,0:T(8,128)(2,1)S(1)}, bf16[64,2560]{1,0:T(8,128)(2,1)S(1)}, u32[]{:S(2)}, u32[]{:S(2)}) collective-permute-start(bf16[64,2560]{1,0:T(8,128)(2,1)S(1)} %pad_maximum_fusion.2.refs_1_), channel_id=1, source_target_pairs={{0,224},{8,232},{16,240},{24,248},{32,0},{40,8},{48,16},{56,24},{6... | collective-permute-start | bytes 983048 | tf_op jit(solution)/shard_map/ppermute | solution.py:30
  134.5 8.7 %collective-permute-start.23 = (bf16[64,2560]{1,0:T(8,128)(2,1)S(1)}, bf16[64,2560]{1,0:T(8,128)(2,1)S(1)}, u32[]{:S(2)}, u32[]{:S(2)}) collective-permute-start(bf16[64,2560]{1,0:T(8,128)(2,1)S(1)} %pad_maximum_fusion.3), channel_id=1, source_target_pairs={{0,32},{8,40},{16,48},{24,56},{32,64},{40,72},{48,80},{56,88},{64,... | collective-permute-start | bytes 983048 | tf_op jit(solution)/shard_map/ppermute | solution.py:30
  134.7 8.7 %collective-permute-start.26 = (bf16[64,2560]{1,0:T(8,128)(2,1)S(1)}, bf16[64,2560]{1,0:T(8,128)(2,1)S(1)}, u32[]{:S(2)}, u32[]{:S(2)}) collective-permute-start(bf16[64,2560]{1,0:T(8,128)(2,1)S(1)} %pad_maximum_fusion.5), channel_id=1, source_target_pairs={{0,224},{8,232},{16,240},{24,248},{32,0},{40,8},{48,16},{56,24},{6... | collective-permute-start | bytes 983048 | tf_op jit(solution)/shard_map/ppermute | solution.py:30
  143.3 7.8 %collective-permute-start.24 = (bf16[64,2560]{1,0:T(8,128)(2,1)S(1)}, bf16[64,2560]{1,0:T(8,128)(2,1)S(1)}, u32[]{:S(2)}, u32[]{:S(2)}) collective-permute-start(bf16[64,2560]{1,0:T(8,128)(2,1)S(1)} %pad_maximum_fusion.4), channel_id=1, source_target_pairs={{0,32},{8,40},{16,48},{24,56},{32,64},{40,72},{48,80},{56,88},{64,... | collective-permute-start | bytes 983048 | tf_op jit(solution)/shard_map/ppermute | solution.py:30
  143.5 7.7 %collective-permute-start.27 = (bf16[64,2048]{1,0:T(8,128)(2,1)S(1)}, bf16[64,2048]{1,0:T(8,128)(2,1)S(1)}, u32[]{:S(2)}, u32[]{:S(2)}) collective-permute-start(bf16[64,2048]{1,0:T(8,128)(2,1)S(1)} %add_convert_fusion), channel_id=1, source_target_pairs={{0,224},{8,232},{16,240},{24,248},{32,0},{40,8},{48,16},{56,24},{6... | collective-permute-start | bytes 786440 | tf_op jit(solution)/shard_map/ppermute | solution.py:30
  156.1 5.8 %collective-permute-start.30 = (f32[125,256]{1,0:T(8,128)S(1)}, f32[125,256]{1,0:T(8,128)S(1)}, u32[]{:S(2)}, u32[]{:S(2)}) collective-permute-start(f32[125,256]{1,0:T(8,128)S(1)} %pad_maximum_fusion.8), channel_id=1, source_target_pairs={{0,8},{8,0},{16,24},{24,16},{32,40},{40,32},{48,56},{56,48},{64,72... | collective-permute-start | bytes 384008 | tf_op jit(solution)/shard_map/ppermute | solution.py:30
  (13 other events, 49.4 us)

commit v5 on v4

--- a/solution.py
+++ b/solution.py
@@ -59,43 +59,45 @@
     targets, features = target_feats.shape
     rows = sum(p.shape[0] for p in pieces)
     count = len(pieces)
-    tile = 256
+    depth = features // 4
+    steps = features // depth
     block = targets // blks
-    per = tile // block
 
     def body(*refs):
         feats, parts = refs[0], refs[1 : 1 + count]
-        out, held, sem = refs[1 + count :]
-
-        @pl.when(pl.program_id(0) == 0)
-        def _():
-            copies, start = [], 0
-            for i, part in enumerate(parts):
-                copies.append(pltpu.make_async_copy(part, held.at[pl.ds(start, part.shape[0])], sem.at[i]))
-                start += part.shape[0]
-            for copy in copies:
-                copy.start()
-            for copy in copies:
-                copy.wait()
-
-        product = lax.dot_general(feats[...], held[...], NT, preferred_element_type=FULL) * scale
-        top = jnp.max(jnp.abs(product).reshape(tile // 8, 8, rows), axis=0)
-        top = jnp.max(jnp.max(top, axis=1, keepdims=True), axis=0, keepdims=True)
-        power = jnp.floor(jnp.log2(jnp.maximum(top, 1e-30)))
-        product = product * jnp.exp2(TOP - power)
-        for i in range(per):
-            out[i, :block] = product[i * block : (i + 1) * block]
-            out[i, block:] = jnp.broadcast_to(power, (16, rows))
+        out, total = refs[1 + count :]
+        step = pl.program_id(0)
+        held = jnp.concatenate([part[...] for part in parts], 0)
+        product = lax.dot_general(feats[...], held, NT, preferred_element_type=FULL)
+
+        @pl.when(step == 0)
+        def _():
+            total[...] = product
+
+        @pl.when(step > 0)
+        def _():
+            total[...] += product
+
+        @pl.when(step == steps - 1)
+        def _():
+            top = jnp.max(jnp.abs(total[...]).reshape(targets // 8, 8, rows), axis=0)
+            top = jnp.max(jnp.max(top, axis=1, keepdims=True), axis=0, keepdims=True) * scale
+            power = jnp.floor(jnp.log2(jnp.maximum(top, 1e-30)))
+            factor = jnp.exp2(TOP - power) * scale
+            for i in range(blks):
+                out[i, :block] = total[i * block : (i + 1) * block] * factor
+                out[i, block:] = jnp.broadcast_to(power, (16, rows))
 
     return call(
         body,
         jax.ShapeDtypeStruct((blks, block + 16, rows), FULL),
-        (targets // tile,),
-        [pl.BlockSpec((tile, features), lambda i: (i, 0))] + [pl.BlockSpec(memory_space=pltpu.HBM)] * count,
-        pl.BlockSpec((per, block + 16, rows), lambda i: (i, 0, 0)),
+        (steps,),
+        [pl.BlockSpec((targets, depth), lambda i: (0, i))]
+        + [pl.BlockSpec((p.shape[0], depth), lambda i: (0, i)) for p in pieces],
+        pl.BlockSpec((blks, block + 16, rows), lambda i: (0, 0, 0)),
         2 * targets * features * rows,
         2 * features * (targets + rows) + 4 * targets * rows,
-        [pltpu.VMEM((rows, features), LOW), pltpu.SemaphoreType.DMA((count,))],
+        [pltpu.VMEM((targets, rows), FULL)],
     )(target_feats, *pieces)
 
 
@@ -157,34 +159,55 @@
     )(jnp.stack([first_class, core]), kernel_low, labels[:, None], labels[None, :], coefs_here, coefs_ring, own_coefs, order)
 
 
-def support_call(body, outs, out_specs, factors, start, count, extra, extra_specs, chip_rows):
+def support_call(body, outs, factors, start, count, extra, extra_specs, chip_rows):
     own_grad, other_grad, target_feats, taken, which = factors
     targets, features = target_feats.shape
     half = features // 2
     steps = half // SUPPORT_TILE
-    rows = slice(start * chip_rows, (start + count) * chip_rows)
+    rows = count * chip_rows
 
     def kernel(which_ref, own, other, feats, theirs, *refs):
-        body(
-            jnp.dot(own[rows, :], feats[...], preferred_element_type=FULL)
-            + jnp.dot(other[rows, :], theirs[...], preferred_element_type=FULL),
-            *refs,
-        )
-
+        grads, tiles, grad_sem, tile_sem = refs[-4:]
+        copies = [
+            pltpu.make_async_copy(grad.at[pl.ds(start * chip_rows, rows)], grads.at[i], grad_sem.at[i])
+            for i, grad in enumerate((own, other))
+        ]
+        first = which_ref[0] * half
+        loads = []
+        for j in range(steps):
+            here = pl.ds(pl.multiple_of(first + j * SUPPORT_TILE, SUPPORT_TILE), SUPPORT_TILE)
+            there = pl.ds(j * SUPPORT_TILE, SUPPORT_TILE)
+            loads.append(
+                [
+                    pltpu.make_async_copy(feats.at[:, here], tiles.at[j, 0], tile_sem.at[j, 0]),
+                    pltpu.make_async_copy(theirs.at[:, there], tiles.at[j, 1], tile_sem.at[j, 1]),
+                ]
+            )
+        for copy in copies + sum(loads, []):
+            copy.start()
+        for copy in copies:
+            copy.wait()
+        for j in range(steps):
+            for load in loads[j]:
+                load.wait()
+            product = jnp.dot(grads[0], tiles[j, 0], preferred_element_type=FULL)
+            body(j, product + jnp.dot(grads[1], tiles[j, 1], preferred_element_type=FULL), *refs[:-4])
+
+    whole = [pl.BlockSpec(o.shape, lambda i, w: (0, 0)) for o in outs]
     return call(
         kernel,
         outs,
-        (steps,),
+        (1,),
+        [pl.BlockSpec(memory_space=pltpu.HBM)] * 4 + extra_specs,
+        tuple(whole),
+        4 * rows * targets * half,
+        4 * targets * half + 4 * rows * half,
         [
-            pl.BlockSpec(own_grad.shape, lambda i, w: (0, 0)),
-            pl.BlockSpec(other_grad.shape, lambda i, w: (0, 0)),
-            pl.BlockSpec((targets, SUPPORT_TILE), lambda i, w: (0, w[0] * steps + i)),
-            pl.BlockSpec((targets, SUPPORT_TILE), lambda i, w: (0, i)),
-        ]
-        + extra_specs,
-        out_specs,
-        4 * count * chip_rows * targets * half,
-        4 * targets * half + 4 * count * chip_rows * half,
+            pltpu.VMEM((2, rows, targets), LOW),
+            pltpu.VMEM((steps, 2, targets, SUPPORT_TILE), LOW),
+            pltpu.SemaphoreType.DMA((2,)),
+            pltpu.SemaphoreType.DMA((steps, 2)),
+        ],
         prefetch=1,
     )(which, own_grad, other_grad, target_feats, taken, *extra)
 
@@ -192,27 +215,20 @@
 def support_first(factors, coef, other_coef, chip_rows):
     half = factors[3].shape[1]
     edge = half // 2
-    steps = half // SUPPORT_TILE
     classes, columns = coef.shape
     rest = classes - chip_rows
     fold = 2 * columns
 
-    def body(product, coef_ref, other_ref, up, down, folded, above, below):
-        step = pl.program_id(0)
-        above[...] = product[chip_rows : 2 * chip_rows]
-        below[...] = product[2 * chip_rows :]
+    def body(j, product, coef_ref, other_ref, up, down, folded, above, below):
+        here = slice(j * SUPPORT_TILE, (j + 1) * SUPPORT_TILE)
+        above[:, here] = product[chip_rows : 2 * chip_rows]
+        below[:, here] = product[2 * chip_rows :]
         far = product[:chip_rows].astype(LOW)
-
-        @pl.when(step < steps // 2)
-        def _():
-            up[:, pl.ds(pl.multiple_of(step * SUPPORT_TILE, SUPPORT_TILE), SUPPORT_TILE)] = far
-
-        @pl.when(step >= steps // 2)
-        def _():
-            down[:, pl.ds(pl.multiple_of((step - steps // 2) * SUPPORT_TILE, SUPPORT_TILE), SUPPORT_TILE)] = far
-
-        @pl.when(step == 0)
-        def _():
+        if here.stop <= edge:
+            up[:, here] = far
+        else:
+            down[:, here.start - edge : here.stop - edge] = far
+        if j == 0:
             total = coef_ref[...] + other_ref[...]
             lower = jnp.concatenate([total[chip_rows:], jnp.zeros((chip_rows - rest, columns), FULL)], 0)
             total = jnp.concatenate([total[:chip_rows], lower], 1)
@@ -220,42 +236,24 @@
             up[:, edge:] = total.astype(LOW)
             down[:, edge:] = total.astype(LOW)
 
-    whole = lambda i, w: (0, 0)
     first = jax.ShapeDtypeStruct((chip_rows, edge + fold), LOW)
-    return support_call(
-        body,
-        (first, first, jax.ShapeDtypeStruct((chip_rows, fold), FULL)) + (jax.ShapeDtypeStruct((chip_rows, half), FULL),) * 2,
-        (pl.BlockSpec((chip_rows, edge + fold), whole),) * 2
-        + (pl.BlockSpec((chip_rows, fold), whole),)
-        + (pl.BlockSpec((chip_rows, SUPPORT_TILE), lambda i, w: (0, i)),) * 2,
-        factors,
-        0,
-        3,
-        [coef, other_coef],
-        [pl.BlockSpec(coef.shape, whole)] * 2,
-        chip_rows,
-    )
+    block = jax.ShapeDtypeStruct((chip_rows, half), FULL)
+    outs = (first, first, jax.ShapeDtypeStruct((chip_rows, fold), FULL), block, block)
+    extra_specs = [pl.BlockSpec(coef.shape, lambda i, w: (0, 0))] * 2
+    return support_call(body, outs, factors, 0, 3, [coef, other_coef], extra_specs, chip_rows)
 
 
 def support_rest(factors, chip_rows, earlier):
     half = factors[3].shape[1]
     count = len(RING) - 3
 
-    def body(product, *refs):
+    def body(j, product, *refs):
         for i, out in enumerate(refs[len(earlier) :]):
-            out[...] = product[i * chip_rows : (i + 1) * chip_rows]
-
-    return support_call(
-        body,
-        (jax.ShapeDtypeStruct((chip_rows, half), FULL),) * count,
-        (pl.BlockSpec((chip_rows, SUPPORT_TILE), lambda i, w: (0, i)),) * count,
-        factors,
-        3,
-        count,
-        list(earlier),
-        [pl.BlockSpec(memory_space=pl.ANY)] * len(earlier),
-        chip_rows,
-    )
+            out[:, j * SUPPORT_TILE : (j + 1) * SUPPORT_TILE] = product[i * chip_rows : (i + 1) * chip_rows]
+
+    outs = (jax.ShapeDtypeStruct((chip_rows, half), FULL),) * count
+    extra_specs = [pl.BlockSpec(memory_space=pl.ANY)] * len(earlier)
+    return support_call(body, outs, factors, 3, count, list(earlier), extra_specs, chip_rows)
 
 
 def order_matrix(shards, rows):

time: 164 us -> 163 us (level)
  transfers between devices with their start and end apart: 33 -> 33, of which waited for: 13 -> 13; matrix products, arithmetic and copies ran while one was open for 9% -> 9% of each run, Pallas kernels for 15% -> 14%
where the time goes in v5:
time: 163 us; the launch traced here: 162 us
  waiting for transfers between devices  61.3 us (38%)
  starting transfers between devices  54.7 us (34%)
  Pallas kernels  27.9 us (17%)
  other arithmetic  10.4 us (6%)
  matrix products  3.89 us (2%)
  local copies, waits for them, and re-layouts  3.16 us (2%)
    ppermute x31, starting transfers between devices, tgt_move(): return lax.ppermute(array, 'tgt', pairs)  44.7 us
    ppermute x31, waiting for transfers between devices, tgt_move(): return lax.ppermute(array, 'tgt', pairs)  33 us
    all_to_all x1, waiting for transfers between devices, shards(): got = lax.all_to_all(part, 'blk', 0, 0, tiled=True).astype(FULL)  16.9 us
    pallas_call x2, Pallas kernels, kernel_part(): call(body, jax.ShapeDtypeStruct((blks, block + 16, rows), FULL), (steps,)...  12.3 us
    all_to_all x1, waiting for transfers between devices, shards(): lax.all_to_all(spread, 'blk', 0, 0, tiled=True).reshape(targets, -1)  11.4 us
    pallas_call x2, Pallas kernels, support_call(): call(kernel, outs, (1,), [pl.BlockSpec(memory_space=pltpu.HBM)] * 4 + ext...  9.91 us
    all_to_all x1, starting transfers between devices, shards(): got = lax.all_to_all(part, 'blk', 0, 0, tiled=True).astype(FULL)  6.35 us
    pallas_call x1, Pallas kernels, gradients(): call(body, (jax.ShapeDtypeStruct((supports, targets), LOW), piece, piece)...  5.65 us
  transfers between devices with their start and end apart: 33, of which 13 were waited for; matrix products, arithmetic and copies ran while one was open for 9% of the time, Pallas kernels for 14%

profile of v5, /device:TPU:1, one launch (start us, length us, event | category | flops | bytes accessed | tf_op | source)
XLA Modules:
  0.0 162.5 jit_solution(16429497172000282720)
XLA Ops:
  2.8 5.1 %slice_select_fusion = bf16[1024,2048]{1,0:T(8,128)(2,1)} fusion(bf16[1024,4096]{1,0:T(8,128)(2,1)} %feats.3, pred[]{:T(512)S(6)} %eq.197), kind=kLoop, calls=%fused_computation | loop fusion | flops 2097152 | bytes 12582913 | tf_op jit(solution)/shard_map/jit(_where)/select_n | solution.py:267
  10.5 4.0 %collective-permute-start.3 = (bf16[32,4096]{1,0:T(8,128)(2,1)S(1)}, bf16[32,4096]{1,0:T(8,128)(2,1)S(1)}, u32[]{:S(2)}, u32[]{:S(2)}) collective-permute-start(bf16[32,4096]{1,0:T(8,128)(2,1)S(1)} %pad_maximum_fusion.6.refs_1_), channel_id=1, source_target_pairs={{0,224},{8,232},{16,240},{24,248},{32,0},{40,8},{48,16},{56,24},{6... | collective-permute-start | bytes 786440 | tf_op jit(solution)/shard_map/ppermute | solution.py:30
  14.6 5.6 %collective-permute-done.2.refs_3_ = bf16[32,4096]{1,0:T(8,128)(2,1)S(1)} collective-permute-done((bf16[32,4096]{1,0:T(8,128)(2,1)S(1)}, bf16[32,4096]{1,0:T(8,128)(2,1)S(1)}, u32[]{:S(2)}, u32[]{:S(2)}) %collective-permute-start.2) | collective-permute-done | bytes 262176 | tf_op jit(solution)/shard_map/ppermute | solution.py:30
  20.2 2.7 %collective-permute-start.7 = (bf16[32,4096]{1,0:T(8,128)(2,1)S(1)}, bf16[32,4096]{1,0:T(8,128)(2,1)S(1)}, u32[]{:S(2)}, u32[]{:S(2)}) collective-permute-start(bf16[32,4096]{1,0:T(8,128)(2,1)S(1)} %collective-permute-done.3.refs_4_), channel_id=1, source_target_pairs={{0,224},{8,232},{16,240},{24,248},{32,0},{40,8},{48,16},{56,24},{6... | collective-permute-start | bytes 786440 | tf_op jit(solution)/shard_map/ppermute | solution.py:30
  27.6 2.7 %collective-permute-start.11 = (bf16[32,4096]{1,0:T(8,128)(2,1)S(1)}, bf16[32,4096]{1,0:T(8,128)(2,1)S(1)}, u32[]{:S(2)}, u32[]{:S(2)}) collective-permute-start(bf16[32,4096]{1,0:T(8,128)(2,1)S(1)} %collective-permute-done.7.refs_8_), channel_id=1, source_target_pairs={{0,224},{8,232},{16,240},{24,248},{32,0},{40,8},{48,16},{56,24},{6... | collective-permute-start | bytes 786440 | tf_op jit(solution)/shard_map/ppermute | solution.py:30
  30.3 6.2 %shard_map.59 = f32[8,144,256]{2,1,0:T(8,128)S(1)} custom-call(bf16[1024,4096]{1,0:T(8,128)(2,1)} %feats.3, bf16[32,4096]{1,0:T(8,128)(2,1)S(1)} %pad_maximum_fusion.6.refs_1_, bf16[32,4096]{1,0:T(8,128)(2,1)S(1)} %collective-permute-done.1.refs_2_, bf16[32,4096]{1,0:T(8,128)(2,1)S(1)} %collective-permute-done.2.refs_3_, ...), custom_call_target="tpu_custom_call" | custom-call | flops 2147483648 | bytes 11534336 | tf_op jit(solution)/shard_map/pallas_call | solution.py:91
  36.7 3.1 %collective-permute-start.8 = (bf16[32,4096]{1,0:T(8,128)(2,1)S(1)}, bf16[32,4096]{1,0:T(8,128)(2,1)S(1)}, u32[]{:S(2)}, u32[]{:S(2)}) collective-permute-start(bf16[32,4096]{1,0:T(8,128)(2,1)S(1)} %collective-permute-done.6.refs_7_), channel_id=1, source_target_pairs={{0,8},{8,0},{16,24},{24,16},{32,40},{40,32},{48,56},{56,48},{64,72... | collective-permute-start | bytes 786440 | tf_op jit(solution)/shard_map/ppermute | solution.py:30
  40.0 2.8 %collective-permute-start.15 = (bf16[32,2048]{1,0:T(8,128)(2,1)S(1)}, bf16[32,2048]{1,0:T(8,128)(2,1)S(1)}, u32[]{:S(2)}, u32[]{:S(2)}) collective-permute-start(bf16[32,2048]{1,0:T(8,128)(2,1)S(1)} %get-tuple-element.32), channel_id=1, source_target_pairs={{0,224},{8,232},{16,240},{24,248},{32,0},{40,8},{48,16},{56,24},{6... | collective-permute-start | bytes 393224 | tf_op jit(solution)/shard_map/ppermute | solution.py:30
  47.9 6.2 %shard_map.60 = f32[8,144,256]{2,1,0:T(8,128)S(1)} custom-call(bf16[1024,4096]{1,0:T(8,128)(2,1)} %feats.3, bf16[32,4096]{1,0:T(8,128)(2,1)S(1)} %collective-permute-done.8.refs_1_, bf16[32,4096]{1,0:T(8,128)(2,1)S(1)} %collective-permute-done.9.refs_2_, bf16[32,4096]{1,0:T(8,128)(2,1)S(1)} %collective-permute-done.10.refs_3_, ...), custom_call_target="tpu_custom_call" | custom-call | flops 2147483648 | bytes 11534336 | tf_op jit(solution)/shard_map/pallas_call | solution.py:91
  55.5 6.4 %all-to-all-start = ((f16[8,288,256]{2,1,0:T(8,128)(2,1)}), f16[8,288,256]{2,1,0:T(8,128)(2,1)S(1)}, u32[]{:S(2)}, u32[]{:S(2)}) async-start(f16[8,288,256]{2,1,0:T(8,128)(2,1)} %pad_maximum_fusion), calls=%async_computation | async-start | bytes 2359296 | tf_op jit(solution)/shard_map/all_to_all | solution.py:372
  62.7 16.9 %all-to-all-done = f16[8,288,256]{2,1,0:T(8,128)(2,1)S(1)} async-done(((f16[8,288,256]{2,1,0:T(8,128)(2,1)}), f16[8,288,256]{2,1,0:T(8,128)(2,1)S(1)}, u32[]{:S(2)}, u32[]{:S(2)}) %all-to-all-start) | async-done | bytes 1179680 | tf_op jit(solution)/shard_map/all_to_all | solution.py:372
  81.1 3.6 %all-to-all-start.1 = ((bf16[8,128,512]{2,1,0:T(8,128)(2,1)}), bf16[8,128,512]{2,1,0:T(8,128)(2,1)S(1)}, u32[]{:S(2)}, u32[]{:S(2)}) async-start(bf16[8,128,512]{2,1,0:T(8,128)(2,1)} %broadcast_in_dim.9), calls=%async_computation.1 | async-start | bytes 2097152 | tf_op jit(solution)/shard_map/all_to_all | solution.py:380
  88.9 11.4 %all-to-all-done.1 = bf16[8,128,512]{2,1,0:T(8,128)(2,1)S(1)} async-done(((bf16[8,128,512]{2,1,0:T(8,128)(2,1)}), bf16[8,128,512]{2,1,0:T(8,128)(2,1)S(1)}, u32[]{:S(2)}, u32[]{:S(2)}) %all-to-all-start.1) | async-done | bytes 1048608 | tf_op jit(solution)/shard_map/all_to_all | solution.py:380
  101.5 5.6 %shard_map.61 = (bf16[512,1024]{1,0:T(8,128)(2,1)S(1)}, f32[125,256]{1,0:T(8,128)S(1)}, f32[125,256]{1,0:T(8,128)S(1)}) custom-call(s32[2]{0:T(128)S(1)} %pad_add_fusion.scalars, bf16[1024,512]{1,0:T(8,128)(2,1)S(1)} %bitcast.77, s32[1024,1]{1,0:T(8,128)S(1)} %copy.6.column, s32[1,1024]{1,0:T(1,128)S(1)} %bitcast.79, ...), custom_call_target="tpu_custom_call" | custom-call | flops 2684354560 | bytes 5242880 | tf_op jit(solution)/shard_map/pallas_call | solution.py:141
  110.9 4.5 %shard_map.62 = (bf16[64,1536]{1,0:T(8,128)(2,1)S(1)}, bf16[64,1536]{1,0:T(8,128)(2,1)S(1)}, f32[64,512]{1,0:T(8,128)S(1)}, f32[64,2048]{1,0:T(8,128)S(1)}, f32[64,2048]{1,0:T(8,128)S(1)}) custom-call(s32[1]{0:T(128)} %bitcast.which_ref, bf16[512,1024]{1,0:T(8,128)(2,1)S(1)} %get-tuple-element.15.own, bf16[512,1024]{1,0:T(8,128)(2,1)S(1)} %collective-permute-done.17.other, ...), custom_call_target="tpu_custom_call" | custom-call | flops 1610612736 | bytes 9961472 | tf_op jit(solution)/shard_map/pallas_call | solution.py:197
  119.0 4.8 %collective-permute-done.20 = bf16[64,1536]{1,0:T(8,128)(2,1)S(1)} collective-permute-done((bf16[64,1536]{1,0:T(8,128)(2,1)S(1)}, bf16[64,1536]{1,0:T(8,128)(2,1)S(1)}, u32[]{:S(2)}, u32[]{:S(2)}) %collective-permute-start.20) | collective-permute-done | bytes 196640 | tf_op jit(solution)/shard_map/ppermute | solution.py:30
  124.1 2.9 %collective-permute-start.25 = (bf16[64,2560]{1,0:T(8,128)(2,1)S(1)}, bf16[64,2560]{1,0:T(8,128)(2,1)S(1)}, u32[]{:S(2)}, u32[]{:S(2)}) collective-permute-start(bf16[64,2560]{1,0:T(8,128)(2,1)S(1)} %pad_maximum_fusion.2.refs_1_), channel_id=1, source_target_pairs={{0,224},{8,232},{16,240},{24,248},{32,0},{40,8},{48,16},{56,24},{6... | collective-permute-start | bytes 983048 | tf_op jit(solution)/shard_map/ppermute | solution.py:30
  127.1 5.4 %shard_map.63 = (f32[64,2048]{1,0:T(8,128)S(1)}, f32[64,2048]{1,0:T(8,128)S(1)}, f32[64,2048]{1,0:T(8,128)S(1)}, f32[64,2048]{1,0:T(8,128)S(1)}, f32[64,2048]{1,0:T(8,128)S(1)}) custom-call(s32[1]{0:T(128)} %bitcast.which_ref, bf16[512,1024]{1,0:T(8,128)(2,1)S(1)} %get-tuple-element.15.own, bf16[512,1024]{1,0:T(8,128)(2,1)S(1)} %collective-permute-done.17.other, ...), custom_call_target="tpu_custom_call" | custom-call | flops 2684354560 | bytes 11010048 | tf_op jit(solution)/shard_map/pallas_call | solution.py:197
  133.9 2.7 %collective-permute-start.26 = (bf16[64,2560]{1,0:T(8,128)(2,1)S(1)}, bf16[64,2560]{1,0:T(8,128)(2,1)S(1)}, u32[]{:S(2)}, u32[]{:S(2)}) collective-permute-start(bf16[64,2560]{1,0:T(8,128)(2,1)S(1)} %pad_maximum_fusion.5), channel_id=1, source_target_pairs={{0,224},{8,232},{16,240},{24,248},{32,0},{40,8},{48,16},{56,24},{6... | collective-permute-start | bytes 983048 | tf_op jit(solution)/shard_map/ppermute | solution.py:30
  136.6 5.8 %collective-permute-done.23 = bf16[64,2560]{1,0:T(8,128)(2,1)S(1)} collective-permute-done((bf16[64,2560]{1,0:T(8,128)(2,1)S(1)}, bf16[64,2560]{1,0:T(8,128)(2,1)S(1)}, u32[]{:S(2)}, u32[]{:S(2)}) %collective-permute-start.23) | collective-permute-done | bytes 327712 | tf_op jit(solution)/shard_map/ppermute | solution.py:30
  142.6 2.7 %collective-permute-start.27 = (bf16[64,2048]{1,0:T(8,128)(2,1)S(1)}, bf16[64,2048]{1,0:T(8,128)(2,1)S(1)}, u32[]{:S(2)}, u32[]{:S(2)}) collective-permute-start(bf16[64,2048]{1,0:T(8,128)(2,1)S(1)} %add_convert_fusion), channel_id=1, source_target_pairs={{0,224},{8,232},{16,240},{24,248},{32,0},{40,8},{48,16},{56,24},{6... | collective-permute-start | bytes 786440 | tf_op jit(solution)/shard_map/ppermute | solution.py:30
  145.3 4.9 %collective-permute-done.24 = bf16[64,2560]{1,0:T(8,128)(2,1)S(1)} collective-permute-done((bf16[64,2560]{1,0:T(8,128)(2,1)S(1)}, bf16[64,2560]{1,0:T(8,128)(2,1)S(1)}, u32[]{:S(2)}, u32[]{:S(2)}) %collective-permute-start.24) | collective-permute-done | bytes 327712 | tf_op jit(solution)/shard_map/ppermute | solution.py:30
  150.6 4.5 %collective-permute-done.28 = bf16[32,3072]{1,0:T(8,128)(2,1)S(1)} collective-permute-done((bf16[32,3072]{1,0:T(8,128)(2,1)S(1)}, bf16[32,3072]{1,0:T(8,128)(2,1)S(1)}, u32[]{:S(2)}, u32[]{:S(2)}) %collective-permute-start.28) | collective-permute-done | bytes 196640 | tf_op jit(solution)/shard_map/ppermute | solution.py:30
  155.2 4.9 %collective-permute-start.30 = (f32[125,256]{1,0:T(8,128)S(1)}, f32[125,256]{1,0:T(8,128)S(1)}, u32[]{:S(2)}, u32[]{:S(2)}) collective-permute-start(f32[125,256]{1,0:T(8,128)S(1)} %pad_maximum_fusion.8), channel_id=1, source_target_pairs={{0,8},{8,0},{16,24},{24,16},{32,40},{40,32},{48,56},{56,48},{64,72... | collective-permute-start | bytes 384008 | tf_op jit(solution)/shard_map/ppermute | solution.py:30
  (119 shorter events, 36.0 us)
Async XLA Ops:
  0.6 8.1 %collective-permute-start = (bf16[16,4096]{1,0:T(8,128)(2,1)}, bf16[16,4096]{1,0:T(8,128)(2,1)S(1)}, u32[]{:S(2)}, u32[]{:S(2)}) collective-permute-start(bf16[16,4096]{1,0:T(8,128)(2,1)} %param.5), channel_id=1, source_target_pairs={{0,16},{8,24},{16,0},{24,8},{32,48},{40,56},{48,32},{56,40},{64,80... | collective-permute-start | bytes 393224 | tf_op jit(solution)/shard_map/ppermute | solution.py:30
  8.8 11.4 %collective-permute-start.2 = (bf16[32,4096]{1,0:T(8,128)(2,1)S(1)}, bf16[32,4096]{1,0:T(8,128)(2,1)S(1)}, u32[]{:S(2)}, u32[]{:S(2)}) collective-permute-start(bf16[32,4096]{1,0:T(8,128)(2,1)S(1)} %pad_maximum_fusion.6.refs_1_), channel_id=1, source_target_pairs={{0,32},{8,40},{16,48},{24,56},{32,64},{40,72},{48,80},{56,88},{64,... | collective-permute-start | bytes 786440 | tf_op jit(solution)/shard_map/ppermute | solution.py:30
  10.5 9.7 %collective-permute-start.3 = (bf16[32,4096]{1,0:T(8,128)(2,1)S(1)}, bf16[32,4096]{1,0:T(8,128)(2,1)S(1)}, u32[]{:S(2)}, u32[]{:S(2)}) collective-permute-start(bf16[32,4096]{1,0:T(8,128)(2,1)S(1)} %pad_maximum_fusion.6.refs_1_), channel_id=1, source_target_pairs={{0,224},{8,232},{16,240},{24,248},{32,0},{40,8},{48,16},{56,24},{6... | collective-permute-start | bytes 786440 | tf_op jit(solution)/shard_map/ppermute | solution.py:30
  20.2 7.5 %collective-permute-start.6 = (bf16[32,4096]{1,0:T(8,128)(2,1)S(1)}, bf16[32,4096]{1,0:T(8,128)(2,1)S(1)}, u32[]{:S(2)}, u32[]{:S(2)}) collective-permute-start(bf16[32,4096]{1,0:T(8,128)(2,1)S(1)} %collective-permute-done.2.refs_3_), channel_id=1, source_target_pairs={{0,32},{8,40},{16,48},{24,56},{32,64},{40,72},{48,80},{56,88},{64,... | collective-permute-start | bytes 786440 | tf_op jit(solution)/shard_map/ppermute | solution.py:30
  20.2 7.5 %collective-permute-start.7 = (bf16[32,4096]{1,0:T(8,128)(2,1)S(1)}, bf16[32,4096]{1,0:T(8,128)(2,1)S(1)}, u32[]{:S(2)}, u32[]{:S(2)}) collective-permute-start(bf16[32,4096]{1,0:T(8,128)(2,1)S(1)} %collective-permute-done.3.refs_4_), channel_id=1, source_target_pairs={{0,224},{8,232},{16,240},{24,248},{32,0},{40,8},{48,16},{56,24},{6... | collective-permute-start | bytes 786440 | tf_op jit(solution)/shard_map/ppermute | solution.py:30
  22.9 7.5 %collective-permute-start.1 = (bf16[32,4096]{1,0:T(8,128)(2,1)S(1)}, bf16[32,4096]{1,0:T(8,128)(2,1)S(1)}, u32[]{:S(2)}, u32[]{:S(2)}) collective-permute-start(bf16[32,4096]{1,0:T(8,128)(2,1)S(1)} %pad_maximum_fusion.6.refs_1_), channel_id=1, source_target_pairs={{0,8},{8,0},{16,24},{24,16},{32,40},{40,32},{48,56},{56,48},{64,72... | collective-permute-start | bytes 786440 | tf_op jit(solution)/shard_map/ppermute | solution.py:30
  27.6 9.0 %collective-permute-start.10 = (bf16[32,4096]{1,0:T(8,128)(2,1)S(1)}, bf16[32,4096]{1,0:T(8,128)(2,1)S(1)}, u32[]{:S(2)}, u32[]{:S(2)}) collective-permute-start(bf16[32,4096]{1,0:T(8,128)(2,1)S(1)} %collective-permute-done.6.refs_7_), channel_id=1, source_target_pairs={{0,32},{8,40},{16,48},{24,56},{32,64},{40,72},{48,80},{56,88},{64,... | collective-permute-start | bytes 786440 | tf_op jit(solution)/shard_map/ppermute | solution.py:30
  27.6 9.0 %collective-permute-start.11 = (bf16[32,4096]{1,0:T(8,128)(2,1)S(1)}, bf16[32,4096]{1,0:T(8,128)(2,1)S(1)}, u32[]{:S(2)}, u32[]{:S(2)}) collective-permute-start(bf16[32,4096]{1,0:T(8,128)(2,1)S(1)} %collective-permute-done.7.refs_8_), channel_id=1, source_target_pairs={{0,224},{8,232},{16,240},{24,248},{32,0},{40,8},{48,16},{56,24},{6... | collective-permute-start | bytes 786440 | tf_op jit(solution)/shard_map/ppermute | solution.py:30
  36.7 6.9 %collective-permute-start.14 = (bf16[32,2048]{1,0:T(8,128)(2,1)S(1)}, bf16[32,2048]{1,0:T(8,128)(2,1)S(1)}, u32[]{:S(2)}, u32[]{:S(2)}) collective-permute-start(bf16[32,2048]{1,0:T(8,128)(2,1)S(1)} %get-tuple-element.33), channel_id=1, source_target_pairs={{0,32},{8,40},{16,48},{24,56},{32,64},{40,72},{48,80},{56,88},{64,... | collective-permute-start | bytes 393224 | tf_op jit(solution)/shard_map/ppermute | solution.py:30
  36.7 10.1 %collective-permute-start.8 = (bf16[32,4096]{1,0:T(8,128)(2,1)S(1)}, bf16[32,4096]{1,0:T(8,128)(2,1)S(1)}, u32[]{:S(2)}, u32[]{:S(2)}) collective-permute-start(bf16[32,4096]{1,0:T(8,128)(2,1)S(1)} %collective-permute-done.6.refs_7_), channel_id=1, source_target_pairs={{0,8},{8,0},{16,24},{24,16},{32,40},{40,32},{48,56},{56,48},{64,72... | collective-permute-start | bytes 786440 | tf_op jit(solution)/shard_map/ppermute | solution.py:30
  39.9 7.1 %collective-permute-start.9 = (bf16[32,4096]{1,0:T(8,128)(2,1)S(1)}, bf16[32,4096]{1,0:T(8,128)(2,1)S(1)}, u32[]{:S(2)}, u32[]{:S(2)}) collective-permute-start(bf16[32,4096]{1,0:T(8,128)(2,1)S(1)} %collective-permute-done.7.refs_8_), channel_id=1, source_target_pairs={{0,8},{8,0},{16,24},{24,16},{32,40},{40,32},{48,56},{56,48},{64,72... | collective-permute-start | bytes 786440 | tf_op jit(solution)/shard_map/ppermute | solution.py:30
  40.0 6.0 %collective-permute-start.15 = (bf16[32,2048]{1,0:T(8,128)(2,1)S(1)}, bf16[32,2048]{1,0:T(8,128)(2,1)S(1)}, u32[]{:S(2)}, u32[]{:S(2)}) collective-permute-start(bf16[32,2048]{1,0:T(8,128)(2,1)S(1)} %get-tuple-element.32), channel_id=1, source_target_pairs={{0,224},{8,232},{16,240},{24,248},{32,0},{40,8},{48,16},{56,24},{6... | collective-permute-start | bytes 393224 | tf_op jit(solution)/shard_map/ppermute | solution.py:30
  46.8 64.0 %collective-permute-start.18 = (bf16[1024,2048]{1,0:T(8,128)(2,1)}, bf16[1024,2048]{1,0:T(8,128)(2,1)}, u32[]{:S(2)}, u32[]{:S(2)}) collective-permute-start(bf16[1024,2048]{1,0:T(8,128)(2,1)} %slice_select_fusion), channel_id=1, source_target_pairs={{0,8},{8,0},{16,24},{24,16},{32,40},{40,32},{48,56},{56,48},{64,72... | collective-permute-start | bytes 12582920 | tf_op jit(solution)/shard_map/ppermute | solution.py:30
  55.5 24.1 %all-to-all-start = ((f16[8,288,256]{2,1,0:T(8,128)(2,1)}), f16[8,288,256]{2,1,0:T(8,128)(2,1)S(1)}, u32[]{:S(2)}, u32[]{:S(2)}) async-start(f16[8,288,256]{2,1,0:T(8,128)(2,1)} %pad_maximum_fusion), calls=%async_computation | async-start | bytes 2359296 | tf_op jit(solution)/shard_map/all_to_all | solution.py:372
  81.1 19.2 %all-to-all-start.1 = ((bf16[8,128,512]{2,1,0:T(8,128)(2,1)}), bf16[8,128,512]{2,1,0:T(8,128)(2,1)S(1)}, u32[]{:S(2)}, u32[]{:S(2)}) async-start(bf16[8,128,512]{2,1,0:T(8,128)(2,1)} %broadcast_in_dim.9), calls=%async_computation.1 | async-start | bytes 2097152 | tf_op jit(solution)/shard_map/all_to_all | solution.py:380
  115.4 8.5 %collective-permute-start.20 = (bf16[64,1536]{1,0:T(8,128)(2,1)S(1)}, bf16[64,1536]{1,0:T(8,128)(2,1)S(1)}, u32[]{:S(2)}, u32[]{:S(2)}) collective-permute-start(bf16[64,1536]{1,0:T(8,128)(2,1)S(1)} %get-tuple-element.19), channel_id=1, source_target_pairs={{0,32},{8,40},{16,48},{24,56},{32,64},{40,72},{48,80},{56,88},{64,... | collective-permute-start | bytes 589832 | tf_op jit(solution)/shard_map/ppermute | solution.py:30
  116.4 7.6 %collective-permute-start.21 = (bf16[64,1536]{1,0:T(8,128)(2,1)S(1)}, bf16[64,1536]{1,0:T(8,128)(2,1)S(1)}, u32[]{:S(2)}, u32[]{:S(2)}) collective-permute-start(bf16[64,1536]{1,0:T(8,128)(2,1)S(1)} %get-tuple-element.21), channel_id=1, source_target_pairs={{0,224},{8,232},{16,240},{24,248},{32,0},{40,8},{48,16},{56,24},{6... | collective-permute-start | bytes 589832 | tf_op jit(solution)/shard_map/ppermute | solution.py:30
  123.9 9.6 %collective-permute-start.22 = (bf16[64,2560]{1,0:T(8,128)(2,1)S(1)}, bf16[64,2560]{1,0:T(8,128)(2,1)S(1)}, u32[]{:S(2)}, u32[]{:S(2)}) collective-permute-start(bf16[64,2560]{1,0:T(8,128)(2,1)S(1)} %pad_maximum_fusion.1.refs_0_), channel_id=1, source_target_pairs={{0,32},{8,40},{16,48},{24,56},{32,64},{40,72},{48,80},{56,88},{64,... | collective-permute-start | bytes 983048 | tf_op jit(solution)/shard_map/ppermute | solution.py:30
  124.1 9.6 %collective-permute-start.25 = (bf16[64,2560]{1,0:T(8,128)(2,1)S(1)}, bf16[64,2560]{1,0:T(8,128)(2,1)S(1)}, u32[]{:S(2)}, u32[]{:S(2)}) collective-permute-start(bf16[64,2560]{1,0:T(8,128)(2,1)S(1)} %pad_maximum_fusion.2.refs_1_), channel_id=1, source_target_pairs={{0,224},{8,232},{16,240},{24,248},{32,0},{40,8},{48,16},{56,24},{6... | collective-permute-start | bytes 983048 | tf_op jit(solution)/shard_map/ppermute | solution.py:30
  133.7 8.7 %collective-permute-start.23 = (bf16[64,2560]{1,0:T(8,128)(2,1)S(1)}, bf16[64,2560]{1,0:T(8,128)(2,1)S(1)}, u32[]{:S(2)}, u32[]{:S(2)}) collective-permute-start(bf16[64,2560]{1,0:T(8,128)(2,1)S(1)} %pad_maximum_fusion.3), channel_id=1, source_target_pairs={{0,32},{8,40},{16,48},{24,56},{32,64},{40,72},{48,80},{56,88},{64,... | collective-permute-start | bytes 983048 | tf_op jit(solution)/shard_map/ppermute | solution.py:30
  133.9 8.7 %collective-permute-start.26 = (bf16[64,2560]{1,0:T(8,128)(2,1)S(1)}, bf16[64,2560]{1,0:T(8,128)(2,1)S(1)}, u32[]{:S(2)}, u32[]{:S(2)}) collective-permute-start(bf16[64,2560]{1,0:T(8,128)(2,1)S(1)} %pad_maximum_fusion.5), channel_id=1, source_target_pairs={{0,224},{8,232},{16,240},{24,248},{32,0},{40,8},{48,16},{56,24},{6... | collective-permute-start | bytes 983048 | tf_op jit(solution)/shard_map/ppermute | solution.py:30
  142.4 7.8 %collective-permute-start.24 = (bf16[64,2560]{1,0:T(8,128)(2,1)S(1)}, bf16[64,2560]{1,0:T(8,128)(2,1)S(1)}, u32[]{:S(2)}, u32[]{:S(2)}) collective-permute-start(bf16[64,2560]{1,0:T(8,128)(2,1)S(1)} %pad_maximum_fusion.4), channel_id=1, source_target_pairs={{0,32},{8,40},{16,48},{24,56},{32,64},{40,72},{48,80},{56,88},{64,... | collective-permute-start | bytes 983048 | tf_op jit(solution)/shard_map/ppermute | solution.py:30
  142.6 7.7 %collective-permute-start.27 = (bf16[64,2048]{1,0:T(8,128)(2,1)S(1)}, bf16[64,2048]{1,0:T(8,128)(2,1)S(1)}, u32[]{:S(2)}, u32[]{:S(2)}) collective-permute-start(bf16[64,2048]{1,0:T(8,128)(2,1)S(1)} %add_convert_fusion), channel_id=1, source_target_pairs={{0,224},{8,232},{16,240},{24,248},{32,0},{40,8},{48,16},{56,24},{6... | collective-permute-start | bytes 786440 | tf_op jit(solution)/shard_map/ppermute | solution.py:30
  155.2 5.8 %collective-permute-start.30 = (f32[125,256]{1,0:T(8,128)S(1)}, f32[125,256]{1,0:T(8,128)S(1)}, u32[]{:S(2)}, u32[]{:S(2)}) collective-permute-start(f32[125,256]{1,0:T(8,128)S(1)} %pad_maximum_fusion.8), channel_id=1, source_target_pairs={{0,8},{8,0},{16,24},{24,16},{32,40},{40,32},{48,56},{56,48},{64,72... | collective-permute-start | bytes 384008 | tf_op jit(solution)/shard_map/ppermute | solution.py:30
  (13 other events, 49.4 us)

commit v6 on v5

--- a/solution.py
+++ b/solution.py
@@ -101,62 +101,93 @@
     )(target_feats, *pieces)
 
 
-def gradients(kernel_low, labels, coefs_here, coefs_ring, own_coefs, order, first_class, core):
+def gradients(kernel_low, labels, coefs_here, coefs_ring, earlier):
     targets, supports = kernel_low.shape
     padded = coefs_here.shape[0]
-    own = own_coefs.shape[0]
-    half = supports // 2
     tile = 256
     steps = targets // tile
 
-    def body(scalars, low, column, row, here, ring, mine, order_ref, grad, keep, give, part):
+    def body(low_ref, column, here, ring, earlier_ref, grad, low, sem):
         step = pl.program_id(0)
-        predict = lax.dot_general(low[...], here[...], NT, preferred_element_type=FULL)
+        loads = [
+            pltpu.make_async_copy(low_ref.at[pl.ds(j * tile, tile)], low.at[pl.ds(j * tile, tile)], sem.at[j])
+            for j in range(steps)
+        ]
+
+        @pl.when(step == 0)
+        def _():
+            for load in loads:
+                load.start()
+
+        for j in range(steps):
+
+            @pl.when(step == j)
+            def _():
+                loads[j].wait()
+
+        some = low[pl.ds(pl.multiple_of(step * tile, tile), tile), :]
+        predict = lax.dot_general(some, here[...], NT, preferred_element_type=FULL)
         ids = lax.broadcasted_iota(jnp.int32, (tile, padded), 1)
         residual = jnp.where(ids == column[...], predict - 1.0, predict).astype(LOW)
         grad[...] = lax.dot_general(ring[...], residual, NT, preferred_element_type=FULL).astype(LOW)
+
+    whole = lambda i: (0, 0)
+    return call(
+        body,
+        jax.ShapeDtypeStruct((supports, targets), LOW),
+        (steps,),
+        [
+            pl.BlockSpec(memory_space=pltpu.HBM),
+            pl.BlockSpec((tile, 1), lambda i: (i, 0)),
+            pl.BlockSpec((padded, supports), whole),
+            pl.BlockSpec((supports, padded), whole),
+            pl.BlockSpec(memory_space=pl.ANY),
+        ],
+        pl.BlockSpec((supports, tile), lambda i: (0, i)),
+        4 * targets * supports * padded,
+        4 * supports * (targets + padded),
+        [pltpu.VMEM((targets, supports), LOW), pltpu.SemaphoreType.DMA((steps,))],
+    )(kernel_low, labels[:, None], coefs_here, coefs_ring, earlier)
+
+
+def coef_part(kernel_low, labels, own_coefs, order, first_class, core, earlier):
+    targets, supports = kernel_low.shape
+    own = own_coefs.shape[0]
+    half = supports // 2
+
+    def body(scalars, low_ref, row, mine, order_ref, earlier_ref, keep, give, low, sem):
+        load = pltpu.make_async_copy(low_ref, low, sem)
+        load.start()
+        load.wait()
         predict = lax.dot_general(mine[...], low[...], NT, preferred_element_type=FULL)
-        ids = lax.broadcasted_iota(jnp.int32, (own, tile), 0) + scalars[0]
+        ids = lax.broadcasted_iota(jnp.int32, (own, targets), 0) + scalars[0]
         residual = jnp.where(ids == row[...], predict - 1.0, predict).astype(LOW)
         ordered = jnp.dot(low[...], order_ref[...], preferred_element_type=FULL).astype(LOW)
-        product = jnp.dot(residual, ordered, preferred_element_type=FULL)
-
-        @pl.when(step == 0)
-        def _():
-            part[...] = product
-
-        @pl.when(step > 0)
-        def _():
-            part[...] += product
-
-        @pl.when(step == steps - 1)
-        def _():
-            left, right = part[:, :half], part[:, half:]
-            first = scalars[1] == 0
-            keep[...] = jnp.where(first, left, right)
-            give[...] = jnp.where(first, right, left)
+        part = jnp.dot(residual, ordered, preferred_element_type=FULL)
+        left, right = part[:, :half], part[:, half:]
+        first = scalars[1] == 0
+        keep[...] = jnp.where(first, left, right)
+        give[...] = jnp.where(first, right, left)
 
     whole = lambda i, f: (0, 0)
     piece = jax.ShapeDtypeStruct((own, half), FULL)
     return call(
         body,
-        (jax.ShapeDtypeStruct((supports, targets), LOW), piece, piece),
-        (steps,),
+        (piece, piece),
+        (1,),
         [
-            pl.BlockSpec((tile, supports), lambda i, f: (i, 0)),
-            pl.BlockSpec((tile, 1), lambda i, f: (i, 0)),
-            pl.BlockSpec((1, tile), lambda i, f: (0, i)),
-            pl.BlockSpec((padded, supports), whole),
-            pl.BlockSpec((supports, padded), whole),
+            pl.BlockSpec(memory_space=pltpu.HBM),
+            pl.BlockSpec((1, targets), whole),
             pl.BlockSpec((own, supports), whole),
             pl.BlockSpec((supports, supports), whole),
+            pl.BlockSpec(memory_space=pl.ANY),
         ],
-        (pl.BlockSpec((supports, tile), lambda i, f: (0, i)),) + (pl.BlockSpec((own, half), whole),) * 2,
-        2 * targets * supports * (2 * padded + supports),
-        2 * supports * (2 * targets + 3 * padded),
-        [pltpu.VMEM((own, supports), FULL)],
+        (pl.BlockSpec((own, half), whole),) * 2,
+        2 * targets * supports * (supports + 2 * own),
+        4 * supports * targets,
+        [pltpu.VMEM((targets, supports), LOW), pltpu.SemaphoreType.DMA],
         prefetch=1,
-    )(jnp.stack([first_class, core]), kernel_low, labels[:, None], labels[None, :], coefs_here, coefs_ring, own_coefs, order)
+    )(jnp.stack([first_class, core]), kernel_low, labels[None, :], own_coefs, order, earlier)
 
 
 def support_call(body, outs, factors, start, count, extra, extra_specs, chip_rows):
@@ -212,14 +243,11 @@
     )(which, own_grad, other_grad, target_feats, taken, *extra)
 
 
-def support_first(factors, coef, other_coef, chip_rows):
+def support_first(factors, chip_rows, earlier):
     half = factors[3].shape[1]
     edge = half // 2
-    classes, columns = coef.shape
-    rest = classes - chip_rows
-    fold = 2 * columns
-
-    def body(j, product, coef_ref, other_ref, up, down, folded, above, below):
+
+    def body(j, product, earlier_ref, up, down, above, below):
         here = slice(j * SUPPORT_TILE, (j + 1) * SUPPORT_TILE)
         above[:, here] = product[chip_rows : 2 * chip_rows]
         below[:, here] = product[2 * chip_rows :]
@@ -228,19 +256,11 @@
             up[:, here] = far
         else:
             down[:, here.start - edge : here.stop - edge] = far
-        if j == 0:
-            total = coef_ref[...] + other_ref[...]
-            lower = jnp.concatenate([total[chip_rows:], jnp.zeros((chip_rows - rest, columns), FULL)], 0)
-            total = jnp.concatenate([total[:chip_rows], lower], 1)
-            folded[...] = total
-            up[:, edge:] = total.astype(LOW)
-            down[:, edge:] = total.astype(LOW)
-
-    first = jax.ShapeDtypeStruct((chip_rows, edge + fold), LOW)
+
+    first = jax.ShapeDtypeStruct((chip_rows, edge), LOW)
     block = jax.ShapeDtypeStruct((chip_rows, half), FULL)
-    outs = (first, first, jax.ShapeDtypeStruct((chip_rows, fold), FULL), block, block)
-    extra_specs = [pl.BlockSpec(coef.shape, lambda i, w: (0, 0))] * 2
-    return support_call(body, outs, factors, 0, 3, [coef, other_coef], extra_specs, chip_rows)
+    outs = (first, first, block, block)
+    return support_call(body, outs, factors, 0, 3, [earlier], [pl.BlockSpec(memory_space=pl.ANY)], chip_rows)
 
 
 def support_rest(factors, chip_rows, earlier):
@@ -271,15 +291,17 @@
     return jnp.where(which == 0, jnp.concatenate([mine, other], 1), jnp.concatenate([other, mine], 1))
 
 
-def sums(factors, coef, other_coef, rows):
+def sums(factors, keep, give, rows):
     z, y, c = place()
     chip_rows = rows * PAIR * CORES
-    classes = coef.shape[0]
-    up, down, total, above, below = support_first(factors, coef, other_coef, chip_rows)
+    classes, columns = keep.shape
+    up, down, above, below = support_first(factors, chip_rows, give)
+    total = jnp.pad(keep + tgt_move(give, 0, 0, 1), ((0, 2 * chip_rows - classes), (0, 0)))
+    total = jnp.concatenate([total[:chip_rows], total[chip_rows:]], 1)
+    up, down = jnp.concatenate([up, total.astype(LOW)], 1), jnp.concatenate([down, total.astype(LOW)], 1)
     part = {FAR - 1: above, 1 - FAR: below}
     wide = above.shape[1]
     half = wide // 2
-    columns = total.shape[1] // 2
     for step in range(FAR, 0, -1):
         if step == FAR - 1:
             part.update(zip(RING[3:], support_rest(factors, chip_rows, (up, down))))
@@ -379,10 +401,11 @@
     spread = jnp.broadcast_to(own_low[None], (blks,) + own_low.shape)
     kernel_low = lax.all_to_all(spread, "blk", 0, 0, tiled=True).reshape(targets, -1)
 
-    kernel_grad, keep, give = gradients(kernel_low, labels, coefs_here, coefs_ring, own_coefs, order, first_class, c)
-    other_grad, other_coef = tgt_move(kernel_grad, 0, 0, 1), tgt_move(give, 0, 0, 1)
+    kernel_grad = gradients(kernel_low, labels, coefs_here, coefs_ring, own_coefs)
+    other_grad = tgt_move(kernel_grad, 0, 0, 1)
+    keep, give = coef_part(kernel_low, labels, own_coefs, order, first_class, c, kernel_grad)
     factors = (kernel_grad, other_grad, target_feats, taken, c[None])
-    support_grad, coef_grad = sums(factors, keep, other_coef, rows)
+    support_grad, coef_grad = sums(factors, keep, give, rows)
     return support_grad * scale, coef_grad / math.sqrt(targets * tgts)
 
 

time: 163 us -> 163 us (level)
    pallas_call x1 -> x2, Pallas kernels: 5.65 us -> 5.52 us  [the longest x1 3.72 us: gradients(): call(body, jax.ShapeDtypeStruct((supports, targets), LOW), (steps,), [pl....]
  transfers between devices with their start and end apart: 33 -> 33, of which waited for: 13 -> 13; matrix products, arithmetic and copies ran while one was open for 9% -> 10% of each run, Pallas kernels for 14% -> 14%
where the time goes in v6:
time: 163 us; the launch traced here: 162 us
  waiting for transfers between devices  60.1 us (37%)
  starting transfers between devices  54.5 us (33%)
  Pallas kernels  27.8 us (17%)
  other arithmetic  10.4 us (6%)
  matrix products  5.04 us (3%)
  local copies, waits for them, and re-layouts  3.15 us (2%)
    ppermute x31, starting transfers between devices, tgt_move(): return lax.ppermute(array, 'tgt', pairs)  44.6 us
    ppermute x31, waiting for transfers between devices, tgt_move(): return lax.ppermute(array, 'tgt', pairs)  32.7 us
    all_to_all x1, waiting for transfers between devices, shards(): got = lax.all_to_all(part, 'blk', 0, 0, tiled=True).astype(FULL)  17.4 us
    pallas_call x2, Pallas kernels, kernel_part(): call(body, jax.ShapeDtypeStruct((blks, block + 16, rows), FULL), (steps,)...  12.4 us
    all_to_all x1, waiting for transfers between devices, shards(): lax.all_to_all(spread, 'blk', 0, 0, tiled=True).reshape(targets, -1)  9.98 us
    pallas_call x2, Pallas kernels, support_call(): call(kernel, outs, (1,), [pl.BlockSpec(memory_space=pltpu.HBM)] * 4 + ext...  9.92 us
    all_to_all x1, starting transfers between devices, shards(): got = lax.all_to_all(part, 'blk', 0, 0, tiled=True).astype(FULL)  6.36 us
    select_n x1, other arithmetic, split(): jnp.where(which == 0, right, left)  5.07 us
  transfers between devices with their start and end apart: 33, of which 13 were waited for; matrix products, arithmetic and copies ran while one was open for 10% of the time, Pallas kernels for 14%

profile of v6, /device:TPU:1, one launch (start us, length us, event | category | flops | bytes accessed | tf_op | source)
XLA Modules:
  0.0 162.1 jit_solution(13644089399462909220)
XLA Ops:
  2.8 5.1 %slice_select_fusion = bf16[1024,2048]{1,0:T(8,128)(2,1)} fusion(bf16[1024,4096]{1,0:T(8,128)(2,1)} %feats.3, pred[]{:T(512)S(6)} %eq.197), kind=kLoop, calls=%fused_computation | loop fusion | flops 2097152 | bytes 12582913 | tf_op jit(solution)/shard_map/jit(_where)/select_n | solution.py:287
  10.5 4.0 %collective-permute-start.3 = (bf16[32,4096]{1,0:T(8,128)(2,1)S(1)}, bf16[32,4096]{1,0:T(8,128)(2,1)S(1)}, u32[]{:S(2)}, u32[]{:S(2)}) collective-permute-start(bf16[32,4096]{1,0:T(8,128)(2,1)S(1)} %pad_maximum_fusion.6.refs_1_), channel_id=1, source_target_pairs={{0,224},{8,232},{16,240},{24,248},{32,0},{40,8},{48,16},{56,24},{6... | collective-permute-start | bytes 786440 | tf_op jit(solution)/shard_map/ppermute | solution.py:30
  14.5 5.6 %collective-permute-done.2.refs_3_ = bf16[32,4096]{1,0:T(8,128)(2,1)S(1)} collective-permute-done((bf16[32,4096]{1,0:T(8,128)(2,1)S(1)}, bf16[32,4096]{1,0:T(8,128)(2,1)S(1)}, u32[]{:S(2)}, u32[]{:S(2)}) %collective-permute-start.2) | collective-permute-done | bytes 262176 | tf_op jit(solution)/shard_map/ppermute | solution.py:30
  20.2 2.7 %collective-permute-start.7 = (bf16[32,4096]{1,0:T(8,128)(2,1)S(1)}, bf16[32,4096]{1,0:T(8,128)(2,1)S(1)}, u32[]{:S(2)}, u32[]{:S(2)}) collective-permute-start(bf16[32,4096]{1,0:T(8,128)(2,1)S(1)} %collective-permute-done.3.refs_4_), channel_id=1, source_target_pairs={{0,224},{8,232},{16,240},{24,248},{32,0},{40,8},{48,16},{56,24},{6... | collective-permute-start | bytes 786440 | tf_op jit(solution)/shard_map/ppermute | solution.py:30
  30.3 6.2 %shard_map.59 = f32[8,144,256]{2,1,0:T(8,128)S(1)} custom-call(bf16[1024,4096]{1,0:T(8,128)(2,1)} %feats.3, bf16[32,4096]{1,0:T(8,128)(2,1)S(1)} %pad_maximum_fusion.6.refs_1_, bf16[32,4096]{1,0:T(8,128)(2,1)S(1)} %collective-permute-done.1.refs_2_, bf16[32,4096]{1,0:T(8,128)(2,1)S(1)} %collective-permute-done.2.refs_3_, ...), custom_call_target="tpu_custom_call" | custom-call | flops 2147483648 | bytes 11534336 | tf_op jit(solution)/shard_map/pallas_call | solution.py:91
  36.8 3.1 %collective-permute-start.8 = (bf16[32,4096]{1,0:T(8,128)(2,1)S(1)}, bf16[32,4096]{1,0:T(8,128)(2,1)S(1)}, u32[]{:S(2)}, u32[]{:S(2)}) collective-permute-start(bf16[32,4096]{1,0:T(8,128)(2,1)S(1)} %collective-permute-done.6.refs_7_), channel_id=1, source_target_pairs={{0,8},{8,0},{16,24},{24,16},{32,40},{40,32},{48,56},{56,48},{64,72... | collective-permute-start | bytes 786440 | tf_op jit(solution)/shard_map/ppermute | solution.py:30
  40.0 2.8 %collective-permute-start.15 = (bf16[32,2048]{1,0:T(8,128)(2,1)S(1)}, bf16[32,2048]{1,0:T(8,128)(2,1)S(1)}, u32[]{:S(2)}, u32[]{:S(2)}) collective-permute-start(bf16[32,2048]{1,0:T(8,128)(2,1)S(1)} %get-tuple-element.28), channel_id=1, source_target_pairs={{0,224},{8,232},{16,240},{24,248},{32,0},{40,8},{48,16},{56,24},{6... | collective-permute-start | bytes 393224 | tf_op jit(solution)/shard_map/ppermute | solution.py:30
  47.9 6.2 %shard_map.60 = f32[8,144,256]{2,1,0:T(8,128)S(1)} custom-call(bf16[1024,4096]{1,0:T(8,128)(2,1)} %feats.3, bf16[32,4096]{1,0:T(8,128)(2,1)S(1)} %collective-permute-done.8.refs_1_, bf16[32,4096]{1,0:T(8,128)(2,1)S(1)} %collective-permute-done.9.refs_2_, bf16[32,4096]{1,0:T(8,128)(2,1)S(1)} %collective-permute-done.10.refs_3_, ...), custom_call_target="tpu_custom_call" | custom-call | flops 2147483648 | bytes 11534336 | tf_op jit(solution)/shard_map/pallas_call | solution.py:91
  55.4 6.4 %all-to-all-start = ((f16[8,288,256]{2,1,0:T(8,128)(2,1)}), f16[8,288,256]{2,1,0:T(8,128)(2,1)S(1)}, u32[]{:S(2)}, u32[]{:S(2)}) async-start(f16[8,288,256]{2,1,0:T(8,128)(2,1)} %pad_maximum_fusion), calls=%async_computation | async-start | bytes 2359296 | tf_op jit(solution)/shard_map/all_to_all | solution.py:394
  62.1 17.4 %all-to-all-done = f16[8,288,256]{2,1,0:T(8,128)(2,1)S(1)} async-done(((f16[8,288,256]{2,1,0:T(8,128)(2,1)}), f16[8,288,256]{2,1,0:T(8,128)(2,1)S(1)}, u32[]{:S(2)}, u32[]{:S(2)}) %all-to-all-start) | async-done | bytes 1179680 | tf_op jit(solution)/shard_map/all_to_all | solution.py:394
  81.0 3.6 %all-to-all-start.1 = ((bf16[8,128,512]{2,1,0:T(8,128)(2,1)}), bf16[8,128,512]{2,1,0:T(8,128)(2,1)S(1)}, u32[]{:S(2)}, u32[]{:S(2)}) async-start(bf16[8,128,512]{2,1,0:T(8,128)(2,1)} %broadcast_in_dim.9), calls=%async_computation.1 | async-start | bytes 2097152 | tf_op jit(solution)/shard_map/all_to_all | solution.py:402
  87.2 2.9 %convolution_convert_fusion.ring = bf16[512,1024]{1,0:T(8,128)(2,1)} fusion(bf16[1000,512]{1,0:T(8,128)(2,1)} %param.6, s32[512]{0:T(512)S(1)} %add.773), kind=kOutput, calls=%fused_computation.1 | convolution fusion | flops 537657344 | bytes 2074624 | tf_op jit(solution)/shard_map/dot_general | solution.py:43
  90.2 10.0 %all-to-all-done.1 = bf16[8,128,512]{2,1,0:T(8,128)(2,1)S(1)} async-done(((bf16[8,128,512]{2,1,0:T(8,128)(2,1)}), bf16[8,128,512]{2,1,0:T(8,128)(2,1)S(1)}, u32[]{:S(2)}, u32[]{:S(2)}) %all-to-all-start.1) | async-done | bytes 1048608 | tf_op jit(solution)/shard_map/all_to_all | solution.py:402
  101.4 3.7 %shard_map.61.earlier_ref.own = bf16[512,1024]{1,0:T(8,128)(2,1)S(1)} custom-call(bf16[1024,512]{1,0:T(8,128)(2,1)S(1)} %bitcast.77, s32[1024,1]{1,0:T(8,128)S(1)} %copy.6.column, bf16[1024,512]{1,0:T(8,128)(2,1)S(1)} %convolution_convert_fusion.1.here, bf16[512,1024]{1,0:T(8,128)(2,1)S(1)} %copy-done.1, ...), custom_call_target="tpu_custom_call" | custom-call | flops 2147483648 | bytes 4194304 | tf_op jit(solution)/shard_map/pallas_call | solution.py:135
  110.0 4.5 %shard_map.63 = (bf16[64,1024]{1,0:T(8,128)(2,1)S(1)}, bf16[64,1024]{1,0:T(8,128)(2,1)S(1)}, f32[64,2048]{1,0:T(8,128)S(1)}, f32[64,2048]{1,0:T(8,128)S(1)}) custom-call(s32[1]{0:T(128)} %bitcast.which_ref, bf16[512,1024]{1,0:T(8,128)(2,1)S(1)} %shard_map.61.earlier_ref.own, bf16[512,1024]{1,0:T(8,128)(2,1)S(1)} %collective-permute-done.17.other, ...), custom_call_target="tpu_custom_call" | custom-call | flops 1610612736 | bytes 9961472 | tf_op jit(solution)/shard_map/pallas_call | solution.py:228
  118.1 5.0 %collective-permute-done.20 = bf16[64,1536]{1,0:T(8,128)(2,1)S(1)} collective-permute-done((bf16[64,1536]{1,0:T(8,128)(2,1)S(1)}, bf16[64,1536]{1,0:T(8,128)(2,1)S(1)}, u32[]{:S(2)}, u32[]{:S(2)}) %collective-permute-start.20) | collective-permute-done | bytes 196640 | tf_op jit(solution)/shard_map/ppermute | solution.py:30
  123.4 3.0 %collective-permute-start.25 = (bf16[64,2560]{1,0:T(8,128)(2,1)S(1)}, bf16[64,2560]{1,0:T(8,128)(2,1)S(1)}, u32[]{:S(2)}, u32[]{:S(2)}) collective-permute-start(bf16[64,2560]{1,0:T(8,128)(2,1)S(1)} %pad_maximum_fusion.2.refs_1_), channel_id=1, source_target_pairs={{0,224},{8,232},{16,240},{24,248},{32,0},{40,8},{48,16},{56,24},{6... | collective-permute-start | bytes 983048 | tf_op jit(solution)/shard_map/ppermute | solution.py:30
  126.4 5.4 %shard_map.64 = (f32[64,2048]{1,0:T(8,128)S(1)}, f32[64,2048]{1,0:T(8,128)S(1)}, f32[64,2048]{1,0:T(8,128)S(1)}, f32[64,2048]{1,0:T(8,128)S(1)}, f32[64,2048]{1,0:T(8,128)S(1)}) custom-call(s32[1]{0:T(128)} %bitcast.which_ref, bf16[512,1024]{1,0:T(8,128)(2,1)S(1)} %shard_map.61.earlier_ref.own, bf16[512,1024]{1,0:T(8,128)(2,1)S(1)} %collective-permute-done.17.other, ...), custom_call_target="tpu_custom_call" | custom-call | flops 2684354560 | bytes 11010048 | tf_op jit(solution)/shard_map/pallas_call | solution.py:228
  133.4 2.7 %collective-permute-start.26 = (bf16[64,2560]{1,0:T(8,128)(2,1)S(1)}, bf16[64,2560]{1,0:T(8,128)(2,1)S(1)}, u32[]{:S(2)}, u32[]{:S(2)}) collective-permute-start(bf16[64,2560]{1,0:T(8,128)(2,1)S(1)} %pad_maximum_fusion.5), channel_id=1, source_target_pairs={{0,224},{8,232},{16,240},{24,248},{32,0},{40,8},{48,16},{56,24},{6... | collective-permute-start | bytes 983048 | tf_op jit(solution)/shard_map/ppermute | solution.py:30
  136.1 5.9 %collective-permute-done.23 = bf16[64,2560]{1,0:T(8,128)(2,1)S(1)} collective-permute-done((bf16[64,2560]{1,0:T(8,128)(2,1)S(1)}, bf16[64,2560]{1,0:T(8,128)(2,1)S(1)}, u32[]{:S(2)}, u32[]{:S(2)}) %collective-permute-start.23) | collective-permute-done | bytes 327712 | tf_op jit(solution)/shard_map/ppermute | solution.py:30
  142.3 2.7 %collective-permute-start.27 = (bf16[64,2048]{1,0:T(8,128)(2,1)S(1)}, bf16[64,2048]{1,0:T(8,128)(2,1)S(1)}, u32[]{:S(2)}, u32[]{:S(2)}) collective-permute-start(bf16[64,2048]{1,0:T(8,128)(2,1)S(1)} %add_convert_fusion), channel_id=1, source_target_pairs={{0,224},{8,232},{16,240},{24,248},{32,0},{40,8},{48,16},{56,24},{6... | collective-permute-start | bytes 786440 | tf_op jit(solution)/shard_map/ppermute | solution.py:30
  145.0 5.1 %collective-permute-done.24 = bf16[64,2560]{1,0:T(8,128)(2,1)S(1)} collective-permute-done((bf16[64,2560]{1,0:T(8,128)(2,1)S(1)}, bf16[64,2560]{1,0:T(8,128)(2,1)S(1)}, u32[]{:S(2)}, u32[]{:S(2)}) %collective-permute-start.24) | collective-permute-done | bytes 327712 | tf_op jit(solution)/shard_map/ppermute | solution.py:30
  150.4 4.5 %collective-permute-done.28 = bf16[32,3072]{1,0:T(8,128)(2,1)S(1)} collective-permute-done((bf16[32,3072]{1,0:T(8,128)(2,1)S(1)}, bf16[32,3072]{1,0:T(8,128)(2,1)S(1)}, u32[]{:S(2)}, u32[]{:S(2)}) %collective-permute-start.28) | collective-permute-done | bytes 196640 | tf_op jit(solution)/shard_map/ppermute | solution.py:30
  155.0 4.7 %collective-permute-start.30 = (f32[125,256]{1,0:T(8,128)S(1)}, f32[125,256]{1,0:T(8,128)S(1)}, u32[]{:S(2)}, u32[]{:S(2)}) collective-permute-start(f32[125,256]{1,0:T(8,128)S(1)} %pad_maximum_fusion.10), channel_id=1, source_target_pairs={{0,8},{8,0},{16,24},{24,16},{32,40},{40,32},{48,56},{56,48},{64,72... | collective-permute-start | bytes 384008 | tf_op jit(solution)/shard_map/ppermute | solution.py:30
  (122 shorter events, 37.8 us)
Async XLA Ops:
  0.6 8.1 %collective-permute-start = (bf16[16,4096]{1,0:T(8,128)(2,1)}, bf16[16,4096]{1,0:T(8,128)(2,1)S(1)}, u32[]{:S(2)}, u32[]{:S(2)}) collective-permute-start(bf16[16,4096]{1,0:T(8,128)(2,1)} %param.5), channel_id=1, source_target_pairs={{0,16},{8,24},{16,0},{24,8},{32,48},{40,56},{48,32},{56,40},{64,80... | collective-permute-start | bytes 393224 | tf_op jit(solution)/shard_map/ppermute | solution.py:30
  8.8 11.4 %collective-permute-start.2 = (bf16[32,4096]{1,0:T(8,128)(2,1)S(1)}, bf16[32,4096]{1,0:T(8,128)(2,1)S(1)}, u32[]{:S(2)}, u32[]{:S(2)}) collective-permute-start(bf16[32,4096]{1,0:T(8,128)(2,1)S(1)} %pad_maximum_fusion.6.refs_1_), channel_id=1, source_target_pairs={{0,32},{8,40},{16,48},{24,56},{32,64},{40,72},{48,80},{56,88},{64,... | collective-permute-start | bytes 786440 | tf_op jit(solution)/shard_map/ppermute | solution.py:30
  10.5 9.7 %collective-permute-start.3 = (bf16[32,4096]{1,0:T(8,128)(2,1)S(1)}, bf16[32,4096]{1,0:T(8,128)(2,1)S(1)}, u32[]{:S(2)}, u32[]{:S(2)}) collective-permute-start(bf16[32,4096]{1,0:T(8,128)(2,1)S(1)} %pad_maximum_fusion.6.refs_1_), channel_id=1, source_target_pairs={{0,224},{8,232},{16,240},{24,248},{32,0},{40,8},{48,16},{56,24},{6... | collective-permute-start | bytes 786440 | tf_op jit(solution)/shard_map/ppermute | solution.py:30
  20.2 7.5 %collective-permute-start.6 = (bf16[32,4096]{1,0:T(8,128)(2,1)S(1)}, bf16[32,4096]{1,0:T(8,128)(2,1)S(1)}, u32[]{:S(2)}, u32[]{:S(2)}) collective-permute-start(bf16[32,4096]{1,0:T(8,128)(2,1)S(1)} %collective-permute-done.2.refs_3_), channel_id=1, source_target_pairs={{0,32},{8,40},{16,48},{24,56},{32,64},{40,72},{48,80},{56,88},{64,... | collective-permute-start | bytes 786440 | tf_op jit(solution)/shard_map/ppermute | solution.py:30
  20.2 7.5 %collective-permute-start.7 = (bf16[32,4096]{1,0:T(8,128)(2,1)S(1)}, bf16[32,4096]{1,0:T(8,128)(2,1)S(1)}, u32[]{:S(2)}, u32[]{:S(2)}) collective-permute-start(bf16[32,4096]{1,0:T(8,128)(2,1)S(1)} %collective-permute-done.3.refs_4_), channel_id=1, source_target_pairs={{0,224},{8,232},{16,240},{24,248},{32,0},{40,8},{48,16},{56,24},{6... | collective-permute-start | bytes 786440 | tf_op jit(solution)/shard_map/ppermute | solution.py:30
  22.9 7.5 %collective-permute-start.1 = (bf16[32,4096]{1,0:T(8,128)(2,1)S(1)}, bf16[32,4096]{1,0:T(8,128)(2,1)S(1)}, u32[]{:S(2)}, u32[]{:S(2)}) collective-permute-start(bf16[32,4096]{1,0:T(8,128)(2,1)S(1)} %pad_maximum_fusion.6.refs_1_), channel_id=1, source_target_pairs={{0,8},{8,0},{16,24},{24,16},{32,40},{40,32},{48,56},{56,48},{64,72... | collective-permute-start | bytes 786440 | tf_op jit(solution)/shard_map/ppermute | solution.py:30
  27.6 9.0 %collective-permute-start.10 = (bf16[32,4096]{1,0:T(8,128)(2,1)S(1)}, bf16[32,4096]{1,0:T(8,128)(2,1)S(1)}, u32[]{:S(2)}, u32[]{:S(2)}) collective-permute-start(bf16[32,4096]{1,0:T(8,128)(2,1)S(1)} %collective-permute-done.6.refs_7_), channel_id=1, source_target_pairs={{0,32},{8,40},{16,48},{24,56},{32,64},{40,72},{48,80},{56,88},{64,... | collective-permute-start | bytes 786440 | tf_op jit(solution)/shard_map/ppermute | solution.py:30
  27.6 9.0 %collective-permute-start.11 = (bf16[32,4096]{1,0:T(8,128)(2,1)S(1)}, bf16[32,4096]{1,0:T(8,128)(2,1)S(1)}, u32[]{:S(2)}, u32[]{:S(2)}) collective-permute-start(bf16[32,4096]{1,0:T(8,128)(2,1)S(1)} %collective-permute-done.7.refs_8_), channel_id=1, source_target_pairs={{0,224},{8,232},{16,240},{24,248},{32,0},{40,8},{48,16},{56,24},{6... | collective-permute-start | bytes 786440 | tf_op jit(solution)/shard_map/ppermute | solution.py:30
  36.7 6.9 %collective-permute-start.14 = (bf16[32,2048]{1,0:T(8,128)(2,1)S(1)}, bf16[32,2048]{1,0:T(8,128)(2,1)S(1)}, u32[]{:S(2)}, u32[]{:S(2)}) collective-permute-start(bf16[32,2048]{1,0:T(8,128)(2,1)S(1)} %get-tuple-element.29), channel_id=1, source_target_pairs={{0,32},{8,40},{16,48},{24,56},{32,64},{40,72},{48,80},{56,88},{64,... | collective-permute-start | bytes 393224 | tf_op jit(solution)/shard_map/ppermute | solution.py:30
  36.8 10.1 %collective-permute-start.8 = (bf16[32,4096]{1,0:T(8,128)(2,1)S(1)}, bf16[32,4096]{1,0:T(8,128)(2,1)S(1)}, u32[]{:S(2)}, u32[]{:S(2)}) collective-permute-start(bf16[32,4096]{1,0:T(8,128)(2,1)S(1)} %collective-permute-done.6.refs_7_), channel_id=1, source_target_pairs={{0,8},{8,0},{16,24},{24,16},{32,40},{40,32},{48,56},{56,48},{64,72... | collective-permute-start | bytes 786440 | tf_op jit(solution)/shard_map/ppermute | solution.py:30
  39.9 7.1 %collective-permute-start.9 = (bf16[32,4096]{1,0:T(8,128)(2,1)S(1)}, bf16[32,4096]{1,0:T(8,128)(2,1)S(1)}, u32[]{:S(2)}, u32[]{:S(2)}) collective-permute-start(bf16[32,4096]{1,0:T(8,128)(2,1)S(1)} %collective-permute-done.7.refs_8_), channel_id=1, source_target_pairs={{0,8},{8,0},{16,24},{24,16},{32,40},{40,32},{48,56},{56,48},{64,72... | collective-permute-start | bytes 786440 | tf_op jit(solution)/shard_map/ppermute | solution.py:30
  40.0 6.0 %collective-permute-start.15 = (bf16[32,2048]{1,0:T(8,128)(2,1)S(1)}, bf16[32,2048]{1,0:T(8,128)(2,1)S(1)}, u32[]{:S(2)}, u32[]{:S(2)}) collective-permute-start(bf16[32,2048]{1,0:T(8,128)(2,1)S(1)} %get-tuple-element.28), channel_id=1, source_target_pairs={{0,224},{8,232},{16,240},{24,248},{32,0},{40,8},{48,16},{56,24},{6... | collective-permute-start | bytes 393224 | tf_op jit(solution)/shard_map/ppermute | solution.py:30
  46.8 63.1 %collective-permute-start.18 = (bf16[1024,2048]{1,0:T(8,128)(2,1)}, bf16[1024,2048]{1,0:T(8,128)(2,1)}, u32[]{:S(2)}, u32[]{:S(2)}) collective-permute-start(bf16[1024,2048]{1,0:T(8,128)(2,1)} %slice_select_fusion), channel_id=1, source_target_pairs={{0,8},{8,0},{16,24},{24,16},{32,40},{40,32},{48,56},{56,48},{64,72... | collective-permute-start | bytes 12582920 | tf_op jit(solution)/shard_map/ppermute | solution.py:30
  55.4 24.1 %all-to-all-start = ((f16[8,288,256]{2,1,0:T(8,128)(2,1)}), f16[8,288,256]{2,1,0:T(8,128)(2,1)S(1)}, u32[]{:S(2)}, u32[]{:S(2)}) async-start(f16[8,288,256]{2,1,0:T(8,128)(2,1)} %pad_maximum_fusion), calls=%async_computation | async-start | bytes 2359296 | tf_op jit(solution)/shard_map/all_to_all | solution.py:394
  81.0 19.1 %all-to-all-start.1 = ((bf16[8,128,512]{2,1,0:T(8,128)(2,1)}), bf16[8,128,512]{2,1,0:T(8,128)(2,1)S(1)}, u32[]{:S(2)}, u32[]{:S(2)}) async-start(bf16[8,128,512]{2,1,0:T(8,128)(2,1)} %broadcast_in_dim.9), calls=%async_computation.1 | async-start | bytes 2097152 | tf_op jit(solution)/shard_map/all_to_all | solution.py:402
  114.5 8.6 %collective-permute-start.20 = (bf16[64,1536]{1,0:T(8,128)(2,1)S(1)}, bf16[64,1536]{1,0:T(8,128)(2,1)S(1)}, u32[]{:S(2)}, u32[]{:S(2)}) collective-permute-start(bf16[64,1536]{1,0:T(8,128)(2,1)S(1)} %get-tuple-element.43), channel_id=1, source_target_pairs={{0,32},{8,40},{16,48},{24,56},{32,64},{40,72},{48,80},{56,88},{64,... | collective-permute-start | bytes 589832 | tf_op jit(solution)/shard_map/ppermute | solution.py:30
  115.5 7.8 %collective-permute-start.21 = (bf16[64,1536]{1,0:T(8,128)(2,1)S(1)}, bf16[64,1536]{1,0:T(8,128)(2,1)S(1)}, u32[]{:S(2)}, u32[]{:S(2)}) collective-permute-start(bf16[64,1536]{1,0:T(8,128)(2,1)S(1)} %get-tuple-element.42), channel_id=1, source_target_pairs={{0,224},{8,232},{16,240},{24,248},{32,0},{40,8},{48,16},{56,24},{6... | collective-permute-start | bytes 589832 | tf_op jit(solution)/shard_map/ppermute | solution.py:30
  123.2 9.8 %collective-permute-start.22 = (bf16[64,2560]{1,0:T(8,128)(2,1)S(1)}, bf16[64,2560]{1,0:T(8,128)(2,1)S(1)}, u32[]{:S(2)}, u32[]{:S(2)}) collective-permute-start(bf16[64,2560]{1,0:T(8,128)(2,1)S(1)} %pad_maximum_fusion.1.refs_0_), channel_id=1, source_target_pairs={{0,32},{8,40},{16,48},{24,56},{32,64},{40,72},{48,80},{56,88},{64,... | collective-permute-start | bytes 983048 | tf_op jit(solution)/shard_map/ppermute | solution.py:30
  123.4 9.8 %collective-permute-start.25 = (bf16[64,2560]{1,0:T(8,128)(2,1)S(1)}, bf16[64,2560]{1,0:T(8,128)(2,1)S(1)}, u32[]{:S(2)}, u32[]{:S(2)}) collective-permute-start(bf16[64,2560]{1,0:T(8,128)(2,1)S(1)} %pad_maximum_fusion.2.refs_1_), channel_id=1, source_target_pairs={{0,224},{8,232},{16,240},{24,248},{32,0},{40,8},{48,16},{56,24},{6... | collective-permute-start | bytes 983048 | tf_op jit(solution)/shard_map/ppermute | solution.py:30
  133.1 8.9 %collective-permute-start.23 = (bf16[64,2560]{1,0:T(8,128)(2,1)S(1)}, bf16[64,2560]{1,0:T(8,128)(2,1)S(1)}, u32[]{:S(2)}, u32[]{:S(2)}) collective-permute-start(bf16[64,2560]{1,0:T(8,128)(2,1)S(1)} %pad_maximum_fusion.3), channel_id=1, source_target_pairs={{0,32},{8,40},{16,48},{24,56},{32,64},{40,72},{48,80},{56,88},{64,... | collective-permute-start | bytes 983048 | tf_op jit(solution)/shard_map/ppermute | solution.py:30
  133.4 8.9 %collective-permute-start.26 = (bf16[64,2560]{1,0:T(8,128)(2,1)S(1)}, bf16[64,2560]{1,0:T(8,128)(2,1)S(1)}, u32[]{:S(2)}, u32[]{:S(2)}) collective-permute-start(bf16[64,2560]{1,0:T(8,128)(2,1)S(1)} %pad_maximum_fusion.5), channel_id=1, source_target_pairs={{0,224},{8,232},{16,240},{24,248},{32,0},{40,8},{48,16},{56,24},{6... | collective-permute-start | bytes 983048 | tf_op jit(solution)/shard_map/ppermute | solution.py:30
  142.1 8.0 %collective-permute-start.24 = (bf16[64,2560]{1,0:T(8,128)(2,1)S(1)}, bf16[64,2560]{1,0:T(8,128)(2,1)S(1)}, u32[]{:S(2)}, u32[]{:S(2)}) collective-permute-start(bf16[64,2560]{1,0:T(8,128)(2,1)S(1)} %pad_maximum_fusion.4), channel_id=1, source_target_pairs={{0,32},{8,40},{16,48},{24,56},{32,64},{40,72},{48,80},{56,88},{64,... | collective-permute-start | bytes 983048 | tf_op jit(solution)/shard_map/ppermute | solution.py:30
  142.3 7.9 %collective-permute-start.27 = (bf16[64,2048]{1,0:T(8,128)(2,1)S(1)}, bf16[64,2048]{1,0:T(8,128)(2,1)S(1)}, u32[]{:S(2)}, u32[]{:S(2)}) collective-permute-start(bf16[64,2048]{1,0:T(8,128)(2,1)S(1)} %add_convert_fusion), channel_id=1, source_target_pairs={{0,224},{8,232},{16,240},{24,248},{32,0},{40,8},{48,16},{56,24},{6... | collective-permute-start | bytes 786440 | tf_op jit(solution)/shard_map/ppermute | solution.py:30
  155.0 5.7 %collective-permute-start.30 = (f32[125,256]{1,0:T(8,128)S(1)}, f32[125,256]{1,0:T(8,128)S(1)}, u32[]{:S(2)}, u32[]{:S(2)}) collective-permute-start(f32[125,256]{1,0:T(8,128)S(1)} %pad_maximum_fusion.10), channel_id=1, source_target_pairs={{0,8},{8,0},{16,24},{24,16},{32,40},{40,32},{48,56},{56,48},{64,72... | collective-permute-start | bytes 384008 | tf_op jit(solution)/shard_map/ppermute | solution.py:30
  (12 other events, 44.2 us)
